TPU v7x, 128 devices: a whole 4x4x4 slice. The times are simulated.
128 devices in a mesh: occ: 4 (over y_hi, core), virt: 32 (over x, y_lo, z).
Axes of the slice: x: 4, y: 4 (y_hi: 2, y_lo: 2; y = y_hi * 2 + y_lo), z: 4, core: 2. Of those that a mesh axis runs over, the one named last changes fastest.
Arguments:
- factors: bfloat16 [2400, 640, 640], P('virt', 'occ'), may hold values from -0.25 to 0.25
- amplitudes: bfloat16 [16, 16, 2, 640], P('occ', None, None, 'virt'), may hold values from -6 to 6
- block_sizes: int32 [8], replicated, may hold values from 1 to 80, 600 in all
Outputs:
- residual: bfloat16 [16, 16, 640, 640], P('occ', None, None, 'virt')
Inputs may be any that keep to these rules, and one draw needn't show every extreme that they name: `block_sizes`: the 8 entries sum to 600, and the largest equals 80.
All inputs are finite; a program needn't handle non-finite values.
Results may differ from a plain program's by a relative error of at most 0.0059.
Values may be sent and summed in bfloat16 or wider, within the bound.
No kernel may reach another device: no remote copies, remote signals or barrier semaphores. Data moves between devices by JAX's collectives and lax.ppermute only.
A program may use at most 192 MiB of HBM per device.

v0:
```python
import jax
import jax.numpy as jnp
from jax import lax
from jax.sharding import PartitionSpec as P


def per_device(factors, amplitudes, block_sizes):
    q_local, b_local, vpadded = factors.shape
    cwindow = amplitudes.shape[2]
    irrep_count = block_sizes.shape[0]
    block_width = vpadded // irrep_count
    position = jnp.arange(vpadded, dtype=jnp.int32)
    onehot = (position // block_width)[:, None] == jnp.arange(irrep_count, dtype=jnp.int32)[None, :]
    size_at = jnp.sum(jnp.where(onehot, block_sizes[None, :], 0), axis=1)
    usable = position % block_width < size_at
    own_cols = jnp.transpose(factors[:, :, :cwindow], (2, 0, 1))
    amps_part, cols_part = (
        lax.all_gather(amplitudes, "virt", axis=3, tiled=True),
        lax.all_gather(own_cols, "virt", axis=1, tiled=True),
    )
    amps_all, window_columns = (
        lax.all_gather(amps_part, "occ", axis=0, tiled=True),
        lax.all_gather(cols_part, "occ", axis=2, tiled=True),
    )
    occ_count = amps_all.shape[0]
    keep = (usable[:cwindow][:, None] & usable[None, :]).astype(jnp.bfloat16)
    masked = (amps_all * keep[None, None]).astype(jnp.float32)
    antisym = (masked - jnp.transpose(masked, (1, 0, 2, 3))).astype(jnp.bfloat16)
    left_operand = jnp.transpose(antisym, (2, 0, 1, 3)).reshape(
        cwindow * occ_count * occ_count, vpadded
    )
    middle_operand = lax.dot_general(
        left_operand,
        factors.reshape(q_local * b_local, vpadded),
        (((1,), (1,)), ((), ())),
        preferred_element_type=jnp.float32,
    )
    middle_operand = middle_operand.astype(jnp.bfloat16).reshape(
        cwindow, occ_count, occ_count, q_local, b_local
    )
    tiles = lax.all_to_all(
        lax.all_to_all(middle_operand, "occ", split_axis=1, concat_axis=4, tiled=True),
        "virt",
        split_axis=4,
        concat_axis=3,
        tiled=True,
    )
    ladder = jnp.einsum(
        "cqa,cijqb->ijab", window_columns, tiles, preferred_element_type=jnp.float32
    )
    tile_width = ladder.shape[3]
    tile_start = lax.axis_index("virt") * tile_width
    usable_tile = lax.dynamic_slice_in_dim(usable, tile_start, tile_width)
    outer = (usable[:, None] & usable_tile[None, :]).astype(jnp.float32)
    return (ladder * outer[None, None]).astype(jnp.bfloat16)


def solution(mesh):
    return jax.shard_map(
        per_device,
        mesh=mesh,
        in_specs=(P("virt", "occ", None), P("occ", None, None, "virt"), P()),
        out_specs=P("occ", None, None, "virt"),
        check_vma=False,
    )
```

profile of v0, /device:TPU:24, one launch (start us, length us, event | category | flops | bytes accessed | tf_op | source)
XLA Modules:
  0.0 951.1 jit_solution(13998359063540881984)
XLA Ops:
  6.5 0.9 copy.42
  7.4 82.4 %all_gather.12 = bf16[4,16,2,640]{1,0,2,3:T(4,128)(2,1)S(1)} all-gather(bf16[4,16,2,20]{1,0,2,3:T(4,128)(2,1)S(1)} %copy.42), channel_id=1, replica_groups=mesh['occ'=4,'virt'=32] {'virt'}, dimensions={3}, use_global_device_ids=true | all-gather | bytes 168960 | tf_op jit(solution)/shard_map/all_gather | solution.py:18
  89.8 1.1 copy.43
  90.9 8.4 all_gather.13
  99.2 0.7 select_reduce_fusion
  100.0 0.1 and_convert_fusion.1
  100.1 0.2 fusion.4
  100.3 0.4 fusion.3
  100.7 18.1 %convolution_convert_fusion = bf16[512,12000]{0,1:T(8,128)(2,1)} fusion(bf16[512,640]{1,0:T(8,128)(2,1)S(1)} %bitcast.37, bf16[12000,640]{1,0:T(8,128)(2,1)} %bitcast.38), kind=kOutput, calls=%fused_computation.1 | convolution fusion | flops 7870464000 | bytes 28303360 | tf_op jit(solution)/shard_map/dot_general | solution.py:32
  118.8 16.4 %copy.46 = bf16[512,12000]{1,0:T(8,128)(2,1)} copy(bf16[512,12000]{0,1:T(8,128)(2,1)} %convolution_convert_fusion) | data formatting | bytes 24576000 | tf_op jit(solution)/shard_map/convert_element_type | solution.py:38
  135.1 30.9 %reshape.102 = bf16[2,16,16,75,160]{4,3,2,1,0:T(8,128)(2,1)} reshape(bf16[512,12000]{1,0:T(8,128)(2,1)} %copy.46) | data formatting | bytes 24576000 | tf_op jit(solution)/shard_map/reshape | solution.py:38
  166.0 19.0 %copy.47 = bf16[2,16,16,75,160]{4,2,3,0,1:T(8,128)(2,1)} copy(bf16[2,16,16,75,160]{4,3,2,1,0:T(8,128)(2,1)} %reshape.102) | data formatting | bytes 24576000 | tf_op jit(solution)/shard_map/reshape | solution.py:38
  185.0 9.0 all-to-all-start
  194.0 0.0 all-gather.3.cloned.1.call-start
  194.0 2.1 slice.7
  196.1 2.6 copy.61
  198.7 0.0 all-gather.3.cloned.1.call-update
  198.7 233.2 %all-to-all-done = bf16[2,16,16,75,160]{4,2,3,0,1:T(8,128)(2,1)} async-done(((bf16[2,16,16,75,160]{4,2,3,0,1:T(8,128)(2,1)}), bf16[2,16,16,75,160]{4,2,3,0,1:T(8,128)(2,1)}, u32[]{:S(2)}, u32[]{:S(2)}) %all-to-all-start) | async-done | bytes 12288032 | tf_op jit(solution)/shard_map/all_to_all | solution.py:42
  431.9 23.4 %copy.68 = bf16[2,4,4,16,75,160]{5,1,3,4,2,0:T(4,128)(2,1)} copy(bf16[2,4,4,16,75,160]{5,3,4,0,2,1:T(8,128)(2,1)} %bitcast.4) | data formatting | bytes 24576000 | tf_op jit(solution)/shard_map/all_to_all | solution.py:42
  455.2 38.8 %copy.57 = bf16[2,4,16,75,4,160]{3,2,1,0,5,4:T(8,128)(2,1)} copy(bf16[2,4,16,75,4,160]{5,4,2,3,1,0:T(4,128)(2,1)} %bitcast.36) | data formatting | bytes 24576000 | tf_op jit(solution)/shard_map/all_to_all | solution.py:42
  494.1 13.3 %all-to-all-start.1 = ((bf16[2,4,16,75,640]{3,2,1,0,4:T(8,128)(2,1)}), bf16[2,4,16,75,640]{3,2,1,0,4:T(8,128)(2,1)}, u32[]{:S(2)}, u32[]{:S(2)}) async-start(bf16[2,4,16,75,640]{3,2,1,0,4:T(8,128)(2,1)} %bitcast.35), calls=%async_computation.1 | async-start | bytes 41943040 | tf_op jit(solution)/shard_map/all_to_all | solution.py:41
  507.4 0.0 all-gather.5.cloned.1.call-start
  507.4 0.0 all-gather.3.cloned.1.call-done
  507.4 7.1 copy.53
  514.5 0.0 all-gather.5.cloned.1.call-update
  514.6 0.1 dynamic_slice.3
  514.6 0.1 and_convert_fusion
  514.7 353.9 %all-to-all-done.1 = bf16[2,4,16,75,640]{3,2,1,0,4:T(8,128)(2,1)} async-done(((bf16[2,4,16,75,640]{3,2,1,0,4:T(8,128)(2,1)}), bf16[2,4,16,75,640]{3,2,1,0,4:T(8,128)(2,1)}, u32[]{:S(2)}, u32[]{:S(2)}) %all-to-all-start.1) | async-done | bytes 12288032 | tf_op jit(solution)/shard_map/all_to_all | solution.py:41
  868.6 23.0 %copy.59 = bf16[2,4,16,32,75,20]{4,3,2,1,5,0:T(8,128)(2,1)} copy(bf16[2,4,16,32,75,20]{4,2,1,0,5,3:T(8,128)(2,1)} %bitcast.9) | data formatting | bytes 24576000 | tf_op jit(solution)/shard_map/all_to_all | solution.py:41
  891.7 36.5 %reshape.105 = bf16[2,4,16,2400,20]{3,2,1,4,0:T(8,128)(2,1)} reshape(bf16[2,4,16,32,75,20]{4,3,2,1,5,0:T(8,128)(2,1)} %copy.59) | data formatting | bytes 24576000 | tf_op jit(solution)/shard_map/all_to_all | solution.py:41
  928.2 0.0 all-gather.5.cloned.1.call-done
  928.2 14.6 %fusion = f32[4,16,20,640,1]{3,1,0,2,4:T(8,128)S(1)} fusion(bf16[2,4,16,2400,20]{3,2,1,4,0:T(8,128)(2,1)} %reshape.105, bf16[2,2400,640]{1,2,0:T(8,128)(2,1)} %all-gather.5.cloned.1.call-done), kind=kOutput, calls=%fused_computation.2 | convolution fusion | flops 7864320000 | bytes 21708800 | tf_op jit(solution)/shard_map/cqa,cijqb->ijab/dot_general | solution.py:48
  942.8 1.5 fusion.2
  (3 shorter events, 0.0 us)
Async XLA Ops:
  185.0 246.8 %all-to-all-start = ((bf16[2,16,16,75,160]{4,2,3,0,1:T(8,128)(2,1)}), bf16[2,16,16,75,160]{4,2,3,0,1:T(8,128)(2,1)}, u32[]{:S(2)}, u32[]{:S(2)}) async-start(bf16[2,16,16,75,160]{4,2,3,0,1:T(8,128)(2,1)} %copy.47), calls=%async_computation | async-start | bytes 39321600 | tf_op jit(solution)/shard_map/all_to_all | solution.py:42
  194.0 313.4 %all-gather.3.cloned.1.call-start = ((), (), s32[]{:S(2)}) async-start(), calls=%async_computation.2 | async-start | bytes 2534400 | tf_op jit(solution)/shard_map/all_gather | solution.py:19
  494.1 374.6 %all-to-all-start.1 = ((bf16[2,4,16,75,640]{3,2,1,0,4:T(8,128)(2,1)}), bf16[2,4,16,75,640]{3,2,1,0,4:T(8,128)(2,1)}, u32[]{:S(2)}, u32[]{:S(2)}) async-start(bf16[2,4,16,75,640]{3,2,1,0,4:T(8,128)(2,1)} %bitcast.35), calls=%async_computation.1 | async-start | bytes 41943040 | tf_op jit(solution)/shard_map/all_to_all | solution.py:41
  507.4 420.8 %all-gather.5.cloned.1.call-start = ((), (), s32[]{:S(2)}) async-start(), calls=%async_computation.3 | async-start | bytes 7782400 | tf_op jit(solution)/shard_map/all_gather | solution.py:23
Sparse Core Ops, SparseCore 0:
  198.8 154.8 all-gather.2
  514.7 165.4 all-gather.4
where the time goes:
time: 969 us; the launch traced here: 951 us
  waiting for transfers between devices  587 us (61%)
  local copies, waits for them, and re-layouts  202 us (21%)
  blocking collectives  90.7 us (9%)
  matrix products  32.7 us (3%)
  starting transfers between devices  22.3 us (2%)
  between operations  13.5 us (1%)
    all_to_all x1, waiting for transfers between devices, per_device(): lax.all_to_all(lax.all_to_all(middle_operand, 'occ', split_axis=1, concat...  354 us
    all_to_all x1, waiting for transfers between devices, per_device(): lax.all_to_all(middle_operand, 'occ', split_axis=1, concat_axis=4, tiled=...  233 us
    all_gather x1, blocking collectives, per_device(): lax.all_gather(amplitudes, 'virt', axis=3, tiled=True)  82.4 us
    all_to_all x2, local copies, waits for them, and re-layouts, per_device(): lax.all_to_all(middle_operand, 'occ', split_axis=1, concat_axis=4, tiled=...  62.2 us
    all_to_all x2, local copies, waits for them, and re-layouts, per_device(): lax.all_to_all(lax.all_to_all(middle_operand, 'occ', split_axis=1, concat...  59.5 us
    reshape x2, local copies, waits for them, and re-layouts, per_device(): middle_operand.astype(jnp.bfloat16)  49.9 us
  transfers between devices with their start and end apart: 4, of which 2 were waited for; matrix products, arithmetic and copies ran while one was open for 14% of the time, Pallas kernels for 0%

commit v1 on v0

v1 whole, which is shorter than its diff:
```python
import functools

import jax
import jax.numpy as jnp
import numpy as np
from jax import lax
from jax.experimental import pallas as pl
from jax.experimental.pallas import tpu as pltpu
from jax.sharding import Mesh, PartitionSpec as P

OCC = ("yh", "core")
TILE = ("yl", "z", "x")
NPAIR = 128
QPAD = 80


def pair_tables(occ, cwin, occ_shards):
    pairs = [(i, j) for i in range(occ) for j in range(i + 1, occ)]
    per = occ // occ_shards
    pick = np.zeros((occ_shards, cwin, per, occ, cwin, NPAIR), np.float32)
    spread = np.zeros((occ, occ, NPAIR), np.float32)
    for p, (i, j) in enumerate(pairs):
        for c in range(cwin):
            pick[i // per, c, i % per, j, c, p] = 1.0
            pick[j // per, c, j % per, i, c, p] = -1.0
        spread[i, j, p] = 1.0
        spread[j, i, p] = -1.0
    return (
        pick.reshape(occ_shards, cwin * per * occ, cwin * NPAIR),
        spread.reshape(occ * occ, NPAIR),
    )


def share(x, axes, count):
    return lax.all_to_all(
        jnp.broadcast_to(x[None], (count,) + x.shape), axes, 0, 0, tiled=True
    )


def middle_kernel(q_local, dests, width, b_ref, a_ref, out_ref):
    step = pl.program_id(0)
    rows, b_local, v = b_ref.shape
    cwin = a_ref.shape[1] // NPAIR
    res = lax.dot_general(
        b_ref[...].reshape(rows * b_local, v),
        a_ref[...],
        (((1,), (0,)), ((), ())),
        preferred_element_type=jnp.float32,
    ).reshape(rows, b_local, cwin * NPAIR)
    q = step * rows + lax.broadcasted_iota(jnp.int32, (rows, 1, 1), 0)
    res = jnp.where(q < q_local, res, 0.0)
    res = jnp.swapaxes(res, 0, 1).astype(jnp.bfloat16)
    res = res.reshape(dests, width, rows, cwin * NPAIR)
    for c in range(cwin):
        for h in range(width):
            out_ref[:, c, :, h * NPAIR : (h + 1) * NPAIR] = res[
                :, h, :, c * NPAIR : (c + 1) * NPAIR
            ]


def middle(factors, amps, dests, width):
    q_local, b_local, v = factors.shape
    cwin = amps.shape[1] // NPAIR
    rows = 16
    return pl.pallas_call(
        functools.partial(middle_kernel, q_local, dests, width),
        grid=(QPAD // rows,),
        in_specs=[
            pl.BlockSpec((rows, b_local, v), lambda s: (s, 0, 0)),
            pl.BlockSpec(amps.shape, lambda s: (0, 0)),
        ],
        out_specs=pl.BlockSpec(
            (dests, cwin, rows, width * NPAIR), lambda s: (0, 0, s, 0)
        ),
        out_shape=jax.ShapeDtypeStruct(
            (dests, cwin, QPAD, width * NPAIR), jnp.bfloat16
        ),
        compiler_params=pltpu.CompilerParams(vmem_limit_bytes=48 << 20),
        cost_estimate=pl.CostEstimate(
            flops=2 * q_local * b_local * v * cwin * NPAIR,
            bytes_accessed=2 * (factors.size + dests * cwin * QPAD * width * NPAIR),
            transcendentals=0,
        ),
    )(factors, amps)


def per_device(factors, amplitudes, block_sizes):
    q_local, b_local, v = factors.shape
    occ_local, occ, cwin, tile = amplitudes.shape
    occ_shards, shards = occ // occ_local, v // tile
    nx = 4
    width = tile // nx
    irreps = block_sizes.shape[0]
    block = v // irreps
    pick_np, spread_np = pair_tables(occ, cwin, occ_shards)

    position = jnp.arange(v, dtype=jnp.int32)
    onehot = (position // block)[:, None] == jnp.arange(irreps, dtype=jnp.int32)[None, :]
    size_at = jnp.sum(jnp.where(onehot, block_sizes[None, :], 0), axis=1)
    usable = position % block < size_at

    own = jnp.transpose(amplitudes, (3, 2, 0, 1)).reshape(tile, cwin * occ_local * occ)
    every = share(own, OCC + ("x", "yl", "z"), occ_shards * shards)
    every = every.reshape(occ_shards, v, cwin * occ_local * occ)
    antisym = jnp.einsum(
        "odl,olm->dm",
        every,
        jnp.asarray(pick_np, jnp.bfloat16),
        preferred_element_type=jnp.float32,
    )
    keep = usable[:, None] & jnp.repeat(usable[:cwin], NPAIR)[None, :]
    antisym = jnp.where(keep, antisym, 0.0).astype(jnp.bfloat16)

    cols = jnp.transpose(factors[:, :, :cwin], (2, 0, 1))
    cols = jnp.pad(cols, ((0, 0), (0, QPAD - q_local), (0, 0)))
    cols = share(cols, OCC, occ_shards)
    cols = jnp.transpose(cols, (1, 2, 0, 3)).reshape(cwin, QPAD, v)
    half = lax.dynamic_index_in_dim(cols, lax.axis_index("core"), 0, keepdims=False)
    half = share(half, TILE, shards).reshape(shards, QPAD, v)
    columns = lax.all_gather(half, "core", axis=0, tiled=False)
    columns = jnp.transpose(columns, (1, 0, 2, 3)).reshape(shards * cwin * QPAD, v)

    mid = middle(factors, antisym, shards, width)
    mid = mid.reshape(shards, cwin * QPAD, width * NPAIR)
    tiles = lax.all_to_all(mid, TILE, 0, 0, tiled=True)
    tiles = tiles.reshape(shards * cwin * QPAD, width * NPAIR)
    ladder = lax.dot_general(
        tiles, columns, (((0,), (0,)), ((), ())), preferred_element_type=jnp.float32
    ).reshape(width, NPAIR, v)

    occ_at = lax.axis_index(OCC)
    x_at = lax.axis_index("x")
    tile_at = lax.axis_index(("yl", "z"))
    b_first = occ_at * b_local + tile_at * tile + x_at * width
    usable_b = lax.dynamic_slice_in_dim(usable, b_first, width)
    outer = usable_b[:, None, None] & usable[None, None, :]
    ladder = jnp.where(outer, ladder, 0.0).astype(jnp.bfloat16)
    spread = spread_np.reshape(occ_shards, occ_local, occ, NPAIR)
    rows = jnp.einsum(
        "oijp,hpa->oihja",
        jnp.asarray(spread, jnp.bfloat16),
        ladder,
        preferred_element_type=jnp.float32,
    ).astype(jnp.bfloat16)

    out = jnp.zeros((occ_local, nx, width, occ, v), jnp.bfloat16)
    for r in range(nx):
        perm = [
            (o * nx + x, ((x + r) % nx) * nx + o)
            for o in range(occ_shards)
            for x in range(nx)
        ]
        part = lax.dynamic_index_in_dim(rows, (x_at + r) % nx, 0, keepdims=False)
        part = lax.ppermute(part, OCC + ("x",), perm)
        out = lax.dynamic_update_slice(
            out, part[:, None], (0, (occ_at - r + nx) % nx, 0, 0, 0)
        )
    out = out.reshape(occ_local, nx * width, occ, v)
    return jnp.transpose(out, (0, 2, 3, 1))


def solution(mesh):
    split = Mesh(
        mesh.devices.reshape(2, 2, 4, 2, 4), ("yh", "core", "x", "yl", "z")
    )
    virt = ("x", "yl", "z")
    return jax.shard_map(
        per_device,
        mesh=split,
        in_specs=(P(virt, OCC, None), P(OCC, None, None, virt), P()),
        out_specs=P(OCC, None, None, virt),
        check_vma=False,
    )
```

time: 969 us -> 283 us (0.29); the launches traced: 951 us -> 281 us
  waiting for transfers between devices: 587 us -> 186 us
  local copies, waits for them, and re-layouts: 202 us -> 25.9 us
  blocking collectives: 90.7 us -> 0 us
  matrix products: 32.7 us -> 6.2 us
  starting transfers between devices: 22.3 us -> 36.7 us
  Pallas kernels: 0 us -> 12.6 us
    all_to_all x2 -> x4, waiting for transfers between devices: 587 us -> 149 us  [the longest x1 91 us: per_device(): tiles = lax.all_to_all(mid, TILE, 0, 0, tiled=True)]
    all_to_all x4 -> x0, local copies, waits for them, and re-layouts: 122 us -> none  [the longest x2 62.2 us: per_device(): lax.all_to_all(middle_operand, 'occ', split_axis=1, concat_axis=4, tiled=...]
    all_gather x2 -> x0, blocking collectives: 90.7 us -> none  [the longest x1 82.4 us: per_device(): lax.all_gather(amplitudes, 'virt', axis=3, tiled=True)]
    reshape x2, local copies, waits for them, and re-layouts: 49.9 us -> 0.36 us  [the longest x1 0.21 us: per_device(): cols = jnp.transpose(cols, (1, 2, 0, 3)).reshape(cwin, QPAD, v)]
    ppermute x0 -> x4, waiting for transfers between devices: none -> 36.4 us  [per_device(): part = lax.ppermute(part, OCC + ('x',), perm)]
    dot_general x2 -> x3, matrix products: 32.7 us -> 6.2 us  [the longest x1 5.26 us: per_device(): lax.dot_general(tiles, columns, (((0,), (0,)), ((), ())), preferred_eleme...]
    convert_element_type x1 -> x0, local copies, waits for them, and re-layouts: 16.4 us -> none  [per_device(): middle_operand.astype(jnp.bfloat16)]
    pallas_call x0 -> x1, Pallas kernels: none -> 12.6 us  [middle(): pl.pallas_call(functools.partial(middle_kernel, q_local, dests, width), g...]
  transfers between devices with their start and end apart: 4 -> 9, of which waited for: 2 -> 8; matrix products, arithmetic and copies ran while one was open for 14% -> 4% of each run, Pallas kernels for 0% -> 4%
where the time goes in v1:
time: 283 us; the launch traced here: 281 us
  waiting for transfers between devices  186 us (66%)
  starting transfers between devices  36.7 us (13%)
  local copies, waits for them, and re-layouts  25.9 us (9%)
  between operations  13.8 us (5%)
  Pallas kernels  12.6 us (4%)
  matrix products  6.2 us (2%)
    all_to_all x1, waiting for transfers between devices, per_device(): tiles = lax.all_to_all(mid, TILE, 0, 0, tiled=True)  91 us
    all_to_all x3, waiting for transfers between devices, share(): lax.all_to_all(jnp.broadcast_to(x[None], (count,) + x.shape), axes, 0, 0,...  58.4 us
    ppermute x4, waiting for transfers between devices, per_device(): part = lax.ppermute(part, OCC + ('x',), perm)  36.4 us
    all_to_all x3, starting transfers between devices, share(): lax.all_to_all(jnp.broadcast_to(x[None], (count,) + x.shape), axes, 0, 0,...  21.6 us
    pallas_call x1, Pallas kernels, middle(): pl.pallas_call(functools.partial(middle_kernel, q_local, dests, width), g...  12.6 us
    dot_general x1, local copies, waits for them, and re-layouts, per_device(): lax.dot_general(tiles, columns, (((0,), (0,)), ((), ())), preferred_eleme...  9.54 us
    ppermute x4, starting transfers between devices, per_device(): part = lax.ppermute(part, OCC + ('x',), perm)  7.82 us
    all_to_all x1, starting transfers between devices, per_device(): tiles = lax.all_to_all(mid, TILE, 0, 0, tiled=True)  7.26 us
  transfers between devices with their start and end apart: 9, of which 8 were waited for; matrix products, arithmetic and copies ran while one was open for 4% of the time, Pallas kernels for 4%

profile of v1, /device:TPU:24, one launch (start us, length us, event | category | flops | bytes accessed | tf_op | source)
XLA Modules:
  0.0 281.2 jit_solution(7344603015228826692)
XLA Ops:
  6.5 2.1 slice_bitcast_fusion
  8.7 0.0 copy-start.3
  8.7 3.0 %copy.42 = bf16[2,75,160]{2,1,0:T(8,128)(2,1)S(1)} copy(bf16[2,75,160]{0,2,1:T(8,128)(2,1)S(1)} %slice_bitcast_fusion) | data formatting | bytes 96000
  11.7 0.7 broadcast_in_dim.81
  12.4 4.8 %all-to-all-start.2 = ((bf16[4,2,80,160]{3,2,1,0:T(8,128)(2,1)}), bf16[4,2,80,160]{3,2,1,0:T(8,128)(2,1)S(1)}, u32[]{:S(2)}, u32[]{:S(2)}) async-start(bf16[4,2,80,160]{3,2,1,0:T(8,128)(2,1)} %broadcast_in_dim.81), calls=%async_computation.2 | async-start | bytes 655360 | tf_op jit(solution)/shard_map/all_to_all | solution.py:35
  17.2 0.0 copy-done.3
  17.2 0.1 copy.31
  17.4 0.1 broadcast_in_dim.78
  17.5 4.8 %all-to-all-done.2 = bf16[4,2,80,160]{3,2,1,0:T(8,128)(2,1)S(1)} async-done(((bf16[4,2,80,160]{3,2,1,0:T(8,128)(2,1)}), bf16[4,2,80,160]{3,2,1,0:T(8,128)(2,1)S(1)}, u32[]{:S(2)}, u32[]{:S(2)}) %all-to-all-start.2) | async-done | bytes 204832 | tf_op jit(solution)/shard_map/all_to_all | solution.py:35
  22.3 1.0 broadcast_in_dim.79
  23.3 10.6 %all-to-all-start = ((bf16[128,20,128]{2,1,0:T(8,128)(2,1)}), bf16[128,20,128]{2,1,0:T(8,128)(2,1)S(1)}, u32[]{:S(2)}, u32[]{:S(2)}) async-start(bf16[128,20,128]{2,1,0:T(8,128)(2,1)} %broadcast_in_dim.79), calls=%async_computation | async-start | bytes 1572864 | tf_op jit(solution)/shard_map/all_to_all | solution.py:35
  33.9 0.3 copy.35
  34.1 0.2 reshape.90
  34.4 13.8 %all-to-all-done = bf16[128,20,128]{2,1,0:T(8,128)(2,1)S(1)} async-done(((bf16[128,20,128]{2,1,0:T(8,128)(2,1)}), bf16[128,20,128]{2,1,0:T(8,128)(2,1)S(1)}, u32[]{:S(2)}, u32[]{:S(2)}) %all-to-all-start) | async-done | bytes 655392 | tf_op jit(solution)/shard_map/all_to_all | solution.py:35
  48.2 1.9 broadcast_in_dim.83
  50.1 0.0 copy-start.4
  50.1 0.0 copy-start.5
  50.1 6.2 %all-to-all-start.3 = ((bf16[32,80,640]{2,1,0:T(8,128)(2,1)}), bf16[32,80,640]{2,1,0:T(8,128)(2,1)}, u32[]{:S(2)}, u32[]{:S(2)}) async-start(bf16[32,80,640]{2,1,0:T(8,128)(2,1)} %broadcast_in_dim.83), calls=%async_computation.3 | async-start | bytes 6553600 | tf_op jit(solution)/shard_map/all_to_all | solution.py:35
  56.3 0.0 all-gather.3.cloned.1.call-start
  56.4 0.0 copy-done.4
  56.4 0.1 select_reduce_fusion
  56.5 0.1 broadcast_bitcast_fusion
  56.6 0.1 reshape.87
  56.7 0.0 copy-done.5
  56.7 0.4 fusion.2.a_ref
  57.1 39.8 %all-to-all-done.3 = bf16[32,80,640]{2,1,0:T(8,128)(2,1)} async-done(((bf16[32,80,640]{2,1,0:T(8,128)(2,1)}), bf16[32,80,640]{2,1,0:T(8,128)(2,1)}, u32[]{:S(2)}, u32[]{:S(2)}) %all-to-all-start.3) | async-done | bytes 3276832 | tf_op jit(solution)/shard_map/all_to_all | solution.py:35
  96.9 0.0 all-gather.3.cloned.1.call-update
  96.9 12.6 %shard_map.55 = bf16[32,2,80,640]{3,2,1,0:T(8,128)(2,1)} custom-call(bf16[75,160,640]{2,1,0:T(8,128)(2,1)} %b_ref.1, bf16[640,256]{1,0:T(8,128)(2,1)S(1)} %fusion.2.a_ref), custom_call_target="tpu_custom_call" | custom-call | flops 3932160000 | bytes 21913600 | tf_op jit(solution)/shard_map/pallas_call | solution.py:65
  109.4 7.3 %all-to-all-start.1 = ((bf16[32,160,640]{2,1,0:T(8,128)(2,1)}), bf16[32,160,640]{2,1,0:T(8,128)(2,1)}, u32[]{:S(2)}, u32[]{:S(2)}) async-start(bf16[32,160,640]{2,1,0:T(8,128)(2,1)} %bitcast.66), calls=%async_computation.1 | async-start | bytes 13107200 | tf_op jit(solution)/shard_map/all_to_all | solution.py:125
  116.8 0.1 dynamic_slice.20
  116.9 0.1 broadcast_and_fusion
  116.9 91.0 %all-to-all-done.1 = bf16[32,160,640]{2,1,0:T(8,128)(2,1)} async-done(((bf16[32,160,640]{2,1,0:T(8,128)(2,1)}), bf16[32,160,640]{2,1,0:T(8,128)(2,1)}, u32[]{:S(2)}, u32[]{:S(2)}) %all-to-all-start.1) | async-done | bytes 6553632 | tf_op jit(solution)/shard_map/all_to_all | solution.py:125
  208.0 9.5 %copy.33 = bf16[640,5120]{1,0:T(8,128)(2,1)} copy(bf16[640,5120]{0,1:T(8,128)(2,1)} %bitcast.6) | data formatting | bytes 13107200 | tf_op jit(solution)/shard_map/dot_general | solution.py:127
  217.5 0.0 all-gather.3.cloned.1.call-done
  217.5 0.0 copy-start
  217.5 3.6 %copy.36 = bf16[32,2,80,640]{3,2,1,0:T(8,128)(2,1)S(1)} copy(bf16[32,2,80,640]{3,2,0,1:T(8,128)(2,1)} %bitcast.67) | data formatting | bytes 13107200 | tf_op jit(solution)/shard_map/transpose | solution.py:121
  221.2 1.1 copy-done
  222.3 0.0 copy-start.2
  222.3 5.3 %fusion = bf16[5,128,640,1,1]{2,1,4,3,0:T(8,128)(2,1)S(1)} fusion(bf16[5,128,5120]{2,1,0:T(8,128)(2,1)S(1)} %bitcast.68, bf16[5120,640,1]{1,0,2:T(8,128)(2,1)S(1)} %bitcast.69, pred[5,640]{1,0:T(8,128)(4,1)S(1)} %broadcast_and_fusion), kind=kOutput, calls=%fused_computation.3 | convolution fusion | flops 4195123200 | bytes 13929600 | tf_op jit(solution)/shard_map/dot_general | solution.py:127
  227.5 0.0 copy-done.2
  227.5 0.6 convolution_convert_fusion
  228.1 0.2 dynamic-slice_bitcast_fusion
  228.3 7.4 %collective-permute-start = (bf16[4,5,16,640]{3,2,0,1:T(8,128)(2,1)S(1)}, bf16[4,5,16,640]{3,2,0,1:T(8,128)(2,1)S(1)}, u32[]{:S(2)}, u32[]{:S(2)}) collective-permute-start(bf16[4,5,16,640]{3,2,0,1:T(8,128)(2,1)S(1)} %get-tuple-element.8), channel_id=1, source_target_pairs={{0,0},{8,32},{16,64},{24,96},{32,8},{40,40},{48,72},{56,104},{64,1... | collective-permute-start | bytes 1228808 | tf_op jit(solution)/shard_map/ppermute | solution.py:154
  235.7 0.1 collective-permute-start.1
  235.9 0.1 collective-permute-start.2
  236.0 0.2 collective-permute-start.3
  236.2 9.2 %collective-permute-done = bf16[4,5,16,640]{3,2,0,1:T(8,128)(2,1)S(1)} collective-permute-done((bf16[4,5,16,640]{3,2,0,1:T(8,128)(2,1)S(1)}, bf16[4,5,16,640]{3,2,0,1:T(8,128)(2,1)S(1)}, u32[]{:S(2)}, u32[]{:S(2)}) %collective-permute-start) | collective-permute-done | bytes 409632 | tf_op jit(solution)/shard_map/ppermute | solution.py:154
  245.4 0.2 broadcast_in_dim.73
  245.6 0.1 bitcast_dynamic-update-slice_fusion.2
  245.6 7.6 %collective-permute-done.1 = bf16[4,5,16,640]{3,2,0,1:T(8,128)(2,1)S(1)} collective-permute-done((bf16[4,5,16,640]{3,2,0,1:T(8,128)(2,1)S(1)}, bf16[4,5,16,640]{3,2,0,1:T(8,128)(2,1)S(1)}, u32[]{:S(2)}, u32[]{:S(2)}) %collective-permute-start.1) | collective-permute-done | bytes 409632 | tf_op jit(solution)/shard_map/ppermute | solution.py:154
  253.3 0.1 bitcast_dynamic-update-slice_fusion.1
  253.3 9.1 %collective-permute-done.2 = bf16[4,5,16,640]{3,2,0,1:T(8,128)(2,1)S(1)} collective-permute-done((bf16[4,5,16,640]{3,2,0,1:T(8,128)(2,1)S(1)}, bf16[4,5,16,640]{3,2,0,1:T(8,128)(2,1)S(1)}, u32[]{:S(2)}, u32[]{:S(2)}) %collective-permute-start.2) | collective-permute-done | bytes 409632 | tf_op jit(solution)/shard_map/ppermute | solution.py:154
  262.5 0.1 bitcast_dynamic-update-slice_fusion
  262.5 0.1 copy.37
  262.7 10.5 %collective-permute-done.3 = bf16[4,5,16,640]{3,2,0,1:T(8,128)(2,1)S(1)} collective-permute-done((bf16[4,5,16,640]{3,2,0,1:T(8,128)(2,1)S(1)}, bf16[4,5,16,640]{3,2,0,1:T(8,128)(2,1)S(1)}, u32[]{:S(2)}, u32[]{:S(2)}) %collective-permute-start.3) | collective-permute-done | bytes 409632 | tf_op jit(solution)/shard_map/ppermute | solution.py:154
  273.1 0.1 copy_dynamic-update-slice_fusion
  273.2 0.0 copy-start.1
  273.2 1.2 copy-done.1
  (5 shorter events, 0.1 us)
Async XLA Ops:
  8.7 8.6 %copy-start.3 = (bf16[4,16,2,20]{3,2,1,0:T(2,128)(2,1)S(1)}, bf16[4,16,2,20]{3,2,1,0:T(2,128)(2,1)}, u32[]{:S(2)}) copy-start(bf16[4,16,2,20]{3,2,1,0:T(2,128)(2,1)} %param.6) | copy-start | bytes 15364
  12.4 9.9 %all-to-all-start.2 = ((bf16[4,2,80,160]{3,2,1,0:T(8,128)(2,1)}), bf16[4,2,80,160]{3,2,1,0:T(8,128)(2,1)S(1)}, u32[]{:S(2)}, u32[]{:S(2)}) async-start(bf16[4,2,80,160]{3,2,1,0:T(8,128)(2,1)} %broadcast_in_dim.81), calls=%async_computation.2 | async-start | bytes 655360 | tf_op jit(solution)/shard_map/all_to_all | solution.py:35
  23.3 24.9 %all-to-all-start = ((bf16[128,20,128]{2,1,0:T(8,128)(2,1)}), bf16[128,20,128]{2,1,0:T(8,128)(2,1)S(1)}, u32[]{:S(2)}, u32[]{:S(2)}) async-start(bf16[128,20,128]{2,1,0:T(8,128)(2,1)} %broadcast_in_dim.79), calls=%async_computation | async-start | bytes 1572864 | tf_op jit(solution)/shard_map/all_to_all | solution.py:35
  50.1 6.3 %copy-start.4 = (s32[8]{0:T(128)S(1)}, s32[8]{0:T(128)}, u32[]{:S(2)}) copy-start(s32[8]{0:T(128)} %param.7) | copy-start | bytes 100
  50.1 6.6 %copy-start.5 = (bf16[4,128,256]{1,2,0:T(8,128)(2,1)S(1)}, bf16[4,128,256]{1,2,0:T(8,128)(2,1)}, u32[]{:S(2)}) copy-start(bf16[4,128,256]{1,2,0:T(8,128)(2,1)} %constant.122.clone) | copy-start | bytes 786436
  50.1 46.8 %all-to-all-start.3 = ((bf16[32,80,640]{2,1,0:T(8,128)(2,1)}), bf16[32,80,640]{2,1,0:T(8,128)(2,1)}, u32[]{:S(2)}, u32[]{:S(2)}) async-start(bf16[32,80,640]{2,1,0:T(8,128)(2,1)} %broadcast_in_dim.83), calls=%async_computation.3 | async-start | bytes 6553600 | tf_op jit(solution)/shard_map/all_to_all | solution.py:35
  56.3 161.2 %all-gather.3.cloned.1.call-start = ((), (), s32[]{:S(2)}) async-start(), calls=%async_computation.4 | async-start | bytes 9830400 | tf_op jit(solution)/shard_map/all_gather | solution.py:120
  109.4 98.5 %all-to-all-start.1 = ((bf16[32,160,640]{2,1,0:T(8,128)(2,1)}), bf16[32,160,640]{2,1,0:T(8,128)(2,1)}, u32[]{:S(2)}, u32[]{:S(2)}) async-start(bf16[32,160,640]{2,1,0:T(8,128)(2,1)} %bitcast.66), calls=%async_computation.1 | async-start | bytes 13107200 | tf_op jit(solution)/shard_map/all_to_all | solution.py:125
  217.5 4.7 %copy-start = (bf16[640,5120]{1,0:T(8,128)(2,1)S(1)}, bf16[640,5120]{1,0:T(8,128)(2,1)}, u32[]{:S(2)}) copy-start(bf16[640,5120]{1,0:T(8,128)(2,1)} %copy.33) | copy-start | bytes 19660804
  222.3 5.3 %copy-start.2 = (bf16[4,4,16,128,1]{3,2,1,0,4:T(8,128)(2,1)S(1)}, bf16[4,4,16,128,1]{3,2,1,0,4:T(8,128)(2,1)}, u32[]{:S(2)}) copy-start(bf16[4,4,16,128,1]{3,2,1,0,4:T(8,128)(2,1)} %constant.128) | copy-start | bytes 196612
  228.3 17.1 %collective-permute-start = (bf16[4,5,16,640]{3,2,0,1:T(8,128)(2,1)S(1)}, bf16[4,5,16,640]{3,2,0,1:T(8,128)(2,1)S(1)}, u32[]{:S(2)}, u32[]{:S(2)}) collective-permute-start(bf16[4,5,16,640]{3,2,0,1:T(8,128)(2,1)S(1)} %get-tuple-element.8), channel_id=1, source_target_pairs={{0,0},{8,32},{16,64},{24,96},{32,8},{40,40},{48,72},{56,104},{64,1... | collective-permute-start | bytes 1228808 | tf_op jit(solution)/shard_map/ppermute | solution.py:154
  235.7 17.5 %collective-permute-start.1 = (bf16[4,5,16,640]{3,2,0,1:T(8,128)(2,1)S(1)}, bf16[4,5,16,640]{3,2,0,1:T(8,128)(2,1)S(1)}, u32[]{:S(2)}, u32[]{:S(2)}) collective-permute-start(bf16[4,5,16,640]{3,2,0,1:T(8,128)(2,1)S(1)} %get-tuple-element.7), channel_id=1, source_target_pairs={{0,32},{8,64},{16,96},{24,0},{32,40},{40,72},{48,104},{56,8},{64,4... | collective-permute-start | bytes 1228808 | tf_op jit(solution)/shard_map/ppermute | solution.py:154
  235.9 26.6 %collective-permute-start.2 = (bf16[4,5,16,640]{3,2,0,1:T(8,128)(2,1)S(1)}, bf16[4,5,16,640]{3,2,0,1:T(8,128)(2,1)S(1)}, u32[]{:S(2)}, u32[]{:S(2)}) collective-permute-start(bf16[4,5,16,640]{3,2,0,1:T(8,128)(2,1)S(1)} %get-tuple-element.6), channel_id=1, source_target_pairs={{0,64},{8,96},{16,0},{24,32},{32,72},{40,104},{48,8},{56,40},{64,8... | collective-permute-start | bytes 1228808 | tf_op jit(solution)/shard_map/ppermute | solution.py:154
  236.0 37.2 %collective-permute-start.3 = (bf16[4,5,16,640]{3,2,0,1:T(8,128)(2,1)S(1)}, bf16[4,5,16,640]{3,2,0,1:T(8,128)(2,1)S(1)}, u32[]{:S(2)}, u32[]{:S(2)}) collective-permute-start(bf16[4,5,16,640]{3,2,0,1:T(8,128)(2,1)S(1)} %get-tuple-element.5), channel_id=1, source_target_pairs={{0,96},{8,0},{16,32},{24,64},{32,104},{40,8},{48,40},{56,72},{64,1... | collective-permute-start | bytes 1228808 | tf_op jit(solution)/shard_map/ppermute | solution.py:154
  273.2 1.2 copy-start.1
Sparse Core Ops, SparseCore 0:
  97.0 20.1 all-gather.2

commit v2 on v1

v2 whole, which is shorter than its diff:
```python
import functools

import jax
import jax.numpy as jnp
import numpy as np
from jax import lax
from jax.experimental import pallas as pl
from jax.experimental.pallas import tpu as pltpu
from jax.sharding import Mesh, PartitionSpec as P

OCC = ("yh", "core")
TILE = ("yl", "z", "x")
NPAIR = 128
QPAD = 80
WIDTHS = (3, 2)


def pair_tables(occ, cwin, occ_shards):
    pairs = [(i, j) for i in range(occ) for j in range(i + 1, occ)]
    per = occ // occ_shards
    pick = np.zeros((occ_shards, cwin, per, occ, cwin, NPAIR), np.float32)
    spread = np.zeros((occ, occ, NPAIR), np.float32)
    for p, (i, j) in enumerate(pairs):
        for c in range(cwin):
            pick[i // per, c, i % per, j, c, p] = 1.0
            pick[j // per, c, j % per, i, c, p] = -1.0
        spread[i, j, p] = 1.0
        spread[j, i, p] = -1.0
    return (
        pick.reshape(occ_shards, cwin * per * occ, cwin * NPAIR),
        spread.reshape(occ * occ, NPAIR),
    )


def share(x, axes, count):
    return lax.all_to_all(
        jnp.broadcast_to(x[None], (count,) + x.shape), axes, 0, 0, tiled=True
    )


def middle_kernel(q_local, dests, widths, b_ref, a_ref, *out_refs):
    step = pl.program_id(0)
    rows, b_local, v = b_ref.shape
    cwin = a_ref.shape[1] // NPAIR
    res = lax.dot_general(
        b_ref[...].reshape(rows * b_local, v),
        a_ref[...],
        (((1,), (0,)), ((), ())),
        preferred_element_type=jnp.float32,
    ).reshape(rows, b_local, cwin * NPAIR)
    q = step * rows + lax.broadcasted_iota(jnp.int32, (rows, 1, 1), 0)
    res = jnp.where(q < q_local, res, 0.0)
    res = jnp.swapaxes(res, 0, 1).astype(jnp.bfloat16)
    res = res.reshape(dests, sum(widths), rows, cwin * NPAIR)
    first = 0
    for out_ref, width in zip(out_refs, widths):
        for c in range(cwin):
            for h in range(width):
                out_ref[:, c, :, h * NPAIR : (h + 1) * NPAIR] = res[
                    :, first + h, :, c * NPAIR : (c + 1) * NPAIR
                ]
        first += width


def middle(factors, amps, dests, widths):
    q_local, b_local, v = factors.shape
    cwin = amps.shape[1] // NPAIR
    rows = 16
    width = sum(widths)
    return pl.pallas_call(
        functools.partial(middle_kernel, q_local, dests, widths),
        grid=(QPAD // rows,),
        in_specs=[
            pl.BlockSpec((rows, b_local, v), lambda s: (s, 0, 0)),
            pl.BlockSpec(amps.shape, lambda s: (0, 0)),
        ],
        out_specs=[
            pl.BlockSpec((dests, cwin, rows, w * NPAIR), lambda s: (0, 0, s, 0))
            for w in widths
        ],
        out_shape=[
            jax.ShapeDtypeStruct((dests, cwin, QPAD, w * NPAIR), jnp.bfloat16)
            for w in widths
        ],
        compiler_params=pltpu.CompilerParams(vmem_limit_bytes=48 << 20),
        cost_estimate=pl.CostEstimate(
            flops=2 * q_local * b_local * v * cwin * NPAIR,
            bytes_accessed=2 * (factors.size + dests * cwin * QPAD * width * NPAIR),
            transcendentals=0,
        ),
    )(factors, amps)


def column_kernel(at_ref, *refs):
    pieces, out_ref = refs[:-1], refs[-1]
    occ_at, core_at = at_ref[0], at_ref[1]
    count = len(pieces)
    a_part = pieces[0].shape[2]
    own = [ref[core_at] for ref in pieces]
    for p in range(count):
        k = lax.rem(occ_at - p + count, count)
        value = own[0]
        for n in range(1, count):
            value = jnp.where(k == n, own[n], value)
        out_ref[:, :, p * a_part : (p + 1) * a_part] = jnp.broadcast_to(
            value[None], (out_ref.shape[0],) + value.shape
        )


def column_copies(pieces, at, copies):
    _, depth, a_part = pieces[0].shape
    vmem = pl.BlockSpec(memory_space=pltpu.VMEM)
    return pl.pallas_call(
        column_kernel,
        in_specs=[pl.BlockSpec(memory_space=pltpu.SMEM)] + [vmem] * len(pieces),
        out_specs=vmem,
        out_shape=jax.ShapeDtypeStruct(
            (copies, depth, len(pieces) * a_part), jnp.bfloat16
        ),
        compiler_params=pltpu.CompilerParams(vmem_limit_bytes=16 << 20),
    )(at, *pieces)


def ladder_kernel(
    groups, at_ref, m_ref, w_own_ref, w_far_ref, keep_ref, spread_ref, *refs
):
    outs, acc = refs[:-1], refs[-1]
    step, last = pl.program_id(0), pl.num_programs(0) - 1
    depth = m_ref.shape[0] * m_ref.shape[2]
    width = acc.shape[1] // NPAIR
    occ_local, occ = outs[0].shape[0], outs[0].shape[2]

    @pl.when(step == 0)
    def _():
        acc[...] = jnp.zeros_like(acc)

    def add(w_ref):
        acc[...] += jnp.dot(
            w_ref[...],
            m_ref[...].reshape(depth, -1),
            preferred_element_type=jnp.float32,
        )

    pl.when(step < groups)(lambda: add(w_own_ref))
    pl.when(step >= groups)(lambda: add(w_far_ref))

    @pl.when(step == last)
    def _():
        for h in range(width):
            part = acc[:, h * NPAIR : (h + 1) * NPAIR].astype(jnp.bfloat16)
            rows = lax.dot_general(
                spread_ref[...],
                part,
                (((1,), (1,)), ((), ())),
                preferred_element_type=jnp.float32,
            )
            rows = (rows * keep_ref[h : h + 1, :]).astype(jnp.bfloat16)
            rows = rows.reshape(len(outs), occ_local, occ, -1)
            for r, out in enumerate(outs):
                out[:, h] = rows[r]


def ladder_rows(tiles, own, far, keep, spread, at, occ_local, occ):
    _, sources, _, depth, lanes = tiles.shape
    a_size = own.shape[1]
    groups = 2
    width = lanes // NPAIR
    shards = occ // occ_local

    def m_at(s, at):
        yl = (at[0] + s % groups) % 2
        c = (at[1] + s // groups) % 2
        return yl, 0, c, 0, 0

    own_at = lambda s, at: (jnp.minimum(s, groups - 1), 0, 0)
    far_at = lambda s, at: (jnp.maximum(s - groups, 0), 0, 0)

    out_block = (occ_local, width, occ, a_size)
    whole = lambda n: lambda s, at: (0,) * n
    return pl.pallas_call(
        functools.partial(ladder_kernel, groups),
        grid_spec=pltpu.PrefetchScalarGridSpec(
            num_scalar_prefetch=1,
            grid=(2 * groups,),
            in_specs=[
                pl.BlockSpec((None, sources, 1, depth, lanes), m_at),
                pl.BlockSpec((None, a_size, sources * depth), own_at),
                pl.BlockSpec((None, a_size, sources * depth), far_at),
                pl.BlockSpec(keep.shape, whole(2)),
                pl.BlockSpec(spread.shape, whole(2)),
            ],
            out_specs=[pl.BlockSpec(out_block, whole(4))] * shards,
            scratch_shapes=[pltpu.VMEM((a_size, lanes), jnp.float32)],
        ),
        out_shape=[jax.ShapeDtypeStruct(out_block, jnp.bfloat16)] * shards,
        compiler_params=pltpu.CompilerParams(vmem_limit_bytes=48 << 20),
        cost_estimate=pl.CostEstimate(
            flops=2 * tiles.size * a_size,
            bytes_accessed=2 * (tiles.size + own.size + far.size),
            transcendentals=0,
        ),
    )(at, tiles, own, far, keep, spread)


def per_device(factors, amplitudes, block_sizes):
    q_local, b_local, v = factors.shape
    occ_local, occ, cwin, tile = amplitudes.shape
    occ_shards, shards = occ // occ_local, v // tile
    nx = lax.axis_size("x")
    width = tile // nx
    irreps = block_sizes.shape[0]
    block = v // irreps
    pick_np, spread_np = pair_tables(occ, cwin, occ_shards)
    occ_at, x_at, core_at = (lax.axis_index(n) for n in (OCC, "x", "core"))

    position = jnp.arange(v, dtype=jnp.int32)
    onehot = (position // block)[:, None] == jnp.arange(irreps, dtype=jnp.int32)[None, :]
    size_at = jnp.sum(jnp.where(onehot, block_sizes[None, :], 0), axis=1)
    usable = position % block < size_at

    own = jnp.transpose(amplitudes, (3, 2, 0, 1)).reshape(tile, cwin * occ_local * occ)
    every = share(own, OCC + ("x", "yl", "z"), occ_shards * shards)
    every = every.reshape(occ_shards, v, cwin * occ_local * occ)
    antisym = jnp.einsum(
        "odl,olm->dm",
        every,
        jnp.asarray(pick_np, jnp.bfloat16),
        preferred_element_type=jnp.float32,
    )
    keep = usable[:, None] & jnp.repeat(usable[:cwin], NPAIR)[None, :]
    antisym = jnp.where(keep, antisym, 0.0).astype(jnp.bfloat16)

    cols = jnp.transpose(factors[:, :, :cwin], (2, 0, 1))
    cols = jnp.pad(cols, ((0, 0), (0, QPAD - q_local), (0, 0)))
    pieces = [cols]
    for k in range(1, occ_shards):
        shift = [(o, (o + k) % occ_shards) for o in range(occ_shards)]
        pieces.append(lax.ppermute(cols, OCC, shift))
    sources = shards // 2
    where = jnp.stack([occ_at, core_at]).astype(jnp.int32)
    half = column_copies(pieces, where, sources)
    half = lax.all_to_all(half, TILE[1:], 0, 0, tiled=True)
    half, mids = lax.optimization_barrier(
        (half, middle(factors, antisym, shards, WIDTHS))
    )
    half = half.reshape(sources * QPAD, v).T
    swap_y = [(0, 3), (3, 0), (1, 2), (2, 1)]
    other = lax.ppermute(half, ("yh", "yl"), swap_y)
    own_cols = jnp.stack([half, other])
    far_cols = lax.ppermute(own_cols, "core", [(0, 1), (1, 0)])

    tile_at = lax.axis_index(("yl", "z"))
    b_first = occ_at * b_local + tile_at * tile + x_at * width
    usable_b = lax.dynamic_slice_in_dim(usable, b_first, width)
    outer = (usable_b[:, None] & usable[None, :]).astype(jnp.float32)
    spread = jnp.asarray(np.concatenate([spread_np, spread_np]), jnp.bfloat16)
    rows_per = occ_local * occ
    spread = lax.dynamic_slice_in_dim(spread, x_at * rows_per, occ * occ)
    at = jnp.stack([lax.axis_index("yl"), core_at]).astype(jnp.int32)

    first, tiles, parts, landed = 0, None, None, []
    for mid, w in zip(mids, WIDTHS):
        mid = mid.reshape(shards, cwin * QPAD, w * NPAIR)
        if tiles is not None:
            tiles, mid = lax.optimization_barrier((tiles, mid))
        tiles = lax.all_to_all(mid, TILE, 0, 0, tiled=True)
        if parts is not None:
            tiles, parts = lax.optimization_barrier((tiles, parts))
        keep = jnp.pad(outer[first : first + w], ((0, -w % 8), (0, 0)))
        parts = ladder_rows(
            tiles.reshape(2, sources, cwin, QPAD, w * NPAIR),
            own_cols, far_cols, keep, spread, at, occ_local, occ,
        )
        if landed:
            arrived, parts = lax.optimization_barrier(
                ([part for part, _, _ in landed], parts)
            )
            landed = [(p,) + old[1:] for p, old in zip(arrived, landed)]
        for r in range(nx):
            perm = [
                (o * nx + x, ((x + r) % nx) * nx + o)
                for o in range(occ_shards)
                for x in range(nx)
            ]
            part = lax.ppermute(parts[r], OCC + ("x",), perm)
            landed.append((part, (occ_at - r + nx) % nx, first))
        first += w
    out = jnp.zeros((occ_local, nx, width, occ, v), jnp.bfloat16)
    for part, x_from, first in landed:
        out = lax.dynamic_update_slice(out, part[:, None], (0, x_from, first, 0, 0))
    out = out.reshape(occ_local, nx * width, occ, v)
    return jnp.transpose(out, (0, 2, 3, 1))


def solution(mesh):
    split = Mesh(
        mesh.devices.reshape(2, 2, 4, 2, 4), ("yh", "core", "x", "yl", "z")
    )
    virt = ("x", "yl", "z")
    return jax.shard_map(
        per_device,
        mesh=split,
        in_specs=(P(virt, OCC, None), P(OCC, None, None, virt), P()),
        out_specs=P(OCC, None, None, virt),
        check_vma=False,
    )
```

time: 283 us -> 195 us (0.69)
  waiting for transfers between devices: 186 us -> 102 us
  Pallas kernels: 12.6 us -> 29.2 us
  between operations: 13.8 us -> 0.36 us
  local copies, waits for them, and re-layouts: 25.9 us -> 12.7 us
  starting transfers between devices: 36.7 us -> 47.4 us
  matrix products: 6.2 us -> 0.37 us
    all_to_all x1 -> x2, waiting for transfers between devices: 91 us -> 30.8 us  [per_device(): tiles = lax.all_to_all(mid, TILE, 0, 0, tiled=True)]
    all_to_all x3 -> x1, waiting for transfers between devices: 58.4 us -> 0.01 us  [share(): lax.all_to_all(jnp.broadcast_to(x[None], (count,) + x.shape), axes, 0, 0,...]
    ppermute x4 -> x13, waiting for transfers between devices: 36.4 us -> 63.8 us  [the longest x1 35.2 us: per_device(): other = lax.ppermute(half, ('yh', 'yl'), swap_y)]
    pallas_call x1 -> x4, Pallas kernels: 12.6 us -> 29.2 us  [the longest x2 15.5 us: ladder_rows(): pl.pallas_call(functools.partial(ladder_kernel, groups), grid_spec=pltpu....]
    ppermute x4 -> x13, starting transfers between devices: 7.82 us -> 18.8 us  [the longest x8 13.4 us: per_device(): part = lax.ppermute(parts[r], OCC + ('x',), perm)]
    all_to_all x3 -> x1, starting transfers between devices: 21.6 us -> 10.7 us  [share(): lax.all_to_all(jnp.broadcast_to(x[None], (count,) + x.shape), axes, 0, 0,...]
    dot_general x1 -> x0, local copies, waits for them, and re-layouts: 9.54 us -> none  [per_device(): lax.dot_general(tiles, columns, (((0,), (0,)), ((), ())), preferred_eleme...]
    all_to_all x0 -> x1, waiting for transfers between devices: none -> 7.46 us  [per_device(): half = lax.all_to_all(half, TILE[1:], 0, 0, tiled=True)]
  transfers between devices with their start and end apart: 9 -> 17, of which waited for: 8 -> 10; matrix products, arithmetic and copies ran while one was open for 4% -> 4% of each run, Pallas kernels for 4% -> 15%
where the time goes in v2:
time: 195 us; the launch traced here: 194 us
  waiting for transfers between devices  102 us (52%)
  starting transfers between devices  47.4 us (24%)
  Pallas kernels  29.2 us (15%)
  local copies, waits for them, and re-layouts  12.7 us (7%)
  other arithmetic  2.06 us (1%)
    ppermute x1, waiting for transfers between devices, per_device(): other = lax.ppermute(half, ('yh', 'yl'), swap_y)  35.2 us
    all_to_all x2, waiting for transfers between devices, per_device(): tiles = lax.all_to_all(mid, TILE, 0, 0, tiled=True)  30.8 us
    ppermute x8, waiting for transfers between devices, per_device(): part = lax.ppermute(parts[r], OCC + ('x',), perm)  22.4 us
    pallas_call x2, Pallas kernels, ladder_rows(): pl.pallas_call(functools.partial(ladder_kernel, groups), grid_spec=pltpu....  15.5 us
    ppermute x8, starting transfers between devices, per_device(): part = lax.ppermute(parts[r], OCC + ('x',), perm)  13.4 us
    pallas_call x1, Pallas kernels, middle(): pl.pallas_call(functools.partial(middle_kernel, q_local, dests, widths),...  11.8 us
    all_to_all x2, starting transfers between devices, per_device(): tiles = lax.all_to_all(mid, TILE, 0, 0, tiled=True)  11.5 us
    all_to_all x1, starting transfers between devices, share(): lax.all_to_all(jnp.broadcast_to(x[None], (count,) + x.shape), axes, 0, 0,...  10.7 us
  transfers between devices with their start and end apart: 17, of which 10 were waited for; matrix products, arithmetic and copies ran while one was open for 4% of the time, Pallas kernels for 15%

profile of v2, /device:TPU:24, one launch (start us, length us, event | category | flops | bytes accessed | tf_op | source)
XLA Modules:
  0.0 194.2 jit_solution(11033062295996858504)
XLA Ops:
  0.0 0.9 copy.18
  0.9 0.1 broadcast_in_dim.63
  1.0 1.1 broadcast_in_dim.64
  2.1 10.7 %all-to-all-start.1 = ((bf16[128,20,128]{2,1,0:T(8,128)(2,1)}), bf16[128,20,128]{2,1,0:T(8,128)(2,1)}, u32[]{:S(2)}, u32[]{:S(2)}) async-start(bf16[128,20,128]{2,1,0:T(8,128)(2,1)} %broadcast_in_dim.64), calls=%async_computation.1 | async-start | bytes 1572864 | tf_op jit(solution)/shard_map/all_to_all | solution.py:36
  12.7 0.0 slice-start
  12.7 1.9 slice-done
  14.7 2.9 %copy.25 = bf16[75,160,2]{1,0,2:T(8,128)(2,1)S(1)} copy(bf16[75,160,2]{2,1,0:T(8,128)(2,1)S(1)} %slice-done) | data formatting | bytes 96000
  17.6 1.2 collective-permute-start.2
  18.9 2.1 %collective-permute-start.1 = (bf16[2,80,160]{2,1,0:T(8,128)(2,1)S(1)}, bf16[2,80,160]{2,1,0:T(8,128)(2,1)S(1)}, u32[]{:S(2)}, u32[]{:S(2)}) collective-permute-start(bf16[2,80,160]{2,1,0:T(8,128)(2,1)S(1)} %pad.12.refs_0_), channel_id=1, source_target_pairs={{0,64},{32,96},{64,0},{96,32},{1,65},{33,97},{65,1},{97,33},{2,66}... | collective-permute-start | bytes 153608 | tf_op jit(solution)/shard_map/ppermute | solution.py:238
  21.0 0.0 collective-permute-start
  21.0 0.1 pad_add_fusion.1.at_ref
  21.1 2.6 %collective-permute-done.2.refs_3_ = bf16[2,80,160]{2,1,0:T(8,128)(2,1)S(1)} collective-permute-done((bf16[2,80,160]{2,1,0:T(8,128)(2,1)S(1)}, bf16[2,80,160]{2,1,0:T(8,128)(2,1)S(1)}, u32[]{:S(2)}, u32[]{:S(2)}) %collective-permute-start.2) | collective-permute-done | bytes 51232 | tf_op jit(solution)/shard_map/ppermute | solution.py:238
  23.7 3.6 %collective-permute-done.1.refs_2_ = bf16[2,80,160]{2,1,0:T(8,128)(2,1)S(1)} collective-permute-done((bf16[2,80,160]{2,1,0:T(8,128)(2,1)S(1)}, bf16[2,80,160]{2,1,0:T(8,128)(2,1)S(1)}, u32[]{:S(2)}, u32[]{:S(2)}) %collective-permute-start.1) | collective-permute-done | bytes 51232 | tf_op jit(solution)/shard_map/ppermute | solution.py:238
  27.3 0.0 collective-permute-done.refs_1_
  27.3 1.9 shard_map.55
  29.2 0.0 all-to-all-done.1
  29.2 6.5 %all-to-all-start = ((bf16[16,80,640]{2,1,0:T(8,128)(2,1)}), bf16[16,80,640]{2,1,0:T(8,128)(2,1)S(1)}, u32[]{:S(2)}, u32[]{:S(2)}) async-start(bf16[16,80,640]{2,1,0:T(8,128)(2,1)} %shard_map.55), calls=%async_computation | async-start | bytes 3276800 | tf_op jit(solution)/shard_map/all_to_all | solution.py:242
  35.8 0.0 copy-done.5
  35.8 0.1 select_reduce_fusion
  35.9 0.1 broadcast_bitcast_fusion
  36.0 1.3 reshape.60
  37.2 0.0 copy-done.6
  37.2 0.4 fusion.1.a_ref
  37.6 11.8 %shard_map.56 = (bf16[32,2,80,384]{3,2,1,0:T(8,128)(2,1)}, bf16[32,2,80,256]{3,2,1,0:T(8,128)(2,1)S(1)}) custom-call(bf16[75,160,640]{2,1,0:T(8,128)(2,1)} %b_ref.1, bf16[640,256]{1,0:T(8,128)(2,1)S(1)} %fusion.1.a_ref), custom_call_target="tpu_custom_call" | custom-call | flops 3932160000 | bytes 21913600 | tf_op jit(solution)/shard_map/pallas_call | solution.py:70
  49.4 1.5 copy-done.1
  50.8 7.5 %all-to-all-done = bf16[16,80,640]{2,1,0:T(8,128)(2,1)S(1)} async-done(((bf16[16,80,640]{2,1,0:T(8,128)(2,1)}), bf16[16,80,640]{2,1,0:T(8,128)(2,1)S(1)}, u32[]{:S(2)}, u32[]{:S(2)}) %all-to-all-start) | async-done | bytes 1638432 | tf_op jit(solution)/shard_map/all_to_all | solution.py:242
  58.3 5.2 %all-to-all-start.2 = ((bf16[32,160,384]{2,1,0:T(8,128)(2,1)}), bf16[32,160,384]{2,1,0:T(8,128)(2,1)}, u32[]{:S(2)}, u32[]{:S(2)}) async-start(bf16[32,160,384]{2,1,0:T(8,128)(2,1)} %bitcast.51), calls=%async_computation.2 | async-start | bytes 7864320 | tf_op jit(solution)/shard_map/all_to_all | solution.py:266
  63.5 1.2 copy.20
  64.7 0.0 copy-start.2
  64.7 2.0 %collective-permute-start.3 = (bf16[640,1280]{1,0:T(8,128)(2,1)S(1)}, bf16[640,1280]{1,0:T(8,128)(2,1)S(1)}, u32[]{:S(2)}, u32[]{:S(2)}) collective-permute-start(bf16[640,1280]{1,0:T(8,128)(2,1)S(1)} %bitcast.49), channel_id=1, source_target_pairs={{0,68},{68,0},{4,64},{64,4},{1,69},{69,1},{5,65},{65,5},{2,70},{70... | collective-permute-start | bytes 4915208 | tf_op jit(solution)/shard_map/ppermute | solution.py:248
  66.7 35.2 %collective-permute-done.3 = bf16[640,1280]{1,0:T(8,128)(2,1)S(1)} collective-permute-done((bf16[640,1280]{1,0:T(8,128)(2,1)S(1)}, bf16[640,1280]{1,0:T(8,128)(2,1)S(1)}, u32[]{:S(2)}, u32[]{:S(2)}) %collective-permute-start.3) | collective-permute-done | bytes 1638432 | tf_op jit(solution)/shard_map/ppermute | solution.py:248
  101.9 0.0 copy-done.2
  101.9 1.7 pad_maximum_fusion.w_own_ref
  103.7 0.0 copy-start
  103.7 0.1 collective-permute-start.4
  103.8 7.8 %all-to-all-done.2 = bf16[32,160,384]{2,1,0:T(8,128)(2,1)} async-done(((bf16[32,160,384]{2,1,0:T(8,128)(2,1)}), bf16[32,160,384]{2,1,0:T(8,128)(2,1)}, u32[]{:S(2)}, u32[]{:S(2)}) %all-to-all-start.2) | async-done | bytes 3932192 | tf_op jit(solution)/shard_map/all_to_all | solution.py:266
  111.5 6.2 %all-to-all-start.3 = ((bf16[32,160,256]{2,1,0:T(8,128)(2,1)}), bf16[32,160,256]{2,1,0:T(8,128)(2,1)}, u32[]{:S(2)}, u32[]{:S(2)}) async-start(bf16[32,160,256]{2,1,0:T(8,128)(2,1)} %bitcast.47), calls=%async_computation.3 | async-start | bytes 5242880 | tf_op jit(solution)/shard_map/all_to_all | solution.py:266
  117.8 0.1 dynamic_slice.6
  117.9 0.1 and_convert_fusion
  118.0 0.1 pad_add_fusion.at_ref
  118.1 0.0 collective-permute-done.4.w_far_ref
  118.1 8.7 %shard_map.57 = (bf16[4,3,16,640]{3,2,1,0:T(8,128)(2,1)}, bf16[4,3,16,640]{3,2,1,0:T(8,128)(2,1)}, bf16[4,3,16,640]{3,2,1,0:T(8,128)(2,1)}, bf16[4,3,16,640]{3,2,1,0:T(8,128)(2,1)}) custom-call(s32[2]{0:T(128)S(1)} %pad_add_fusion.at_ref, bf16[2,16,2,80,384]{4,3,2,1,0:T(8,128)(2,1)} %bitcast.9.m_ref, bf16[2,640,1280]{2,1,0:T(8,128)(2,1)S(1)} %pad_maximum_fusion.w_own_ref, ...), custom_call_target="tpu_custom_call" | custom-call | flops 2516582400 | bytes 10485760 | tf_op jit(solution)/shard_map/pallas_call | solution.py:180
  126.8 7.6 %collective-permute-start.5 = (bf16[4,3,16,640]{3,2,1,0:T(8,128)(2,1)}, bf16[4,3,16,640]{3,2,1,0:T(8,128)(2,1)S(1)}, u32[]{:S(2)}, u32[]{:S(2)}) collective-permute-start(bf16[4,3,16,640]{3,2,1,0:T(8,128)(2,1)} %get-tuple-element.32), channel_id=1, source_target_pairs={{0,0},{8,32},{16,64},{24,96},{32,8},{40,40},{48,72},{56,104},{64,1... | collective-permute-start | bytes 737288 | tf_op jit(solution)/shard_map/ppermute | solution.py:285
  134.4 0.1 collective-permute-start.6
  134.5 0.1 collective-permute-start.7
  134.6 1.0 collective-permute-start.8
  135.6 23.0 %all-to-all-done.3 = bf16[32,160,256]{2,1,0:T(8,128)(2,1)} async-done(((bf16[32,160,256]{2,1,0:T(8,128)(2,1)}), bf16[32,160,256]{2,1,0:T(8,128)(2,1)}, u32[]{:S(2)}, u32[]{:S(2)}) %all-to-all-start.3) | async-done | bytes 2621472 | tf_op jit(solution)/shard_map/all_to_all | solution.py:266
  158.5 6.8 %shard_map.58 = (bf16[4,2,16,640]{3,2,1,0:T(8,128)(2,1)S(1)}, bf16[4,2,16,640]{3,2,1,0:T(8,128)(2,1)S(1)}, bf16[4,2,16,640]{3,2,1,0:T(8,128)(2,1)S(1)}, bf16[4,2,16,640]{3,2,1,0:T(8,128)(2,1)S(1)}) custom-call(s32[2]{0:T(128)S(1)} %pad_add_fusion.at_ref, bf16[2,16,2,80,256]{4,3,2,1,0:T(8,128)(2,1)} %bitcast.15.m_ref, bf16[2,640,1280]{2,1,0:T(8,128)(2,1)} %copy-done, ...), custom_call_target="tpu_custom_call" | custom-call | flops 1677721600 | bytes 9175040 | tf_op jit(solution)/shard_map/pallas_call | solution.py:180
  165.4 0.0 collective-permute-done.5
  165.4 0.0 collective-permute-done.6
  165.4 0.0 collective-permute-done.7
  165.4 8.2 %collective-permute-done.8 = bf16[4,3,16,640]{3,2,1,0:T(8,128)(2,1)S(1)} collective-permute-done((bf16[4,3,16,640]{3,2,1,0:T(8,128)(2,1)}, bf16[4,3,16,640]{3,2,1,0:T(8,128)(2,1)S(1)}, u32[]{:S(2)}, u32[]{:S(2)}) %collective-permute-start.8) | collective-permute-done | bytes 245792 | tf_op jit(solution)/shard_map/ppermute | solution.py:285
  173.6 2.2 %collective-permute-start.9 = (bf16[4,2,16,640]{3,2,1,0:T(8,128)(2,1)S(1)}, bf16[4,2,16,640]{3,2,1,0:T(8,128)(2,1)S(1)}, u32[]{:S(2)}, u32[]{:S(2)}) collective-permute-start(bf16[4,2,16,640]{3,2,1,0:T(8,128)(2,1)S(1)} %get-tuple-element.47), channel_id=1, source_target_pairs={{0,0},{8,32},{16,64},{24,96},{32,8},{40,40},{48,72},{56,104},{64,1... | collective-permute-start | bytes 491528 | tf_op jit(solution)/shard_map/ppermute | solution.py:285
  175.7 0.1 collective-permute-start.10
  175.8 2.4 %collective-permute-start.11 = (bf16[4,2,16,640]{3,2,1,0:T(8,128)(2,1)S(1)}, bf16[4,2,16,640]{3,2,1,0:T(8,128)(2,1)S(1)}, u32[]{:S(2)}, u32[]{:S(2)}) collective-permute-start(bf16[4,2,16,640]{3,2,1,0:T(8,128)(2,1)S(1)} %get-tuple-element.49), channel_id=1, source_target_pairs={{0,64},{8,96},{16,0},{24,32},{32,72},{40,104},{48,8},{56,40},{64,8... | collective-permute-start | bytes 491528 | tf_op jit(solution)/shard_map/ppermute | solution.py:285
  178.2 0.0 collective-permute-start.12
  178.2 0.1 broadcast_in_dim.59
  178.5 7.6 %collective-permute-done.9 = bf16[4,2,16,640]{3,2,1,0:T(8,128)(2,1)S(1)} collective-permute-done((bf16[4,2,16,640]{3,2,1,0:T(8,128)(2,1)S(1)}, bf16[4,2,16,640]{3,2,1,0:T(8,128)(2,1)S(1)}, u32[]{:S(2)}, u32[]{:S(2)}) %collective-permute-start.9) | collective-permute-done | bytes 163872 | tf_op jit(solution)/shard_map/ppermute | solution.py:285
  186.1 0.0 collective-permute-done.10
  186.2 3.6 %collective-permute-done.11 = bf16[4,2,16,640]{3,2,1,0:T(8,128)(2,1)S(1)} collective-permute-done((bf16[4,2,16,640]{3,2,1,0:T(8,128)(2,1)S(1)}, bf16[4,2,16,640]{3,2,1,0:T(8,128)(2,1)S(1)}, u32[]{:S(2)}, u32[]{:S(2)}) %collective-permute-start.11) | collective-permute-done | bytes 163872 | tf_op jit(solution)/shard_map/ppermute | solution.py:285
  189.8 0.1 copy.21
  190.0 3.0 %collective-permute-done.12 = bf16[4,2,16,640]{3,2,1,0:T(8,128)(2,1)S(1)} collective-permute-done((bf16[4,2,16,640]{3,2,1,0:T(8,128)(2,1)S(1)}, bf16[4,2,16,640]{3,2,1,0:T(8,128)(2,1)S(1)}, u32[]{:S(2)}, u32[]{:S(2)}) %collective-permute-start.12) | collective-permute-done | bytes 163872 | tf_op jit(solution)/shard_map/ppermute | solution.py:285
  193.0 0.0 copy-start.3
  193.0 1.2 copy-done.3
  (23 shorter events, 0.3 us)
Async XLA Ops:
  2.1 27.2 %all-to-all-start.1 = ((bf16[128,20,128]{2,1,0:T(8,128)(2,1)}), bf16[128,20,128]{2,1,0:T(8,128)(2,1)}, u32[]{:S(2)}, u32[]{:S(2)}) async-start(bf16[128,20,128]{2,1,0:T(8,128)(2,1)} %broadcast_in_dim.64), calls=%async_computation.1 | async-start | bytes 1572864 | tf_op jit(solution)/shard_map/all_to_all | solution.py:36
  12.7 1.9 slice-start
  17.6 6.0 %collective-permute-start.2 = (bf16[2,80,160]{2,1,0:T(8,128)(2,1)S(1)}, bf16[2,80,160]{2,1,0:T(8,128)(2,1)S(1)}, u32[]{:S(2)}, u32[]{:S(2)}) collective-permute-start(bf16[2,80,160]{2,1,0:T(8,128)(2,1)S(1)} %pad.12.refs_0_), channel_id=1, source_target_pairs={{0,96},{32,0},{64,32},{96,64},{1,97},{33,1},{65,33},{97,65},{2,98}... | collective-permute-start | bytes 153608 | tf_op jit(solution)/shard_map/ppermute | solution.py:238
  18.9 8.4 %collective-permute-start.1 = (bf16[2,80,160]{2,1,0:T(8,128)(2,1)S(1)}, bf16[2,80,160]{2,1,0:T(8,128)(2,1)S(1)}, u32[]{:S(2)}, u32[]{:S(2)}) collective-permute-start(bf16[2,80,160]{2,1,0:T(8,128)(2,1)S(1)} %pad.12.refs_0_), channel_id=1, source_target_pairs={{0,64},{32,96},{64,0},{96,32},{1,65},{33,97},{65,1},{97,33},{2,66}... | collective-permute-start | bytes 153608 | tf_op jit(solution)/shard_map/ppermute | solution.py:238
  21.0 6.3 %collective-permute-start = (bf16[2,80,160]{2,1,0:T(8,128)(2,1)S(1)}, bf16[2,80,160]{2,1,0:T(8,128)(2,1)S(1)}, u32[]{:S(2)}, u32[]{:S(2)}) collective-permute-start(bf16[2,80,160]{2,1,0:T(8,128)(2,1)S(1)} %pad.12.refs_0_), channel_id=1, source_target_pairs={{0,32},{32,64},{64,96},{96,0},{1,33},{33,65},{65,97},{97,1},{2,34}... | collective-permute-start | bytes 153608 | tf_op jit(solution)/shard_map/ppermute | solution.py:238
  29.2 6.5 %copy-start.5 = (s32[8]{0:T(128)S(1)}, s32[8]{0:T(128)}, u32[]{:S(2)}) copy-start(s32[8]{0:T(128)} %param.7) | copy-start | bytes 100
  29.2 8.0 %copy-start.6 = (bf16[4,128,256]{1,2,0:T(8,128)(2,1)S(1)}, bf16[4,128,256]{1,2,0:T(8,128)(2,1)}, u32[]{:S(2)}) copy-start(bf16[4,128,256]{1,2,0:T(8,128)(2,1)} %constant.105.clone) | copy-start | bytes 786436
  29.2 29.1 %all-to-all-start = ((bf16[16,80,640]{2,1,0:T(8,128)(2,1)}), bf16[16,80,640]{2,1,0:T(8,128)(2,1)S(1)}, u32[]{:S(2)}, u32[]{:S(2)}) async-start(bf16[16,80,640]{2,1,0:T(8,128)(2,1)} %shard_map.55), calls=%async_computation | async-start | bytes 3276800 | tf_op jit(solution)/shard_map/all_to_all | solution.py:242
  49.4 1.5 copy-start.1
  58.3 53.2 %all-to-all-start.2 = ((bf16[32,160,384]{2,1,0:T(8,128)(2,1)}), bf16[32,160,384]{2,1,0:T(8,128)(2,1)}, u32[]{:S(2)}, u32[]{:S(2)}) async-start(bf16[32,160,384]{2,1,0:T(8,128)(2,1)} %bitcast.51), calls=%async_computation.2 | async-start | bytes 7864320 | tf_op jit(solution)/shard_map/all_to_all | solution.py:266
  64.7 37.2 %copy-start.2 = (bf16[1280,640]{0,1:T(8,128)(2,1)}, bf16[1280,640]{0,1:T(8,128)(2,1)S(1)}, u32[]{:S(2)}) copy-start(bf16[1280,640]{0,1:T(8,128)(2,1)S(1)} %copy.20) | copy-start | bytes 4915204
  64.7 37.2 %collective-permute-start.3 = (bf16[640,1280]{1,0:T(8,128)(2,1)S(1)}, bf16[640,1280]{1,0:T(8,128)(2,1)S(1)}, u32[]{:S(2)}, u32[]{:S(2)}) collective-permute-start(bf16[640,1280]{1,0:T(8,128)(2,1)S(1)} %bitcast.49), channel_id=1, source_target_pairs={{0,68},{68,0},{4,64},{64,4},{1,69},{69,1},{5,65},{65,5},{2,70},{70... | collective-permute-start | bytes 4915208 | tf_op jit(solution)/shard_map/ppermute | solution.py:248
  103.7 14.4 %copy-start = (bf16[2,640,1280]{2,1,0:T(8,128)(2,1)}, bf16[2,640,1280]{2,1,0:T(8,128)(2,1)S(1)}, u32[]{:S(2)}) copy-start(bf16[2,640,1280]{2,1,0:T(8,128)(2,1)S(1)} %pad_maximum_fusion.w_own_ref) | copy-start | bytes 9830404
  103.7 14.4 %collective-permute-start.4 = (bf16[2,640,1280]{2,1,0:T(8,128)(2,1)S(1)}, bf16[2,640,1280]{2,1,0:T(8,128)(2,1)}, u32[]{:S(2)}, u32[]{:S(2)}) collective-permute-start(bf16[2,640,1280]{2,1,0:T(8,128)(2,1)S(1)} %pad_maximum_fusion.w_own_ref), channel_id=1, source_target_pairs={{0,32},{32,0},{1,33},{33,1},{2,34},{34,2},{3,35},{35,3},{4,36},{36... | collective-permute-start | bytes 9830408 | tf_op jit(solution)/shard_map/ppermute | solution.py:250
  111.5 6.5 %copy-start.4 = (bf16[512,128]{1,0:T(8,128)(2,1)S(1)}, bf16[512,128]{1,0:T(8,128)(2,1)}, u32[]{:S(2)}) copy-start(bf16[512,128]{1,0:T(8,128)(2,1)} %constant.106.clone) | copy-start | bytes 393220
  111.5 47.0 %all-to-all-start.3 = ((bf16[32,160,256]{2,1,0:T(8,128)(2,1)}), bf16[32,160,256]{2,1,0:T(8,128)(2,1)}, u32[]{:S(2)}, u32[]{:S(2)}) async-start(bf16[32,160,256]{2,1,0:T(8,128)(2,1)} %bitcast.47), calls=%async_computation.3 | async-start | bytes 5242880 | tf_op jit(solution)/shard_map/all_to_all | solution.py:266
  126.8 38.6 %collective-permute-start.5 = (bf16[4,3,16,640]{3,2,1,0:T(8,128)(2,1)}, bf16[4,3,16,640]{3,2,1,0:T(8,128)(2,1)S(1)}, u32[]{:S(2)}, u32[]{:S(2)}) collective-permute-start(bf16[4,3,16,640]{3,2,1,0:T(8,128)(2,1)} %get-tuple-element.32), channel_id=1, source_target_pairs={{0,0},{8,32},{16,64},{24,96},{32,8},{40,40},{48,72},{56,104},{64,1... | collective-permute-start | bytes 737288 | tf_op jit(solution)/shard_map/ppermute | solution.py:285
  134.4 31.0 %collective-permute-start.6 = (bf16[4,3,16,640]{3,2,1,0:T(8,128)(2,1)}, bf16[4,3,16,640]{3,2,1,0:T(8,128)(2,1)S(1)}, u32[]{:S(2)}, u32[]{:S(2)}) collective-permute-start(bf16[4,3,16,640]{3,2,1,0:T(8,128)(2,1)} %get-tuple-element.33), channel_id=1, source_target_pairs={{0,32},{8,64},{16,96},{24,0},{32,40},{40,72},{48,104},{56,8},{64,4... | collective-permute-start | bytes 737288 | tf_op jit(solution)/shard_map/ppermute | solution.py:285
  134.5 30.9 %collective-permute-start.7 = (bf16[4,3,16,640]{3,2,1,0:T(8,128)(2,1)}, bf16[4,3,16,640]{3,2,1,0:T(8,128)(2,1)S(1)}, u32[]{:S(2)}, u32[]{:S(2)}) collective-permute-start(bf16[4,3,16,640]{3,2,1,0:T(8,128)(2,1)} %get-tuple-element.34), channel_id=1, source_target_pairs={{0,64},{8,96},{16,0},{24,32},{32,72},{40,104},{48,8},{56,40},{64,8... | collective-permute-start | bytes 737288 | tf_op jit(solution)/shard_map/ppermute | solution.py:285
  134.6 39.0 %collective-permute-start.8 = (bf16[4,3,16,640]{3,2,1,0:T(8,128)(2,1)}, bf16[4,3,16,640]{3,2,1,0:T(8,128)(2,1)S(1)}, u32[]{:S(2)}, u32[]{:S(2)}) collective-permute-start(bf16[4,3,16,640]{3,2,1,0:T(8,128)(2,1)} %get-tuple-element.35), channel_id=1, source_target_pairs={{0,96},{8,0},{16,32},{24,64},{32,104},{40,8},{48,40},{56,72},{64,1... | collective-permute-start | bytes 737288 | tf_op jit(solution)/shard_map/ppermute | solution.py:285
  173.6 12.5 %collective-permute-start.9 = (bf16[4,2,16,640]{3,2,1,0:T(8,128)(2,1)S(1)}, bf16[4,2,16,640]{3,2,1,0:T(8,128)(2,1)S(1)}, u32[]{:S(2)}, u32[]{:S(2)}) collective-permute-start(bf16[4,2,16,640]{3,2,1,0:T(8,128)(2,1)S(1)} %get-tuple-element.47), channel_id=1, source_target_pairs={{0,0},{8,32},{16,64},{24,96},{32,8},{40,40},{48,72},{56,104},{64,1... | collective-permute-start | bytes 491528 | tf_op jit(solution)/shard_map/ppermute | solution.py:285
  175.7 10.4 %collective-permute-start.10 = (bf16[4,2,16,640]{3,2,1,0:T(8,128)(2,1)S(1)}, bf16[4,2,16,640]{3,2,1,0:T(8,128)(2,1)S(1)}, u32[]{:S(2)}, u32[]{:S(2)}) collective-permute-start(bf16[4,2,16,640]{3,2,1,0:T(8,128)(2,1)S(1)} %get-tuple-element.48), channel_id=1, source_target_pairs={{0,32},{8,64},{16,96},{24,0},{32,40},{40,72},{48,104},{56,8},{64,4... | collective-permute-start | bytes 491528 | tf_op jit(solution)/shard_map/ppermute | solution.py:285
  175.8 14.0 %collective-permute-start.11 = (bf16[4,2,16,640]{3,2,1,0:T(8,128)(2,1)S(1)}, bf16[4,2,16,640]{3,2,1,0:T(8,128)(2,1)S(1)}, u32[]{:S(2)}, u32[]{:S(2)}) collective-permute-start(bf16[4,2,16,640]{3,2,1,0:T(8,128)(2,1)S(1)} %get-tuple-element.49), channel_id=1, source_target_pairs={{0,64},{8,96},{16,0},{24,32},{32,72},{40,104},{48,8},{56,40},{64,8... | collective-permute-start | bytes 491528 | tf_op jit(solution)/shard_map/ppermute | solution.py:285
  178.2 14.8 %collective-permute-start.12 = (bf16[4,2,16,640]{3,2,1,0:T(8,128)(2,1)S(1)}, bf16[4,2,16,640]{3,2,1,0:T(8,128)(2,1)S(1)}, u32[]{:S(2)}, u32[]{:S(2)}) collective-permute-start(bf16[4,2,16,640]{3,2,1,0:T(8,128)(2,1)S(1)} %get-tuple-element.50), channel_id=1, source_target_pairs={{0,96},{8,0},{16,32},{24,64},{32,104},{40,8},{48,40},{56,72},{64,1... | collective-permute-start | bytes 491528 | tf_op jit(solution)/shard_map/ppermute | solution.py:285
  193.0 1.2 copy-start.3

commit v3 on v2

--- a/solution.py
+++ b/solution.py
@@ -11,24 +11,34 @@
 OCC = ("yh", "core")
 TILE = ("yl", "z", "x")
 NPAIR = 128
+OWNED = 56
 QPAD = 80
-WIDTHS = (3, 2)
+WIDTHS = (4, 1)
 
 
 def pair_tables(occ, cwin, occ_shards):
     pairs = [(i, j) for i in range(occ) for j in range(i + 1, occ)]
     per = occ // occ_shards
     pick = np.zeros((occ_shards, cwin, per, occ, cwin, NPAIR), np.float32)
-    spread = np.zeros((occ, occ, NPAIR), np.float32)
+    select = np.zeros((occ_shards, OWNED, NPAIR), np.float32)
+    spread = np.zeros((occ_shards, per, occ, OWNED), np.float32)
+    count = [0] * occ_shards
     for p, (i, j) in enumerate(pairs):
         for c in range(cwin):
             pick[i // per, c, i % per, j, c, p] = 1.0
             pick[j // per, c, j % per, i, c, p] = -1.0
-        spread[i, j, p] = 1.0
-        spread[j, i, p] = -1.0
+        for o in sorted({i // per, j // per}):
+            n = count[o]
+            count[o] += 1
+            select[o, n, p] = 1.0
+            if i // per == o:
+                spread[o, i % per, j, n] = 1.0
+            if j // per == o:
+                spread[o, j % per, i, n] = -1.0
     return (
         pick.reshape(occ_shards, cwin * per * occ, cwin * NPAIR),
-        spread.reshape(occ * occ, NPAIR),
+        select.reshape(occ_shards * OWNED, NPAIR),
+        spread.reshape(occ_shards, per * occ, OWNED),
     )
 
 
@@ -122,84 +132,115 @@
 
 
 def ladder_kernel(
-    groups, at_ref, m_ref, w_own_ref, w_far_ref, keep_ref, spread_ref, *refs
+    first, at_ref, own_ref, keep_ref, select_ref, m_hbm, far_hbm, *refs
 ):
-    outs, acc = refs[:-1], refs[-1]
-    step, last = pl.program_id(0), pl.num_programs(0) - 1
-    depth = m_ref.shape[0] * m_ref.shape[2]
-    width = acc.shape[1] // NPAIR
-    occ_local, occ = outs[0].shape[0], outs[0].shape[2]
-
-    @pl.when(step == 0)
-    def _():
-        acc[...] = jnp.zeros_like(acc)
-
-    def add(w_ref):
-        acc[...] += jnp.dot(
-            w_ref[...],
-            m_ref[...].reshape(depth, -1),
+    outs, (m_buf, far_buf, acc, sems) = refs[:-4], refs[-4:]
+    _, sources, depth, lanes = m_buf.shape
+    width = lanes // NPAIR
+    steps = [(c, yl) for c in range(2) for yl in range(2)]
+    tiles = [
+        pltpu.make_async_copy(
+            m_hbm.at[(at_ref[0] + yl) % 2, :, (at_ref[1] + c) % 2],
+            m_buf.at[n],
+            sems.at[n],
+        )
+        for n, (c, yl) in enumerate(steps)
+    ]
+    fars = [
+        pltpu.make_async_copy(far_hbm.at[yl], far_buf.at[yl], sems.at[4 + yl])
+        for yl in range(2)
+    ]
+    for copy in (tiles[0], tiles[1], fars[0], tiles[2], fars[1], tiles[3]):
+        copy.start()
+    for n, (c, yl) in enumerate(steps):
+        tiles[n].wait()
+        if c:
+            fars[yl].wait()
+        part = jnp.dot(
+            (far_buf if c else own_ref)[yl],
+            m_buf[n].reshape(sources * depth, lanes),
             preferred_element_type=jnp.float32,
         )
-
-    pl.when(step < groups)(lambda: add(w_own_ref))
-    pl.when(step >= groups)(lambda: add(w_far_ref))
-
-    @pl.when(step == last)
-    def _():
-        for h in range(width):
-            part = acc[:, h * NPAIR : (h + 1) * NPAIR].astype(jnp.bfloat16)
-            rows = lax.dot_general(
-                spread_ref[...],
-                part,
-                (((1,), (1,)), ((), ())),
-                preferred_element_type=jnp.float32,
-            )
-            rows = (rows * keep_ref[h : h + 1, :]).astype(jnp.bfloat16)
-            rows = rows.reshape(len(outs), occ_local, occ, -1)
-            for r, out in enumerate(outs):
-                out[:, h] = rows[r]
-
-
-def ladder_rows(tiles, own, far, keep, spread, at, occ_local, occ):
-    _, sources, _, depth, lanes = tiles.shape
+        acc[...] = part if n == 0 else acc[...] + part
+    for h in range(width):
+        part = acc[:, h * NPAIR : (h + 1) * NPAIR].astype(jnp.bfloat16)
+        rows = lax.dot_general(
+            select_ref[...],
+            part,
+            (((1,), (1,)), ((), ())),
+            preferred_element_type=jnp.float32,
+        )
+        rows = (rows * keep_ref[first + h : first + h + 1, :]).astype(jnp.bfloat16)
+        rows = rows.reshape(len(outs), OWNED, -1)
+        for r, out in enumerate(outs):
+            out[h] = rows[r]
+
+
+def ladder_rows(first, tiles, own, far, keep, select, at):
     a_size = own.shape[1]
-    groups = 2
-    width = lanes // NPAIR
-    shards = occ // occ_local
-
-    def m_at(s, at):
-        yl = (at[0] + s % groups) % 2
-        c = (at[1] + s // groups) % 2
-        return yl, 0, c, 0, 0
-
-    own_at = lambda s, at: (jnp.minimum(s, groups - 1), 0, 0)
-    far_at = lambda s, at: (jnp.maximum(s - groups, 0), 0, 0)
-
-    out_block = (occ_local, width, occ, a_size)
-    whole = lambda n: lambda s, at: (0,) * n
+    lanes = tiles.shape[4]
+    owners = select.shape[0] // OWNED
+    out = jax.ShapeDtypeStruct((lanes // NPAIR, OWNED, a_size), jnp.bfloat16)
+    vmem = pl.BlockSpec(memory_space=pltpu.VMEM)
+    hbm = pl.BlockSpec(memory_space=pl.ANY)
     return pl.pallas_call(
-        functools.partial(ladder_kernel, groups),
-        grid_spec=pltpu.PrefetchScalarGridSpec(
-            num_scalar_prefetch=1,
-            grid=(2 * groups,),
-            in_specs=[
-                pl.BlockSpec((None, sources, 1, depth, lanes), m_at),
-                pl.BlockSpec((None, a_size, sources * depth), own_at),
-                pl.BlockSpec((None, a_size, sources * depth), far_at),
-                pl.BlockSpec(keep.shape, whole(2)),
-                pl.BlockSpec(spread.shape, whole(2)),
-            ],
-            out_specs=[pl.BlockSpec(out_block, whole(4))] * shards,
-            scratch_shapes=[pltpu.VMEM((a_size, lanes), jnp.float32)],
-        ),
-        out_shape=[jax.ShapeDtypeStruct(out_block, jnp.bfloat16)] * shards,
-        compiler_params=pltpu.CompilerParams(vmem_limit_bytes=48 << 20),
+        functools.partial(ladder_kernel, first),
+        in_specs=[pl.BlockSpec(memory_space=pltpu.SMEM), vmem, vmem, vmem, hbm, hbm],
+        out_specs=[vmem] * owners,
+        out_shape=[out] * owners,
+        scratch_shapes=[
+            pltpu.VMEM((4, tiles.shape[1]) + tiles.shape[3:], jnp.bfloat16),
+            pltpu.VMEM(far.shape, jnp.bfloat16),
+            pltpu.VMEM((a_size, lanes), jnp.float32),
+            pltpu.SemaphoreType.DMA((6,)),
+        ],
+        compiler_params=pltpu.CompilerParams(vmem_limit_bytes=24 << 20),
         cost_estimate=pl.CostEstimate(
             flops=2 * tiles.size * a_size,
             bytes_accessed=2 * (tiles.size + own.size + far.size),
             transcendentals=0,
         ),
-    )(at, tiles, own, far, keep, spread)
+    )(at, own, keep, select, tiles, far)
+
+
+def unpack_kernel(widths, at_ref, spread_ref, *refs):
+    parts, out_ref = refs[:-1], refs[-1]
+    r = pl.program_id(0)
+    occ_local, _, _, occ, a_size = out_ref.shape
+    count = len(parts) // len(widths)
+
+    def source(n):
+        first = 0
+        for k, width in enumerate(widths):
+            for h in range(width):
+                rows = jnp.dot(
+                    spread_ref[at_ref[count]],
+                    parts[k * count + n][h],
+                    preferred_element_type=jnp.float32,
+                ).astype(jnp.bfloat16)
+                out_ref[:, 0, first + h] = rows.reshape(occ_local, occ, a_size)
+            first += width
+
+    for n in range(count):
+        pl.when(r == n)(functools.partial(source, n))
+
+
+def unpack(parts, spread, x_from, shape):
+    occ_local, count, width, occ, a_size = shape
+    vmem = pl.BlockSpec(memory_space=pltpu.VMEM)
+    return pl.pallas_call(
+        functools.partial(unpack_kernel, WIDTHS),
+        grid_spec=pltpu.PrefetchScalarGridSpec(
+            num_scalar_prefetch=1,
+            grid=(count,),
+            in_specs=[vmem] * (1 + len(parts)),
+            out_specs=pl.BlockSpec(
+                (occ_local, 1, width, occ, a_size), lambda r, at: (0, at[r], 0, 0, 0)
+            ),
+        ),
+        out_shape=jax.ShapeDtypeStruct(shape, jnp.bfloat16),
+        compiler_params=pltpu.CompilerParams(vmem_limit_bytes=16 << 20),
+    )(x_from, spread, *parts)
 
 
 def per_device(factors, amplitudes, block_sizes):
@@ -210,7 +251,7 @@
     width = tile // nx
     irreps = block_sizes.shape[0]
     block = v // irreps
-    pick_np, spread_np = pair_tables(occ, cwin, occ_shards)
+    pick_np, select_np, spread_np = pair_tables(occ, cwin, occ_shards)
     occ_at, x_at, core_at = (lax.axis_index(n) for n in (OCC, "x", "core"))
 
     position = jnp.arange(v, dtype=jnp.int32)
@@ -219,6 +260,7 @@
     usable = position % block < size_at
 
     own = jnp.transpose(amplitudes, (3, 2, 0, 1)).reshape(tile, cwin * occ_local * occ)
+    core_swap = [(0, 1), (1, 0)]
     every = share(own, OCC + ("x", "yl", "z"), occ_shards * shards)
     every = every.reshape(occ_shards, v, cwin * occ_local * occ)
     antisym = jnp.einsum(
@@ -247,17 +289,21 @@
     swap_y = [(0, 3), (3, 0), (1, 2), (2, 1)]
     other = lax.ppermute(half, ("yh", "yl"), swap_y)
     own_cols = jnp.stack([half, other])
-    far_cols = lax.ppermute(own_cols, "core", [(0, 1), (1, 0)])
+    far_cols = lax.ppermute(own_cols, "core", core_swap)
 
     tile_at = lax.axis_index(("yl", "z"))
     b_first = occ_at * b_local + tile_at * tile + x_at * width
     usable_b = lax.dynamic_slice_in_dim(usable, b_first, width)
     outer = (usable_b[:, None] & usable[None, :]).astype(jnp.float32)
-    spread = jnp.asarray(np.concatenate([spread_np, spread_np]), jnp.bfloat16)
-    rows_per = occ_local * occ
-    spread = lax.dynamic_slice_in_dim(spread, x_at * rows_per, occ * occ)
+    outer = jnp.pad(outer, ((0, -width % 8), (0, 0)))
+    select = jnp.asarray(np.concatenate([select_np, select_np]), jnp.bfloat16)
+    select = lax.dynamic_slice_in_dim(select, x_at * OWNED, occ_shards * OWNED)
+    spread = jnp.asarray(spread_np, jnp.bfloat16)
     at = jnp.stack([lax.axis_index("yl"), core_at]).astype(jnp.int32)
 
+    shape = (occ_local, nx, width, occ, v)
+    x_from = (occ_at - jnp.arange(nx, dtype=jnp.int32) + nx) % nx
+    x_from = jnp.append(x_from, occ_at.astype(jnp.int32))
     first, tiles, parts, landed = 0, None, None, []
     for mid, w in zip(mids, WIDTHS):
         mid = mid.reshape(shards, cwin * QPAD, w * NPAIR)
@@ -266,28 +312,24 @@
         tiles = lax.all_to_all(mid, TILE, 0, 0, tiled=True)
         if parts is not None:
             tiles, parts = lax.optimization_barrier((tiles, parts))
-        keep = jnp.pad(outer[first : first + w], ((0, -w % 8), (0, 0)))
         parts = ladder_rows(
+            first,
             tiles.reshape(2, sources, cwin, QPAD, w * NPAIR),
-            own_cols, far_cols, keep, spread, at, occ_local, occ,
+            own_cols, far_cols, outer, select, at,
         )
         if landed:
-            arrived, parts = lax.optimization_barrier(
-                ([part for part, _, _ in landed], parts)
-            )
-            landed = [(p,) + old[1:] for p, old in zip(arrived, landed)]
+            landed, _ = lax.optimization_barrier((landed, parts))
+        sent = {}
         for r in range(nx):
             perm = [
                 (o * nx + x, ((x + r) % nx) * nx + o)
                 for o in range(occ_shards)
                 for x in range(nx)
             ]
-            part = lax.ppermute(parts[r], OCC + ("x",), perm)
-            landed.append((part, (occ_at - r + nx) % nx, first))
+            sent[r] = lax.ppermute(parts[r], OCC + ("x",), perm)
+        landed += [sent[r] for r in range(nx)]
         first += w
-    out = jnp.zeros((occ_local, nx, width, occ, v), jnp.bfloat16)
-    for part, x_from, first in landed:
-        out = lax.dynamic_update_slice(out, part[:, None], (0, x_from, first, 0, 0))
+    out = unpack(landed, spread, x_from, shape)
     out = out.reshape(occ_local, nx * width, occ, v)
     return jnp.transpose(out, (0, 2, 3, 1))
 

time: 195 us -> 190 us (0.974)
  waiting for transfers between devices: 102 us -> 81 us
  starting transfers between devices: 47.4 us -> 64 us
  local copies, waits for them, and re-layouts: 12.7 us -> 10.7 us
    ppermute x9, waiting for transfers between devices: 22.4 us -> 6.15 us  [the longest x8 6.15 us: per_device(): sent[r] = lax.ppermute(parts[r], OCC + ('x',), perm)]
    ppermute x9, starting transfers between devices: 13.4 us -> 27.9 us  [the longest x8 27.8 us: per_device(): sent[r] = lax.ppermute(parts[r], OCC + ('x',), perm)]
    all_to_all x2, waiting for transfers between devices: 30.8 us -> 25.9 us  [per_device(): tiles = lax.all_to_all(mid, TILE, 0, 0, tiled=True)]
    all_to_all x2, starting transfers between devices: 11.5 us -> 13.7 us  [per_device(): tiles = lax.all_to_all(mid, TILE, 0, 0, tiled=True)]
    unnamed x15 -> x13, local copies, waits for them, and re-layouts: 5.59 us -> 4.04 us
    pallas_call x2 -> x3, Pallas kernels: 15.5 us -> 16.5 us  [the longest x2 12.4 us: ladder_rows(): pl.pallas_call(functools.partial(ladder_kernel, first), in_specs=[pl.Bloc...]
  transfers between devices with their start and end apart: 17 -> 17, of which waited for: 10 -> 8; matrix products, arithmetic and copies ran while one was open for 4% -> 4% of each run, Pallas kernels for 15% -> 14%
where the time goes in v3:
time: 190 us; the launch traced here: 189 us
  waiting for transfers between devices  81 us (43%)
  starting transfers between devices  64 us (34%)
  Pallas kernels  30.5 us (16%)
  local copies, waits for them, and re-layouts  10.7 us (6%)
  other arithmetic  2.19 us (1%)
    ppermute x1, waiting for transfers between devices, per_device(): other = lax.ppermute(half, ('yh', 'yl'), swap_y)  35.2 us
    ppermute x8, starting transfers between devices, per_device(): sent[r] = lax.ppermute(parts[r], OCC + ('x',), perm)  27.8 us
    all_to_all x2, waiting for transfers between devices, per_device(): tiles = lax.all_to_all(mid, TILE, 0, 0, tiled=True)  25.9 us
    all_to_all x2, starting transfers between devices, per_device(): tiles = lax.all_to_all(mid, TILE, 0, 0, tiled=True)  13.7 us
    pallas_call x2, Pallas kernels, ladder_rows(): pl.pallas_call(functools.partial(ladder_kernel, first), in_specs=[pl.Bloc...  12.4 us
    pallas_call x1, Pallas kernels, middle(): pl.pallas_call(functools.partial(middle_kernel, q_local, dests, widths),...  12.1 us
    all_to_all x1, starting transfers between devices, share(): lax.all_to_all(jnp.broadcast_to(x[None], (count,) + x.shape), axes, 0, 0,...  10.7 us
    all_to_all x1, waiting for transfers between devices, per_device(): half = lax.all_to_all(half, TILE[1:], 0, 0, tiled=True)  7.51 us
  transfers between devices with their start and end apart: 17, of which 8 were waited for; matrix products, arithmetic and copies ran while one was open for 4% of the time, Pallas kernels for 14%

profile of v3, /device:TPU:24, one launch (start us, length us, event | category | flops | bytes accessed | tf_op | source)
XLA Modules:
  0.0 188.9 jit_solution(10713635878982633248)
XLA Ops:
  0.0 0.9 copy.15
  0.9 0.1 broadcast_in_dim.35
  1.0 1.0 broadcast_in_dim.36
  2.1 10.7 %all-to-all-start.1 = ((bf16[128,20,128]{2,1,0:T(8,128)(2,1)}), bf16[128,20,128]{2,1,0:T(8,128)(2,1)}, u32[]{:S(2)}, u32[]{:S(2)}) async-start(bf16[128,20,128]{2,1,0:T(8,128)(2,1)} %broadcast_in_dim.36), calls=%async_computation.1 | async-start | bytes 1572864 | tf_op jit(solution)/shard_map/all_to_all | solution.py:46
  12.7 0.0 slice-start
  12.7 1.9 %slice-done = bf16[75,160,2]{2,1,0:T(8,128)(2,1)S(1)} async-done(((bf16[75,160,640]{2,1,0:T(8,128)(2,1)}), bf16[75,160,2]{2,1,0:T(8,128)(2,1)S(1)}, s32[]{:S(2)}) %slice-start) | async-done | bytes 48024 | tf_op jit(solution)/shard_map/slice | solution.py:275
  14.7 2.9 %copy.20 = bf16[75,160,2]{1,0,2:T(8,128)(2,1)S(1)} copy(bf16[75,160,2]{2,1,0:T(8,128)(2,1)S(1)} %slice-done) | data formatting | bytes 96000
  17.6 0.0 copy-start.4
  17.7 1.2 collective-permute-start.2
  18.9 2.1 %collective-permute-start.1 = (bf16[2,80,160]{2,1,0:T(8,128)(2,1)S(1)}, bf16[2,80,160]{2,1,0:T(8,128)(2,1)S(1)}, u32[]{:S(2)}, u32[]{:S(2)}) collective-permute-start(bf16[2,80,160]{2,1,0:T(8,128)(2,1)S(1)} %pad.10.refs_0_), channel_id=1, source_target_pairs={{0,64},{32,96},{64,0},{96,32},{1,65},{33,97},{65,1},{97,33},{2,66}... | collective-permute-start | bytes 153608 | tf_op jit(solution)/shard_map/ppermute | solution.py:280
  21.0 0.0 collective-permute-start
  21.0 0.1 pad_add_fusion.2.at_ref
  21.1 2.6 %collective-permute-done.2.refs_3_ = bf16[2,80,160]{2,1,0:T(8,128)(2,1)S(1)} collective-permute-done((bf16[2,80,160]{2,1,0:T(8,128)(2,1)S(1)}, bf16[2,80,160]{2,1,0:T(8,128)(2,1)S(1)}, u32[]{:S(2)}, u32[]{:S(2)}) %collective-permute-start.2) | collective-permute-done | bytes 51232 | tf_op jit(solution)/shard_map/ppermute | solution.py:280
  23.7 3.6 %collective-permute-done.1.refs_2_ = bf16[2,80,160]{2,1,0:T(8,128)(2,1)S(1)} collective-permute-done((bf16[2,80,160]{2,1,0:T(8,128)(2,1)S(1)}, bf16[2,80,160]{2,1,0:T(8,128)(2,1)S(1)}, u32[]{:S(2)}, u32[]{:S(2)}) %collective-permute-start.1) | collective-permute-done | bytes 51232 | tf_op jit(solution)/shard_map/ppermute | solution.py:280
  27.3 0.0 collective-permute-done.refs_1_
  27.3 1.9 %shard_map.64 = bf16[16,80,640]{2,1,0:T(8,128)(2,1)} custom-call(s32[2]{0:T(128)S(1)} %pad_add_fusion.2.at_ref, bf16[2,80,160]{2,1,0:T(8,128)(2,1)S(1)} %pad.10.refs_0_, bf16[2,80,160]{2,1,0:T(8,128)(2,1)S(1)} %collective-permute-done.refs_1_, bf16[2,80,160]{2,1,0:T(8,128)(2,1)S(1)} %collective-permute-done.1.refs_2_, ...), custom_call_target="tpu_custom_call" | custom-call | tf_op jit(solution)/shard_map/pallas_call | solution.py:123
  29.2 0.0 all-to-all-done.1
  29.2 6.4 %all-to-all-start = ((bf16[16,80,640]{2,1,0:T(8,128)(2,1)}), bf16[16,80,640]{2,1,0:T(8,128)(2,1)S(1)}, u32[]{:S(2)}, u32[]{:S(2)}) async-start(bf16[16,80,640]{2,1,0:T(8,128)(2,1)} %shard_map.64), calls=%async_computation | async-start | bytes 3276800 | tf_op jit(solution)/shard_map/all_to_all | solution.py:284
  35.6 0.0 copy-done.4
  35.7 0.1 select_reduce_fusion
  35.8 0.1 broadcast_bitcast_fusion
  35.8 1.3 reshape.65
  37.1 0.0 copy-done.5
  37.1 0.4 fusion.1.a_ref
  37.5 12.1 %shard_map.65 = (bf16[32,2,80,512]{3,2,1,0:T(8,128)(2,1)}, bf16[32,2,80,128]{3,2,1,0:T(8,128)(2,1)S(1)}) custom-call(bf16[75,160,640]{2,1,0:T(8,128)(2,1)} %b_ref.1, bf16[640,256]{1,0:T(8,128)(2,1)S(1)} %fusion.1.a_ref), custom_call_target="tpu_custom_call" | custom-call | flops 3932160000 | bytes 21913600 | tf_op jit(solution)/shard_map/pallas_call | solution.py:80
  49.6 1.1 copy-done
  50.6 7.5 %all-to-all-done = bf16[16,80,640]{2,1,0:T(8,128)(2,1)S(1)} async-done(((bf16[16,80,640]{2,1,0:T(8,128)(2,1)}), bf16[16,80,640]{2,1,0:T(8,128)(2,1)S(1)}, u32[]{:S(2)}, u32[]{:S(2)}) %all-to-all-start) | async-done | bytes 1638432 | tf_op jit(solution)/shard_map/all_to_all | solution.py:284
  58.2 5.2 %all-to-all-start.2 = ((bf16[32,160,512]{2,1,0:T(8,128)(2,1)}), bf16[32,160,512]{2,1,0:T(8,128)(2,1)}, u32[]{:S(2)}, u32[]{:S(2)}) async-start(bf16[32,160,512]{2,1,0:T(8,128)(2,1)} %bitcast.33), calls=%async_computation.2 | async-start | bytes 10485760 | tf_op jit(solution)/shard_map/all_to_all | solution.py:312
  63.4 1.2 copy.17
  64.6 0.0 copy-start.2
  64.6 2.0 %collective-permute-start.3 = (bf16[640,1280]{1,0:T(8,128)(2,1)S(1)}, bf16[640,1280]{1,0:T(8,128)(2,1)S(1)}, u32[]{:S(2)}, u32[]{:S(2)}) collective-permute-start(bf16[640,1280]{1,0:T(8,128)(2,1)S(1)} %bitcast.31), channel_id=1, source_target_pairs={{0,68},{68,0},{4,64},{64,4},{1,69},{69,1},{5,65},{65,5},{2,70},{70... | collective-permute-start | bytes 4915208 | tf_op jit(solution)/shard_map/ppermute | solution.py:290
  66.6 35.2 %collective-permute-done.3 = bf16[640,1280]{1,0:T(8,128)(2,1)S(1)} collective-permute-done((bf16[640,1280]{1,0:T(8,128)(2,1)S(1)}, bf16[640,1280]{1,0:T(8,128)(2,1)S(1)}, u32[]{:S(2)}, u32[]{:S(2)}) %collective-permute-start.3) | collective-permute-done | bytes 1638432 | tf_op jit(solution)/shard_map/ppermute | solution.py:290
  101.8 0.0 copy-done.2
  101.8 1.8 pad_maximum_fusion.own_ref
  103.6 0.1 collective-permute-start.4
  103.7 23.3 %all-to-all-done.2 = bf16[32,160,512]{2,1,0:T(8,128)(2,1)} async-done(((bf16[32,160,512]{2,1,0:T(8,128)(2,1)}), bf16[32,160,512]{2,1,0:T(8,128)(2,1)}, u32[]{:S(2)}, u32[]{:S(2)}) %all-to-all-start.2) | async-done | bytes 5242912 | tf_op jit(solution)/shard_map/all_to_all | solution.py:312
  126.9 8.5 %all-to-all-start.3 = ((bf16[32,160,128]{2,1,0:T(8,128)(2,1)}), bf16[32,160,128]{2,1,0:T(8,128)(2,1)}, u32[]{:S(2)}, u32[]{:S(2)}) async-start(bf16[32,160,128]{2,1,0:T(8,128)(2,1)} %bitcast.29), calls=%async_computation.3 | async-start | bytes 2621440 | tf_op jit(solution)/shard_map/all_to_all | solution.py:312
  135.4 0.1 dynamic_slice.6
  135.5 0.1 pad_add_fusion.1.at_ref
  135.6 0.1 broadcast_and_fusion
  135.7 0.0 copy-done.3
  135.7 0.0 collective-permute-done.4.far_hbm
  135.7 7.0 %shard_map.66 = (bf16[4,56,640]{2,1,0:T(8,128)(2,1)}, bf16[4,56,640]{2,1,0:T(8,128)(2,1)}, bf16[4,56,640]{2,1,0:T(8,128)(2,1)}, bf16[4,56,640]{2,1,0:T(8,128)(2,1)}) custom-call(s32[2]{0:T(128)S(1)} %pad_add_fusion.1.at_ref, bf16[2,640,1280]{2,1,0:T(8,128)(2,1)S(1)} %pad_maximum_fusion.own_ref, f32[8,640]{1,0:T(8,128)S(1)} %pad_convert_fusion.keep_ref, ...), custom_call_target="tpu_custom_call" | custom-call | flops 3355443200 | bytes 11796480 | tf_op jit(solution)/shard_map/pallas_call | solution.py:186
  142.7 6.1 %collective-permute-start.5 = (bf16[4,56,640]{2,1,0:T(8,128)(2,1)}, bf16[4,56,640]{2,1,0:T(8,128)(2,1)}, u32[]{:S(2)}, u32[]{:S(2)}) collective-permute-start(bf16[4,56,640]{2,1,0:T(8,128)(2,1)} %get-tuple-element.28), channel_id=1, source_target_pairs={{0,0},{8,32},{16,64},{24,96},{32,8},{40,40},{48,72},{56,104},{64,1... | collective-permute-start | bytes 860168 | tf_op jit(solution)/shard_map/ppermute | solution.py:329
  148.8 1.5 collective-permute-start.6
  150.4 0.0 collective-permute-start.7
  150.4 1.8 collective-permute-start.8
  152.1 2.6 %all-to-all-done.3 = bf16[32,160,128]{2,1,0:T(8,128)(2,1)} async-done(((bf16[32,160,128]{2,1,0:T(8,128)(2,1)}), bf16[32,160,128]{2,1,0:T(8,128)(2,1)}, u32[]{:S(2)}, u32[]{:S(2)}) %all-to-all-start.3) | async-done | bytes 1310752 | tf_op jit(solution)/shard_map/all_to_all | solution.py:312
  154.8 5.4 %shard_map.67 = (bf16[1,56,640]{2,1,0:T(8,128)(2,1)S(1)}, bf16[1,56,640]{2,1,0:T(8,128)(2,1)S(1)}, bf16[1,56,640]{2,1,0:T(8,128)(2,1)S(1)}, bf16[1,56,640]{2,1,0:T(8,128)(2,1)S(1)}) custom-call(s32[2]{0:T(128)S(1)} %pad_add_fusion.1.at_ref, bf16[2,640,1280]{2,1,0:T(8,128)(2,1)S(1)} %pad_maximum_fusion.own_ref, f32[8,640]{1,0:T(8,128)S(1)} %pad_convert_fusion.keep_ref, ...), custom_call_target="tpu_custom_call" | custom-call | flops 838860800 | bytes 7864320 | tf_op jit(solution)/shard_map/pallas_call | solution.py:186
  160.2 4.5 %collective-permute-start.9 = (bf16[1,56,640]{2,1,0:T(8,128)(2,1)S(1)}, bf16[1,56,640]{2,1,0:T(8,128)(2,1)S(1)}, u32[]{:S(2)}, u32[]{:S(2)}) collective-permute-start(bf16[1,56,640]{2,1,0:T(8,128)(2,1)S(1)} %get-tuple-element.35), channel_id=1, source_target_pairs={{0,0},{8,32},{16,64},{24,96},{32,8},{40,40},{48,72},{56,104},{64,1... | collective-permute-start | bytes 215048 | tf_op jit(solution)/shard_map/ppermute | solution.py:329
  164.7 0.0 collective-permute-done.5.refs_0_
  164.7 3.7 %collective-permute-start.10 = (bf16[1,56,640]{2,1,0:T(8,128)(2,1)S(1)}, bf16[1,56,640]{2,1,0:T(8,128)(2,1)S(1)}, u32[]{:S(2)}, u32[]{:S(2)}) collective-permute-start(bf16[1,56,640]{2,1,0:T(8,128)(2,1)S(1)} %get-tuple-element.36), channel_id=1, source_target_pairs={{0,32},{8,64},{16,96},{24,0},{32,40},{40,72},{48,104},{56,8},{64,4... | collective-permute-start | bytes 215048 | tf_op jit(solution)/shard_map/ppermute | solution.py:329
  168.4 0.0 collective-permute-done.6.refs_1_
  168.4 4.4 %collective-permute-start.11 = (bf16[1,56,640]{2,1,0:T(8,128)(2,1)S(1)}, bf16[1,56,640]{2,1,0:T(8,128)(2,1)S(1)}, u32[]{:S(2)}, u32[]{:S(2)}) collective-permute-start(bf16[1,56,640]{2,1,0:T(8,128)(2,1)S(1)} %get-tuple-element.37), channel_id=1, source_target_pairs={{0,64},{8,96},{16,0},{24,32},{32,72},{40,104},{48,8},{56,40},{64,8... | collective-permute-start | bytes 215048 | tf_op jit(solution)/shard_map/ppermute | solution.py:329
  172.8 0.0 collective-permute-done.7.refs_2_
  172.8 5.8 %collective-permute-start.12 = (bf16[1,56,640]{2,1,0:T(8,128)(2,1)S(1)}, bf16[1,56,640]{2,1,0:T(8,128)(2,1)S(1)}, u32[]{:S(2)}, u32[]{:S(2)}) collective-permute-start(bf16[1,56,640]{2,1,0:T(8,128)(2,1)S(1)} %get-tuple-element.38), channel_id=1, source_target_pairs={{0,96},{8,0},{16,32},{24,64},{32,104},{40,8},{48,40},{56,72},{64,1... | collective-permute-start | bytes 215048 | tf_op jit(solution)/shard_map/ppermute | solution.py:329
  178.6 0.1 pad_add_fusion.at_ref
  178.7 2.5 %collective-permute-done.8.refs_3_ = bf16[4,56,640]{2,1,0:T(8,128)(2,1)} collective-permute-done((bf16[4,56,640]{2,1,0:T(8,128)(2,1)}, bf16[4,56,640]{2,1,0:T(8,128)(2,1)}, u32[]{:S(2)}, u32[]{:S(2)}) %collective-permute-start.8) | collective-permute-done | bytes 286752 | tf_op jit(solution)/shard_map/ppermute | solution.py:329
  181.2 0.0 collective-permute-done.9.refs_4_
  181.2 0.0 collective-permute-done.10.refs_5_
  181.2 0.0 collective-permute-done.11.refs_6_
  181.2 3.7 %collective-permute-done.12.refs_7_ = bf16[1,56,640]{2,1,0:T(8,128)(2,1)S(1)} collective-permute-done((bf16[1,56,640]{2,1,0:T(8,128)(2,1)S(1)}, bf16[1,56,640]{2,1,0:T(8,128)(2,1)S(1)}, u32[]{:S(2)}, u32[]{:S(2)}) %collective-permute-start.12) | collective-permute-done | bytes 71712 | tf_op jit(solution)/shard_map/ppermute | solution.py:329
  184.8 0.0 copy-done.1
  184.8 4.1 %shard_map.68 = bf16[4,4,5,16,640]{4,3,2,1,0:T(8,128)(2,1)} custom-call(s32[5]{0:T(128)S(1)} %pad_add_fusion.at_ref, bf16[4,64,56]{2,1,0:T(8,128)(2,1)S(1)} %copy-done.1, bf16[4,56,640]{2,1,0:T(8,128)(2,1)} %collective-permute-done.5.refs_0_, bf16[4,56,640]{2,1,0:T(8,128)(2,1)} %collective-permute-done.6.refs_1_, ...), custom_call_target="tpu_custom_call" | custom-call | tf_op jit(solution)/shard_map/pallas_call | solution.py:231
  (11 shorter events, 0.1 us)
Async XLA Ops:
  2.1 27.2 %all-to-all-start.1 = ((bf16[128,20,128]{2,1,0:T(8,128)(2,1)}), bf16[128,20,128]{2,1,0:T(8,128)(2,1)}, u32[]{:S(2)}, u32[]{:S(2)}) async-start(bf16[128,20,128]{2,1,0:T(8,128)(2,1)} %broadcast_in_dim.36), calls=%async_computation.1 | async-start | bytes 1572864 | tf_op jit(solution)/shard_map/all_to_all | solution.py:46
  12.7 1.9 %slice-start = ((bf16[75,160,640]{2,1,0:T(8,128)(2,1)}), bf16[75,160,2]{2,1,0:T(8,128)(2,1)S(1)}, s32[]{:S(2)}) async-start(bf16[75,160,640]{2,1,0:T(8,128)(2,1)} %b_ref.1), calls=%async_computation.4 | async-start | bytes 6144000 | tf_op jit(solution)/shard_map/slice | solution.py:275
  17.6 18.0 %copy-start.4 = (s32[8]{0:T(128)S(1)}, s32[8]{0:T(128)}, u32[]{:S(2)}) copy-start(s32[8]{0:T(128)} %param.8) | copy-start | bytes 100
  17.7 6.0 %collective-permute-start.2 = (bf16[2,80,160]{2,1,0:T(8,128)(2,1)S(1)}, bf16[2,80,160]{2,1,0:T(8,128)(2,1)S(1)}, u32[]{:S(2)}, u32[]{:S(2)}) collective-permute-start(bf16[2,80,160]{2,1,0:T(8,128)(2,1)S(1)} %pad.10.refs_0_), channel_id=1, source_target_pairs={{0,96},{32,0},{64,32},{96,64},{1,97},{33,1},{65,33},{97,65},{2,98}... | collective-permute-start | bytes 153608 | tf_op jit(solution)/shard_map/ppermute | solution.py:280
  18.9 8.4 %collective-permute-start.1 = (bf16[2,80,160]{2,1,0:T(8,128)(2,1)S(1)}, bf16[2,80,160]{2,1,0:T(8,128)(2,1)S(1)}, u32[]{:S(2)}, u32[]{:S(2)}) collective-permute-start(bf16[2,80,160]{2,1,0:T(8,128)(2,1)S(1)} %pad.10.refs_0_), channel_id=1, source_target_pairs={{0,64},{32,96},{64,0},{96,32},{1,65},{33,97},{65,1},{97,33},{2,66}... | collective-permute-start | bytes 153608 | tf_op jit(solution)/shard_map/ppermute | solution.py:280
  21.0 6.3 %collective-permute-start = (bf16[2,80,160]{2,1,0:T(8,128)(2,1)S(1)}, bf16[2,80,160]{2,1,0:T(8,128)(2,1)S(1)}, u32[]{:S(2)}, u32[]{:S(2)}) collective-permute-start(bf16[2,80,160]{2,1,0:T(8,128)(2,1)S(1)} %pad.10.refs_0_), channel_id=1, source_target_pairs={{0,32},{32,64},{64,96},{96,0},{1,33},{33,65},{65,97},{97,1},{2,34}... | collective-permute-start | bytes 153608 | tf_op jit(solution)/shard_map/ppermute | solution.py:280
  21.1 16.0 %copy-start.5 = (bf16[4,128,256]{1,2,0:T(8,128)(2,1)S(1)}, bf16[4,128,256]{1,2,0:T(8,128)(2,1)}, u32[]{:S(2)}) copy-start(bf16[4,128,256]{1,2,0:T(8,128)(2,1)} %constant.83.clone) | copy-start | bytes 786436
  29.2 28.9 %all-to-all-start = ((bf16[16,80,640]{2,1,0:T(8,128)(2,1)}), bf16[16,80,640]{2,1,0:T(8,128)(2,1)S(1)}, u32[]{:S(2)}, u32[]{:S(2)}) async-start(bf16[16,80,640]{2,1,0:T(8,128)(2,1)} %shard_map.64), calls=%async_computation | async-start | bytes 3276800 | tf_op jit(solution)/shard_map/all_to_all | solution.py:284
  49.6 1.1 copy-start
  58.2 68.8 %all-to-all-start.2 = ((bf16[32,160,512]{2,1,0:T(8,128)(2,1)}), bf16[32,160,512]{2,1,0:T(8,128)(2,1)}, u32[]{:S(2)}, u32[]{:S(2)}) async-start(bf16[32,160,512]{2,1,0:T(8,128)(2,1)} %bitcast.33), calls=%async_computation.2 | async-start | bytes 10485760 | tf_op jit(solution)/shard_map/all_to_all | solution.py:312
  64.6 37.2 %copy-start.2 = (bf16[1280,640]{0,1:T(8,128)(2,1)}, bf16[1280,640]{0,1:T(8,128)(2,1)S(1)}, u32[]{:S(2)}) copy-start(bf16[1280,640]{0,1:T(8,128)(2,1)S(1)} %copy.17) | copy-start | bytes 4915204
  64.6 37.1 %collective-permute-start.3 = (bf16[640,1280]{1,0:T(8,128)(2,1)S(1)}, bf16[640,1280]{1,0:T(8,128)(2,1)S(1)}, u32[]{:S(2)}, u32[]{:S(2)}) collective-permute-start(bf16[640,1280]{1,0:T(8,128)(2,1)S(1)} %bitcast.31), channel_id=1, source_target_pairs={{0,68},{68,0},{4,64},{64,4},{1,69},{69,1},{5,65},{65,5},{2,70},{70... | collective-permute-start | bytes 4915208 | tf_op jit(solution)/shard_map/ppermute | solution.py:290
  101.8 33.9 %copy-start.3 = (bf16[448,128]{1,0:T(8,128)(2,1)S(1)}, bf16[448,128]{1,0:T(8,128)(2,1)}, u32[]{:S(2)}) copy-start(bf16[448,128]{1,0:T(8,128)(2,1)} %constant.84.clone) | copy-start | bytes 344068
  103.6 32.1 %collective-permute-start.4 = (bf16[2,640,1280]{2,1,0:T(8,128)(2,1)S(1)}, bf16[2,640,1280]{2,1,0:T(8,128)(2,1)}, u32[]{:S(2)}, u32[]{:S(2)}) collective-permute-start(bf16[2,640,1280]{2,1,0:T(8,128)(2,1)S(1)} %pad_maximum_fusion.own_ref), channel_id=1, source_target_pairs={{0,32},{32,0},{1,33},{33,1},{2,34},{34,2},{3,35},{35,3},{4,36},{36... | collective-permute-start | bytes 9830408 | tf_op jit(solution)/shard_map/ppermute | solution.py:292
  126.9 27.8 %all-to-all-start.3 = ((bf16[32,160,128]{2,1,0:T(8,128)(2,1)}), bf16[32,160,128]{2,1,0:T(8,128)(2,1)}, u32[]{:S(2)}, u32[]{:S(2)}) async-start(bf16[32,160,128]{2,1,0:T(8,128)(2,1)} %bitcast.29), calls=%async_computation.3 | async-start | bytes 2621440 | tf_op jit(solution)/shard_map/all_to_all | solution.py:312
  142.7 22.0 %collective-permute-start.5 = (bf16[4,56,640]{2,1,0:T(8,128)(2,1)}, bf16[4,56,640]{2,1,0:T(8,128)(2,1)}, u32[]{:S(2)}, u32[]{:S(2)}) collective-permute-start(bf16[4,56,640]{2,1,0:T(8,128)(2,1)} %get-tuple-element.28), channel_id=1, source_target_pairs={{0,0},{8,32},{16,64},{24,96},{32,8},{40,40},{48,72},{56,104},{64,1... | collective-permute-start | bytes 860168 | tf_op jit(solution)/shard_map/ppermute | solution.py:329
  148.8 19.5 %collective-permute-start.6 = (bf16[4,56,640]{2,1,0:T(8,128)(2,1)}, bf16[4,56,640]{2,1,0:T(8,128)(2,1)}, u32[]{:S(2)}, u32[]{:S(2)}) collective-permute-start(bf16[4,56,640]{2,1,0:T(8,128)(2,1)} %get-tuple-element.29), channel_id=1, source_target_pairs={{0,32},{8,64},{16,96},{24,0},{32,40},{40,72},{48,104},{56,8},{64,4... | collective-permute-start | bytes 860168 | tf_op jit(solution)/shard_map/ppermute | solution.py:329
  150.4 22.4 %collective-permute-start.7 = (bf16[4,56,640]{2,1,0:T(8,128)(2,1)}, bf16[4,56,640]{2,1,0:T(8,128)(2,1)}, u32[]{:S(2)}, u32[]{:S(2)}) collective-permute-start(bf16[4,56,640]{2,1,0:T(8,128)(2,1)} %get-tuple-element.30), channel_id=1, source_target_pairs={{0,64},{8,96},{16,0},{24,32},{32,72},{40,104},{48,8},{56,40},{64,8... | collective-permute-start | bytes 860168 | tf_op jit(solution)/shard_map/ppermute | solution.py:329
  150.4 30.8 %collective-permute-start.8 = (bf16[4,56,640]{2,1,0:T(8,128)(2,1)}, bf16[4,56,640]{2,1,0:T(8,128)(2,1)}, u32[]{:S(2)}, u32[]{:S(2)}) collective-permute-start(bf16[4,56,640]{2,1,0:T(8,128)(2,1)} %get-tuple-element.31), channel_id=1, source_target_pairs={{0,96},{8,0},{16,32},{24,64},{32,104},{40,8},{48,40},{56,72},{64,1... | collective-permute-start | bytes 860168 | tf_op jit(solution)/shard_map/ppermute | solution.py:329
  154.8 30.1 %copy-start.1 = (bf16[4,64,56]{2,1,0:T(8,128)(2,1)S(1)}, bf16[4,64,56]{2,1,0:T(8,128)(2,1)}, u32[]{:S(2)}) copy-start(bf16[4,64,56]{2,1,0:T(8,128)(2,1)} %constant.85.clone.spread_ref) | copy-start | bytes 86020
  160.2 21.0 %collective-permute-start.9 = (bf16[1,56,640]{2,1,0:T(8,128)(2,1)S(1)}, bf16[1,56,640]{2,1,0:T(8,128)(2,1)S(1)}, u32[]{:S(2)}, u32[]{:S(2)}) collective-permute-start(bf16[1,56,640]{2,1,0:T(8,128)(2,1)S(1)} %get-tuple-element.35), channel_id=1, source_target_pairs={{0,0},{8,32},{16,64},{24,96},{32,8},{40,40},{48,72},{56,104},{64,1... | collective-permute-start | bytes 215048 | tf_op jit(solution)/shard_map/ppermute | solution.py:329
  164.7 16.5 %collective-permute-start.10 = (bf16[1,56,640]{2,1,0:T(8,128)(2,1)S(1)}, bf16[1,56,640]{2,1,0:T(8,128)(2,1)S(1)}, u32[]{:S(2)}, u32[]{:S(2)}) collective-permute-start(bf16[1,56,640]{2,1,0:T(8,128)(2,1)S(1)} %get-tuple-element.36), channel_id=1, source_target_pairs={{0,32},{8,64},{16,96},{24,0},{32,40},{40,72},{48,104},{56,8},{64,4... | collective-permute-start | bytes 215048 | tf_op jit(solution)/shard_map/ppermute | solution.py:329
  168.4 12.8 %collective-permute-start.11 = (bf16[1,56,640]{2,1,0:T(8,128)(2,1)S(1)}, bf16[1,56,640]{2,1,0:T(8,128)(2,1)S(1)}, u32[]{:S(2)}, u32[]{:S(2)}) collective-permute-start(bf16[1,56,640]{2,1,0:T(8,128)(2,1)S(1)} %get-tuple-element.37), channel_id=1, source_target_pairs={{0,64},{8,96},{16,0},{24,32},{32,72},{40,104},{48,8},{56,40},{64,8... | collective-permute-start | bytes 215048 | tf_op jit(solution)/shard_map/ppermute | solution.py:329
  172.8 12.0 %collective-permute-start.12 = (bf16[1,56,640]{2,1,0:T(8,128)(2,1)S(1)}, bf16[1,56,640]{2,1,0:T(8,128)(2,1)S(1)}, u32[]{:S(2)}, u32[]{:S(2)}) collective-permute-start(bf16[1,56,640]{2,1,0:T(8,128)(2,1)S(1)} %get-tuple-element.38), channel_id=1, source_target_pairs={{0,96},{8,0},{16,32},{24,64},{32,104},{40,8},{48,40},{56,72},{64,1... | collective-permute-start | bytes 215048 | tf_op jit(solution)/shard_map/ppermute | solution.py:329

commit v4 on v3

--- a/solution.py
+++ b/solution.py
@@ -203,44 +203,43 @@
     )(at, own, keep, select, tiles, far)
 
 
-def unpack_kernel(widths, at_ref, spread_ref, *refs):
-    parts, out_ref = refs[:-1], refs[-1]
+def unpack_kernel(at_ref, spread_ref, *refs):
+    out_ref = refs[-1]
     r = pl.program_id(0)
-    occ_local, _, _, occ, a_size = out_ref.shape
-    count = len(parts) // len(widths)
-
-    def source(n):
-        first = 0
-        for k, width in enumerate(widths):
-            for h in range(width):
-                rows = jnp.dot(
-                    spread_ref[at_ref[count]],
-                    parts[k * count + n][h],
-                    preferred_element_type=jnp.float32,
-                ).astype(jnp.bfloat16)
-                out_ref[:, 0, first + h] = rows.reshape(occ_local, occ, a_size)
-            first += width
-
-    for n in range(count):
-        pl.when(r == n)(functools.partial(source, n))
-
-
-def unpack(parts, spread, x_from, shape):
-    occ_local, count, width, occ, a_size = shape
+    occ_local, _, width, occ, a_size = out_ref.shape
+    spread = spread_ref[at_ref[pl.num_programs(0)]]
+
+    def source(part_ref):
+        for h in range(width):
+            rows = jnp.dot(spread, part_ref[h], preferred_element_type=jnp.float32)
+            rows = rows.astype(jnp.bfloat16)
+            out_ref[:, 0, h] = rows.reshape(occ_local, occ, a_size)
+
+    for n in range(4):
+        pl.when(r == n)(functools.partial(source, refs[n]))
+
+
+def unpack(parts, spread, x_from, first, out, shape):
+    occ_local, count, _, occ, a_size = shape
+    width = parts[0].shape[0]
     vmem = pl.BlockSpec(memory_space=pltpu.VMEM)
+    so_far = [] if out is None else [out]
     return pl.pallas_call(
-        functools.partial(unpack_kernel, WIDTHS),
+        unpack_kernel,
         grid_spec=pltpu.PrefetchScalarGridSpec(
             num_scalar_prefetch=1,
             grid=(count,),
-            in_specs=[vmem] * (1 + len(parts)),
+            in_specs=[vmem] * (1 + count)
+            + [pl.BlockSpec(memory_space=pl.ANY)] * len(so_far),
             out_specs=pl.BlockSpec(
-                (occ_local, 1, width, occ, a_size), lambda r, at: (0, at[r], 0, 0, 0)
+                (occ_local, 1, width, occ, a_size),
+                lambda r, at: (0, at[r], first // width, 0, 0),
             ),
         ),
         out_shape=jax.ShapeDtypeStruct(shape, jnp.bfloat16),
+        input_output_aliases={2 + count: 0} if so_far else {},
         compiler_params=pltpu.CompilerParams(vmem_limit_bytes=16 << 20),
-    )(x_from, spread, *parts)
+    )(x_from, spread, *parts, *so_far)
 
 
 def per_device(factors, amplitudes, block_sizes):
@@ -304,7 +303,7 @@
     shape = (occ_local, nx, width, occ, v)
     x_from = (occ_at - jnp.arange(nx, dtype=jnp.int32) + nx) % nx
     x_from = jnp.append(x_from, occ_at.astype(jnp.int32))
-    first, tiles, parts, landed = 0, None, None, []
+    first, tiles, parts, landed, out = 0, None, None, [], None
     for mid, w in zip(mids, WIDTHS):
         mid = mid.reshape(shards, cwin * QPAD, w * NPAIR)
         if tiles is not None:
@@ -319,17 +318,17 @@
         )
         if landed:
             landed, _ = lax.optimization_barrier((landed, parts))
-        sent = {}
+            out = unpack(landed, spread, x_from, 0, out, shape)
+        landed = []
         for r in range(nx):
             perm = [
                 (o * nx + x, ((x + r) % nx) * nx + o)
                 for o in range(occ_shards)
                 for x in range(nx)
             ]
-            sent[r] = lax.ppermute(parts[r], OCC + ("x",), perm)
-        landed += [sent[r] for r in range(nx)]
+            landed.append(lax.ppermute(parts[r], OCC + ("x",), perm))
         first += w
-    out = unpack(landed, spread, x_from, shape)
+    out = unpack(landed, spread, x_from, first - w, out, shape)
     out = out.reshape(occ_local, nx * width, occ, v)
     return jnp.transpose(out, (0, 2, 3, 1))
 

time: 190 us -> 188 us (0.989)
  waiting for transfers between devices: 81 us -> 77.4 us
  Pallas kernels: 30.5 us -> 32.7 us
    ppermute x8, waiting for transfers between devices: 6.15 us -> 2.48 us  [per_device(): landed.append(lax.ppermute(parts[r], OCC + ('x',), perm))]
    pallas_call x1 -> x2, Pallas kernels: 4.1 us -> 6.29 us  [unpack(): pl.pallas_call(unpack_kernel, grid_spec=pltpu.PrefetchScalarGridSpec(num_...]
  transfers between devices with their start and end apart: 17 -> 17, of which waited for: 8 -> 7; matrix products, arithmetic and copies ran while one was open for 4% -> 4% of each run, Pallas kernels for 14% -> 16%
where the time goes in v4:
time: 188 us
  waiting for transfers between devices  77.4 us (41%)
  starting transfers between devices  64.1 us (34%)
  Pallas kernels  32.7 us (17%)
  local copies, waits for them, and re-layouts  10.7 us (6%)
  other arithmetic  2.15 us (1%)
    ppermute x1, waiting for transfers between devices, per_device(): other = lax.ppermute(half, ('yh', 'yl'), swap_y)  35.2 us
    ppermute x8, starting transfers between devices, per_device(): landed.append(lax.ppermute(parts[r], OCC + ('x',), perm))  27.9 us
    all_to_all x2, waiting for transfers between devices, per_device(): tiles = lax.all_to_all(mid, TILE, 0, 0, tiled=True)  25.9 us
    all_to_all x2, starting transfers between devices, per_device(): tiles = lax.all_to_all(mid, TILE, 0, 0, tiled=True)  13.6 us
    pallas_call x2, Pallas kernels, ladder_rows(): pl.pallas_call(functools.partial(ladder_kernel, first), in_specs=[pl.Bloc...  12.4 us
    pallas_call x1, Pallas kernels, middle(): pl.pallas_call(functools.partial(middle_kernel, q_local, dests, widths),...  12.1 us
    all_to_all x1, starting transfers between devices, share(): lax.all_to_all(jnp.broadcast_to(x[None], (count,) + x.shape), axes, 0, 0,...  10.7 us
    all_to_all x1, waiting for transfers between devices, per_device(): half = lax.all_to_all(half, TILE[1:], 0, 0, tiled=True)  7.52 us
  transfers between devices with their start and end apart: 17, of which 7 were waited for; matrix products, arithmetic and copies ran while one was open for 4% of the time, Pallas kernels for 16%

profile of v4, /device:TPU:24, one launch (start us, length us, event | category | flops | bytes accessed | tf_op | source)
XLA Modules:
  0.0 187.6 jit_solution(17474543748982499120)
XLA Ops:
  0.0 0.9 copy.16
  0.9 0.1 broadcast_in_dim.35
  1.0 1.0 broadcast_in_dim.36
  2.1 10.7 %all-to-all-start.1 = ((bf16[128,20,128]{2,1,0:T(8,128)(2,1)}), bf16[128,20,128]{2,1,0:T(8,128)(2,1)}, u32[]{:S(2)}, u32[]{:S(2)}) async-start(bf16[128,20,128]{2,1,0:T(8,128)(2,1)} %broadcast_in_dim.36), calls=%async_computation.1 | async-start | bytes 1572864 | tf_op jit(solution)/shard_map/all_to_all | solution.py:46
  12.7 0.0 slice-start
  12.7 1.9 %slice-done = bf16[75,160,2]{2,1,0:T(8,128)(2,1)S(1)} async-done(((bf16[75,160,640]{2,1,0:T(8,128)(2,1)}), bf16[75,160,2]{2,1,0:T(8,128)(2,1)S(1)}, s32[]{:S(2)}) %slice-start) | async-done | bytes 48024 | tf_op jit(solution)/shard_map/slice | solution.py:274
  14.7 2.9 %copy.21 = bf16[75,160,2]{1,0,2:T(8,128)(2,1)S(1)} copy(bf16[75,160,2]{2,1,0:T(8,128)(2,1)S(1)} %slice-done) | data formatting | bytes 96000
  17.6 1.2 collective-permute-start.2
  18.9 2.1 %collective-permute-start.1 = (bf16[2,80,160]{2,1,0:T(8,128)(2,1)S(1)}, bf16[2,80,160]{2,1,0:T(8,128)(2,1)S(1)}, u32[]{:S(2)}, u32[]{:S(2)}) collective-permute-start(bf16[2,80,160]{2,1,0:T(8,128)(2,1)S(1)} %pad.10.refs_0_), channel_id=1, source_target_pairs={{0,64},{32,96},{64,0},{96,32},{1,65},{33,97},{65,1},{97,33},{2,66}... | collective-permute-start | bytes 153608 | tf_op jit(solution)/shard_map/ppermute | solution.py:279
  21.0 0.0 collective-permute-start
  21.0 0.1 pad_add_fusion.2.at_ref
  21.1 2.6 %collective-permute-done.2.refs_3_ = bf16[2,80,160]{2,1,0:T(8,128)(2,1)S(1)} collective-permute-done((bf16[2,80,160]{2,1,0:T(8,128)(2,1)S(1)}, bf16[2,80,160]{2,1,0:T(8,128)(2,1)S(1)}, u32[]{:S(2)}, u32[]{:S(2)}) %collective-permute-start.2) | collective-permute-done | bytes 51232 | tf_op jit(solution)/shard_map/ppermute | solution.py:279
  23.7 3.6 %collective-permute-done.1.refs_2_ = bf16[2,80,160]{2,1,0:T(8,128)(2,1)S(1)} collective-permute-done((bf16[2,80,160]{2,1,0:T(8,128)(2,1)S(1)}, bf16[2,80,160]{2,1,0:T(8,128)(2,1)S(1)}, u32[]{:S(2)}, u32[]{:S(2)}) %collective-permute-start.1) | collective-permute-done | bytes 51232 | tf_op jit(solution)/shard_map/ppermute | solution.py:279
  27.3 0.0 collective-permute-done.refs_1_
  27.3 1.9 %shard_map.64 = bf16[16,80,640]{2,1,0:T(8,128)(2,1)} custom-call(s32[2]{0:T(128)S(1)} %pad_add_fusion.2.at_ref, bf16[2,80,160]{2,1,0:T(8,128)(2,1)S(1)} %pad.10.refs_0_, bf16[2,80,160]{2,1,0:T(8,128)(2,1)S(1)} %collective-permute-done.refs_1_, bf16[2,80,160]{2,1,0:T(8,128)(2,1)S(1)} %collective-permute-done.1.refs_2_, ...), custom_call_target="tpu_custom_call" | custom-call | tf_op jit(solution)/shard_map/pallas_call | solution.py:123
  29.2 0.0 all-to-all-done.1
  29.2 6.5 %all-to-all-start = ((bf16[16,80,640]{2,1,0:T(8,128)(2,1)}), bf16[16,80,640]{2,1,0:T(8,128)(2,1)S(1)}, u32[]{:S(2)}, u32[]{:S(2)}) async-start(bf16[16,80,640]{2,1,0:T(8,128)(2,1)} %shard_map.64), calls=%async_computation | async-start | bytes 3276800 | tf_op jit(solution)/shard_map/all_to_all | solution.py:283
  35.8 0.0 copy-done.4
  35.8 0.1 select_reduce_fusion
  35.9 0.1 broadcast_bitcast_fusion
  36.0 1.3 reshape.65
  37.2 0.0 copy-done.5
  37.2 0.4 fusion.1.a_ref
  37.6 12.1 %shard_map.65 = (bf16[32,2,80,512]{3,2,1,0:T(8,128)(2,1)}, bf16[32,2,80,128]{3,2,1,0:T(8,128)(2,1)S(1)}) custom-call(bf16[75,160,640]{2,1,0:T(8,128)(2,1)} %b_ref.1, bf16[640,256]{1,0:T(8,128)(2,1)S(1)} %fusion.1.a_ref), custom_call_target="tpu_custom_call" | custom-call | flops 3932160000 | bytes 21913600 | tf_op jit(solution)/shard_map/pallas_call | solution.py:80
  49.7 1.1 copy-done
  50.8 7.5 %all-to-all-done = bf16[16,80,640]{2,1,0:T(8,128)(2,1)S(1)} async-done(((bf16[16,80,640]{2,1,0:T(8,128)(2,1)}), bf16[16,80,640]{2,1,0:T(8,128)(2,1)S(1)}, u32[]{:S(2)}, u32[]{:S(2)}) %all-to-all-start) | async-done | bytes 1638432 | tf_op jit(solution)/shard_map/all_to_all | solution.py:283
  58.3 5.2 %all-to-all-start.2 = ((bf16[32,160,512]{2,1,0:T(8,128)(2,1)}), bf16[32,160,512]{2,1,0:T(8,128)(2,1)}, u32[]{:S(2)}, u32[]{:S(2)}) async-start(bf16[32,160,512]{2,1,0:T(8,128)(2,1)} %bitcast.33), calls=%async_computation.2 | async-start | bytes 10485760 | tf_op jit(solution)/shard_map/all_to_all | solution.py:311
  63.5 1.2 copy.18
  64.8 0.0 copy-start.2
  64.8 2.0 %collective-permute-start.3 = (bf16[640,1280]{1,0:T(8,128)(2,1)S(1)}, bf16[640,1280]{1,0:T(8,128)(2,1)S(1)}, u32[]{:S(2)}, u32[]{:S(2)}) collective-permute-start(bf16[640,1280]{1,0:T(8,128)(2,1)S(1)} %bitcast.31), channel_id=1, source_target_pairs={{0,68},{68,0},{4,64},{64,4},{1,69},{69,1},{5,65},{65,5},{2,70},{70... | collective-permute-start | bytes 4915208 | tf_op jit(solution)/shard_map/ppermute | solution.py:289
  66.7 35.2 %collective-permute-done.3 = bf16[640,1280]{1,0:T(8,128)(2,1)S(1)} collective-permute-done((bf16[640,1280]{1,0:T(8,128)(2,1)S(1)}, bf16[640,1280]{1,0:T(8,128)(2,1)S(1)}, u32[]{:S(2)}, u32[]{:S(2)}) %collective-permute-start.3) | collective-permute-done | bytes 1638432 | tf_op jit(solution)/shard_map/ppermute | solution.py:289
  101.9 0.0 copy-done.2
  101.9 1.7 pad_maximum_fusion.own_ref
  103.7 0.0 copy-start.3
  103.7 0.1 collective-permute-start.4
  103.8 23.3 %all-to-all-done.2 = bf16[32,160,512]{2,1,0:T(8,128)(2,1)} async-done(((bf16[32,160,512]{2,1,0:T(8,128)(2,1)}), bf16[32,160,512]{2,1,0:T(8,128)(2,1)}, u32[]{:S(2)}, u32[]{:S(2)}) %all-to-all-start.2) | async-done | bytes 5242912 | tf_op jit(solution)/shard_map/all_to_all | solution.py:311
  127.1 8.4 %all-to-all-start.3 = ((bf16[32,160,128]{2,1,0:T(8,128)(2,1)}), bf16[32,160,128]{2,1,0:T(8,128)(2,1)}, u32[]{:S(2)}, u32[]{:S(2)}) async-start(bf16[32,160,128]{2,1,0:T(8,128)(2,1)} %bitcast.29), calls=%async_computation.3 | async-start | bytes 2621440 | tf_op jit(solution)/shard_map/all_to_all | solution.py:311
  135.5 0.1 dynamic_slice.6
  135.6 0.1 pad_add_fusion.1.at_ref
  135.7 0.1 broadcast_and_fusion
  135.7 0.0 copy-done.3
  135.8 0.0 collective-permute-done.4.far_hbm
  135.8 7.0 %shard_map.66 = (bf16[4,56,640]{2,1,0:T(8,128)(2,1)}, bf16[4,56,640]{2,1,0:T(8,128)(2,1)}, bf16[4,56,640]{2,1,0:T(8,128)(2,1)}, bf16[4,56,640]{2,1,0:T(8,128)(2,1)}) custom-call(s32[2]{0:T(128)S(1)} %pad_add_fusion.1.at_ref, bf16[2,640,1280]{2,1,0:T(8,128)(2,1)S(1)} %pad_maximum_fusion.own_ref, f32[8,640]{1,0:T(8,128)S(1)} %pad_convert_fusion.keep_ref, ...), custom_call_target="tpu_custom_call" | custom-call | flops 3355443200 | bytes 11796480 | tf_op jit(solution)/shard_map/pallas_call | solution.py:186
  142.8 6.2 %collective-permute-start.9 = (bf16[4,56,640]{2,1,0:T(8,128)(2,1)}, bf16[4,56,640]{2,1,0:T(8,128)(2,1)}, u32[]{:S(2)}, u32[]{:S(2)}) collective-permute-start(bf16[4,56,640]{2,1,0:T(8,128)(2,1)} %get-tuple-element.30), channel_id=1, source_target_pairs={{0,0},{8,32},{16,64},{24,96},{32,8},{40,40},{48,72},{56,104},{64,1... | collective-permute-start | bytes 860168 | tf_op jit(solution)/shard_map/ppermute | solution.py:329
  149.0 1.5 collective-permute-start.10
  150.4 0.0 collective-permute-start.11
  150.5 1.8 collective-permute-start.12
  152.3 2.6 %all-to-all-done.3 = bf16[32,160,128]{2,1,0:T(8,128)(2,1)} async-done(((bf16[32,160,128]{2,1,0:T(8,128)(2,1)}), bf16[32,160,128]{2,1,0:T(8,128)(2,1)}, u32[]{:S(2)}, u32[]{:S(2)}) %all-to-all-start.3) | async-done | bytes 1310752 | tf_op jit(solution)/shard_map/all_to_all | solution.py:311
  154.9 5.4 %shard_map.67 = (bf16[1,56,640]{2,1,0:T(8,128)(2,1)S(1)}, bf16[1,56,640]{2,1,0:T(8,128)(2,1)S(1)}, bf16[1,56,640]{2,1,0:T(8,128)(2,1)S(1)}, bf16[1,56,640]{2,1,0:T(8,128)(2,1)S(1)}) custom-call(s32[2]{0:T(128)S(1)} %pad_add_fusion.1.at_ref, bf16[2,640,1280]{2,1,0:T(8,128)(2,1)S(1)} %pad_maximum_fusion.own_ref, f32[8,640]{1,0:T(8,128)S(1)} %pad_convert_fusion.keep_ref, ...), custom_call_target="tpu_custom_call" | custom-call | flops 838860800 | bytes 7864320 | tf_op jit(solution)/shard_map/pallas_call | solution.py:186
  160.3 4.5 %collective-permute-start.5 = (bf16[1,56,640]{2,1,0:T(8,128)(2,1)S(1)}, bf16[1,56,640]{2,1,0:T(8,128)(2,1)S(1)}, u32[]{:S(2)}, u32[]{:S(2)}) collective-permute-start(bf16[1,56,640]{2,1,0:T(8,128)(2,1)S(1)} %get-tuple-element.35), channel_id=1, source_target_pairs={{0,0},{8,32},{16,64},{24,96},{32,8},{40,40},{48,72},{56,104},{64,1... | collective-permute-start | bytes 215048 | tf_op jit(solution)/shard_map/ppermute | solution.py:329
  164.8 0.0 collective-permute-done.9.refs_0_
  164.8 3.7 %collective-permute-start.6 = (bf16[1,56,640]{2,1,0:T(8,128)(2,1)S(1)}, bf16[1,56,640]{2,1,0:T(8,128)(2,1)S(1)}, u32[]{:S(2)}, u32[]{:S(2)}) collective-permute-start(bf16[1,56,640]{2,1,0:T(8,128)(2,1)S(1)} %get-tuple-element.36), channel_id=1, source_target_pairs={{0,32},{8,64},{16,96},{24,0},{32,40},{40,72},{48,104},{56,8},{64,4... | collective-permute-start | bytes 215048 | tf_op jit(solution)/shard_map/ppermute | solution.py:329
  168.5 0.0 collective-permute-done.10.refs_1_
  168.5 4.4 %collective-permute-start.7 = (bf16[1,56,640]{2,1,0:T(8,128)(2,1)S(1)}, bf16[1,56,640]{2,1,0:T(8,128)(2,1)S(1)}, u32[]{:S(2)}, u32[]{:S(2)}) collective-permute-start(bf16[1,56,640]{2,1,0:T(8,128)(2,1)S(1)} %get-tuple-element.37), channel_id=1, source_target_pairs={{0,64},{8,96},{16,0},{24,32},{32,72},{40,104},{48,8},{56,40},{64,8... | collective-permute-start | bytes 215048 | tf_op jit(solution)/shard_map/ppermute | solution.py:329
  172.9 0.0 collective-permute-done.11.refs_2_
  172.9 5.8 %collective-permute-start.8 = (bf16[1,56,640]{2,1,0:T(8,128)(2,1)S(1)}, bf16[1,56,640]{2,1,0:T(8,128)(2,1)S(1)}, u32[]{:S(2)}, u32[]{:S(2)}) collective-permute-start(bf16[1,56,640]{2,1,0:T(8,128)(2,1)S(1)} %get-tuple-element.38), channel_id=1, source_target_pairs={{0,96},{8,0},{16,32},{24,64},{32,104},{40,8},{48,40},{56,72},{64,1... | collective-permute-start | bytes 215048 | tf_op jit(solution)/shard_map/ppermute | solution.py:329
  178.8 0.1 pad_add_fusion.at_ref
  178.8 2.5 %collective-permute-done.12.refs_3_ = bf16[4,56,640]{2,1,0:T(8,128)(2,1)} collective-permute-done((bf16[4,56,640]{2,1,0:T(8,128)(2,1)}, bf16[4,56,640]{2,1,0:T(8,128)(2,1)}, u32[]{:S(2)}, u32[]{:S(2)}) %collective-permute-start.12) | collective-permute-done | bytes 286752 | tf_op jit(solution)/shard_map/ppermute | solution.py:329
  181.3 4.0 %shard_map.68.refs_4_ = bf16[4,4,5,16,640]{4,3,2,1,0:T(8,128)(2,1)} custom-call(s32[5]{0:T(128)S(1)} %pad_add_fusion.at_ref, bf16[4,64,56]{2,1,0:T(8,128)(2,1)S(1)} %copy-done.1, bf16[4,56,640]{2,1,0:T(8,128)(2,1)} %collective-permute-done.9.refs_0_, bf16[4,56,640]{2,1,0:T(8,128)(2,1)} %collective-permute-done.10.refs_1_, ...), custom_call_target="tpu_custom_call" | custom-call | tf_op jit(solution)/shard_map/pallas_call | solution.py:227
  185.3 0.0 collective-permute-done.5.refs_0_
  185.3 0.0 collective-permute-done.6.refs_1_
  185.3 0.0 collective-permute-done.7.refs_2_
  185.3 0.0 collective-permute-done.8.refs_3_
  185.3 2.3 %shard_map.69 = bf16[4,4,5,16,640]{4,3,2,1,0:T(8,128)(2,1)} custom-call(s32[5]{0:T(128)S(1)} %pad_add_fusion.at_ref, bf16[4,64,56]{2,1,0:T(8,128)(2,1)S(1)} %copy-done.1, bf16[1,56,640]{2,1,0:T(8,128)(2,1)S(1)} %collective-permute-done.5.refs_0_, bf16[1,56,640]{2,1,0:T(8,128)(2,1)S(1)} %collective-permute-done.6.refs_1_, ...), custom_call_target="tpu_custom_call", output_to_operand_aliasing={{}: (6, {})} | custom-call | tf_op jit(solution)/shard_map/pallas_call | solution.py:227
  (12 shorter events, 0.1 us)
Async XLA Ops:
  2.1 27.2 %all-to-all-start.1 = ((bf16[128,20,128]{2,1,0:T(8,128)(2,1)}), bf16[128,20,128]{2,1,0:T(8,128)(2,1)}, u32[]{:S(2)}, u32[]{:S(2)}) async-start(bf16[128,20,128]{2,1,0:T(8,128)(2,1)} %broadcast_in_dim.36), calls=%async_computation.1 | async-start | bytes 1572864 | tf_op jit(solution)/shard_map/all_to_all | solution.py:46
  12.7 1.9 %slice-start = ((bf16[75,160,640]{2,1,0:T(8,128)(2,1)}), bf16[75,160,2]{2,1,0:T(8,128)(2,1)S(1)}, s32[]{:S(2)}) async-start(bf16[75,160,640]{2,1,0:T(8,128)(2,1)} %b_ref.1), calls=%async_computation.4 | async-start | bytes 6144000 | tf_op jit(solution)/shard_map/slice | solution.py:274
  17.6 6.0 %collective-permute-start.2 = (bf16[2,80,160]{2,1,0:T(8,128)(2,1)S(1)}, bf16[2,80,160]{2,1,0:T(8,128)(2,1)S(1)}, u32[]{:S(2)}, u32[]{:S(2)}) collective-permute-start(bf16[2,80,160]{2,1,0:T(8,128)(2,1)S(1)} %pad.10.refs_0_), channel_id=1, source_target_pairs={{0,96},{32,0},{64,32},{96,64},{1,97},{33,1},{65,33},{97,65},{2,98}... | collective-permute-start | bytes 153608 | tf_op jit(solution)/shard_map/ppermute | solution.py:279
  18.9 8.4 %collective-permute-start.1 = (bf16[2,80,160]{2,1,0:T(8,128)(2,1)S(1)}, bf16[2,80,160]{2,1,0:T(8,128)(2,1)S(1)}, u32[]{:S(2)}, u32[]{:S(2)}) collective-permute-start(bf16[2,80,160]{2,1,0:T(8,128)(2,1)S(1)} %pad.10.refs_0_), channel_id=1, source_target_pairs={{0,64},{32,96},{64,0},{96,32},{1,65},{33,97},{65,1},{97,33},{2,66}... | collective-permute-start | bytes 153608 | tf_op jit(solution)/shard_map/ppermute | solution.py:279
  21.0 6.3 %collective-permute-start = (bf16[2,80,160]{2,1,0:T(8,128)(2,1)S(1)}, bf16[2,80,160]{2,1,0:T(8,128)(2,1)S(1)}, u32[]{:S(2)}, u32[]{:S(2)}) collective-permute-start(bf16[2,80,160]{2,1,0:T(8,128)(2,1)S(1)} %pad.10.refs_0_), channel_id=1, source_target_pairs={{0,32},{32,64},{64,96},{96,0},{1,33},{33,65},{65,97},{97,1},{2,34}... | collective-permute-start | bytes 153608 | tf_op jit(solution)/shard_map/ppermute | solution.py:279
  29.2 6.5 %copy-start.4 = (s32[8]{0:T(128)S(1)}, s32[8]{0:T(128)}, u32[]{:S(2)}) copy-start(s32[8]{0:T(128)} %param.8) | copy-start | bytes 100
  29.2 8.0 %copy-start.5 = (bf16[4,128,256]{1,2,0:T(8,128)(2,1)S(1)}, bf16[4,128,256]{1,2,0:T(8,128)(2,1)}, u32[]{:S(2)}) copy-start(bf16[4,128,256]{1,2,0:T(8,128)(2,1)} %constant.83.clone) | copy-start | bytes 786436
  29.2 29.1 %all-to-all-start = ((bf16[16,80,640]{2,1,0:T(8,128)(2,1)}), bf16[16,80,640]{2,1,0:T(8,128)(2,1)S(1)}, u32[]{:S(2)}, u32[]{:S(2)}) async-start(bf16[16,80,640]{2,1,0:T(8,128)(2,1)} %shard_map.64), calls=%async_computation | async-start | bytes 3276800 | tf_op jit(solution)/shard_map/all_to_all | solution.py:283
  49.7 1.1 copy-start
  58.3 68.8 %all-to-all-start.2 = ((bf16[32,160,512]{2,1,0:T(8,128)(2,1)}), bf16[32,160,512]{2,1,0:T(8,128)(2,1)}, u32[]{:S(2)}, u32[]{:S(2)}) async-start(bf16[32,160,512]{2,1,0:T(8,128)(2,1)} %bitcast.33), calls=%async_computation.2 | async-start | bytes 10485760 | tf_op jit(solution)/shard_map/all_to_all | solution.py:311
  64.8 37.2 %copy-start.2 = (bf16[1280,640]{0,1:T(8,128)(2,1)}, bf16[1280,640]{0,1:T(8,128)(2,1)S(1)}, u32[]{:S(2)}) copy-start(bf16[1280,640]{0,1:T(8,128)(2,1)S(1)} %copy.18) | copy-start | bytes 4915204
  64.8 37.2 %collective-permute-start.3 = (bf16[640,1280]{1,0:T(8,128)(2,1)S(1)}, bf16[640,1280]{1,0:T(8,128)(2,1)S(1)}, u32[]{:S(2)}, u32[]{:S(2)}) collective-permute-start(bf16[640,1280]{1,0:T(8,128)(2,1)S(1)} %bitcast.31), channel_id=1, source_target_pairs={{0,68},{68,0},{4,64},{64,4},{1,69},{69,1},{5,65},{65,5},{2,70},{70... | collective-permute-start | bytes 4915208 | tf_op jit(solution)/shard_map/ppermute | solution.py:289
  103.7 32.1 %copy-start.3 = (bf16[448,128]{1,0:T(8,128)(2,1)S(1)}, bf16[448,128]{1,0:T(8,128)(2,1)}, u32[]{:S(2)}) copy-start(bf16[448,128]{1,0:T(8,128)(2,1)} %constant.84.clone) | copy-start | bytes 344068
  103.7 32.1 %collective-permute-start.4 = (bf16[2,640,1280]{2,1,0:T(8,128)(2,1)S(1)}, bf16[2,640,1280]{2,1,0:T(8,128)(2,1)}, u32[]{:S(2)}, u32[]{:S(2)}) collective-permute-start(bf16[2,640,1280]{2,1,0:T(8,128)(2,1)S(1)} %pad_maximum_fusion.own_ref), channel_id=1, source_target_pairs={{0,32},{32,0},{1,33},{33,1},{2,34},{34,2},{3,35},{35,3},{4,36},{36... | collective-permute-start | bytes 9830408 | tf_op jit(solution)/shard_map/ppermute | solution.py:291
  127.1 27.8 %all-to-all-start.3 = ((bf16[32,160,128]{2,1,0:T(8,128)(2,1)}), bf16[32,160,128]{2,1,0:T(8,128)(2,1)}, u32[]{:S(2)}, u32[]{:S(2)}) async-start(bf16[32,160,128]{2,1,0:T(8,128)(2,1)} %bitcast.29), calls=%async_computation.3 | async-start | bytes 2621440 | tf_op jit(solution)/shard_map/all_to_all | solution.py:311
  142.8 22.0 %collective-permute-start.9 = (bf16[4,56,640]{2,1,0:T(8,128)(2,1)}, bf16[4,56,640]{2,1,0:T(8,128)(2,1)}, u32[]{:S(2)}, u32[]{:S(2)}) collective-permute-start(bf16[4,56,640]{2,1,0:T(8,128)(2,1)} %get-tuple-element.30), channel_id=1, source_target_pairs={{0,0},{8,32},{16,64},{24,96},{32,8},{40,40},{48,72},{56,104},{64,1... | collective-permute-start | bytes 860168 | tf_op jit(solution)/shard_map/ppermute | solution.py:329
  149.0 19.5 %collective-permute-start.10 = (bf16[4,56,640]{2,1,0:T(8,128)(2,1)}, bf16[4,56,640]{2,1,0:T(8,128)(2,1)}, u32[]{:S(2)}, u32[]{:S(2)}) collective-permute-start(bf16[4,56,640]{2,1,0:T(8,128)(2,1)} %get-tuple-element.31), channel_id=1, source_target_pairs={{0,32},{8,64},{16,96},{24,0},{32,40},{40,72},{48,104},{56,8},{64,4... | collective-permute-start | bytes 860168 | tf_op jit(solution)/shard_map/ppermute | solution.py:329
  150.4 22.5 %collective-permute-start.11 = (bf16[4,56,640]{2,1,0:T(8,128)(2,1)}, bf16[4,56,640]{2,1,0:T(8,128)(2,1)}, u32[]{:S(2)}, u32[]{:S(2)}) collective-permute-start(bf16[4,56,640]{2,1,0:T(8,128)(2,1)} %get-tuple-element.32), channel_id=1, source_target_pairs={{0,64},{8,96},{16,0},{24,32},{32,72},{40,104},{48,8},{56,40},{64,8... | collective-permute-start | bytes 860168 | tf_op jit(solution)/shard_map/ppermute | solution.py:329
  150.5 30.9 %collective-permute-start.12 = (bf16[4,56,640]{2,1,0:T(8,128)(2,1)}, bf16[4,56,640]{2,1,0:T(8,128)(2,1)}, u32[]{:S(2)}, u32[]{:S(2)}) collective-permute-start(bf16[4,56,640]{2,1,0:T(8,128)(2,1)} %get-tuple-element.33), channel_id=1, source_target_pairs={{0,96},{8,0},{16,32},{24,64},{32,104},{40,8},{48,40},{56,72},{64,1... | collective-permute-start | bytes 860168 | tf_op jit(solution)/shard_map/ppermute | solution.py:329
  154.9 26.4 %copy-start.1 = (bf16[4,64,56]{2,1,0:T(8,128)(2,1)S(1)}, bf16[4,64,56]{2,1,0:T(8,128)(2,1)}, u32[]{:S(2)}) copy-start(bf16[4,64,56]{2,1,0:T(8,128)(2,1)} %constant.85.clone.spread_ref) | copy-start | bytes 86020
  160.3 25.0 %collective-permute-start.5 = (bf16[1,56,640]{2,1,0:T(8,128)(2,1)S(1)}, bf16[1,56,640]{2,1,0:T(8,128)(2,1)S(1)}, u32[]{:S(2)}, u32[]{:S(2)}) collective-permute-start(bf16[1,56,640]{2,1,0:T(8,128)(2,1)S(1)} %get-tuple-element.35), channel_id=1, source_target_pairs={{0,0},{8,32},{16,64},{24,96},{32,8},{40,40},{48,72},{56,104},{64,1... | collective-permute-start | bytes 215048 | tf_op jit(solution)/shard_map/ppermute | solution.py:329
  164.8 20.4 %collective-permute-start.6 = (bf16[1,56,640]{2,1,0:T(8,128)(2,1)S(1)}, bf16[1,56,640]{2,1,0:T(8,128)(2,1)S(1)}, u32[]{:S(2)}, u32[]{:S(2)}) collective-permute-start(bf16[1,56,640]{2,1,0:T(8,128)(2,1)S(1)} %get-tuple-element.36), channel_id=1, source_target_pairs={{0,32},{8,64},{16,96},{24,0},{32,40},{40,72},{48,104},{56,8},{64,4... | collective-permute-start | bytes 215048 | tf_op jit(solution)/shard_map/ppermute | solution.py:329
  168.5 16.8 %collective-permute-start.7 = (bf16[1,56,640]{2,1,0:T(8,128)(2,1)S(1)}, bf16[1,56,640]{2,1,0:T(8,128)(2,1)S(1)}, u32[]{:S(2)}, u32[]{:S(2)}) collective-permute-start(bf16[1,56,640]{2,1,0:T(8,128)(2,1)S(1)} %get-tuple-element.37), channel_id=1, source_target_pairs={{0,64},{8,96},{16,0},{24,32},{32,72},{40,104},{48,8},{56,40},{64,8... | collective-permute-start | bytes 215048 | tf_op jit(solution)/shard_map/ppermute | solution.py:329
  172.9 12.4 %collective-permute-start.8 = (bf16[1,56,640]{2,1,0:T(8,128)(2,1)S(1)}, bf16[1,56,640]{2,1,0:T(8,128)(2,1)S(1)}, u32[]{:S(2)}, u32[]{:S(2)}) collective-permute-start(bf16[1,56,640]{2,1,0:T(8,128)(2,1)S(1)} %get-tuple-element.38), channel_id=1, source_target_pairs={{0,96},{8,0},{16,32},{24,64},{32,104},{40,8},{48,40},{56,72},{64,1... | collective-permute-start | bytes 215048 | tf_op jit(solution)/shard_map/ppermute | solution.py:329

commit v5 on v4

--- a/solution.py
+++ b/solution.py
@@ -203,40 +203,45 @@
     )(at, own, keep, select, tiles, far)
 
 
-def unpack_kernel(at_ref, spread_ref, *refs):
-    out_ref = refs[-1]
-    r = pl.program_id(0)
-    occ_local, _, width, occ, a_size = out_ref.shape
-    spread = spread_ref[at_ref[pl.num_programs(0)]]
-
-    def source(part_ref):
+def unpack_kernel(first, at_ref, spread_ref, *refs):
+    out_hbm, buf, sems = refs[-3:]
+    count, occ_local, width, occ, a_size = buf.shape
+    spread = spread_ref[at_ref[count]]
+    copies = []
+    for r in range(count):
         for h in range(width):
-            rows = jnp.dot(spread, part_ref[h], preferred_element_type=jnp.float32)
+            rows = jnp.dot(spread, refs[r][h], preferred_element_type=jnp.float32)
             rows = rows.astype(jnp.bfloat16)
-            out_ref[:, 0, h] = rows.reshape(occ_local, occ, a_size)
-
-    for n in range(4):
-        pl.when(r == n)(functools.partial(source, refs[n]))
+            buf[r, :, h] = rows.reshape(occ_local, occ, a_size)
+        copies.append(
+            pltpu.make_async_copy(
+                buf.at[r],
+                out_hbm.at[:, at_ref[r], pl.ds(first, width)],
+                sems.at[r],
+            )
+        )
+        copies[r].start()
+    for copy in copies:
+        copy.wait()
 
 
 def unpack(parts, spread, x_from, first, out, shape):
     occ_local, count, _, occ, a_size = shape
     width = parts[0].shape[0]
     vmem = pl.BlockSpec(memory_space=pltpu.VMEM)
+    hbm = pl.BlockSpec(memory_space=pl.ANY)
     so_far = [] if out is None else [out]
     return pl.pallas_call(
-        unpack_kernel,
-        grid_spec=pltpu.PrefetchScalarGridSpec(
-            num_scalar_prefetch=1,
-            grid=(count,),
-            in_specs=[vmem] * (1 + count)
-            + [pl.BlockSpec(memory_space=pl.ANY)] * len(so_far),
-            out_specs=pl.BlockSpec(
-                (occ_local, 1, width, occ, a_size),
-                lambda r, at: (0, at[r], first // width, 0, 0),
-            ),
-        ),
+        functools.partial(unpack_kernel, first),
+        in_specs=[pl.BlockSpec(memory_space=pltpu.SMEM)]
+        + [vmem] * (1 + count)
+        + [hbm] * len(so_far),
+        out_specs=hbm,
         out_shape=jax.ShapeDtypeStruct(shape, jnp.bfloat16),
+        scratch_shapes=[
+            pltpu.VMEM((count, occ_local, width, occ, a_size), jnp.bfloat16),
+            pltpu.SemaphoreType.DMA((count,)),
+        ],
         input_output_aliases={2 + count: 0} if so_far else {},
         compiler_params=pltpu.CompilerParams(vmem_limit_bytes=16 << 20),
     )(x_from, spread, *parts, *so_far)

time: 188 us -> 187 us (level)
  Pallas kernels: 32.7 us -> 30.4 us
    pallas_call x2, Pallas kernels: 6.29 us -> 3.98 us  [unpack(): pl.pallas_call(functools.partial(unpack_kernel, first), in_specs=[pl.Bloc...]
  transfers between devices with their start and end apart: 17 -> 17, of which waited for: 7 -> 8; matrix products, arithmetic and copies ran while one was open for 4% -> 4% of each run, Pallas kernels for 16% -> 16%
where the time goes in v5:
time: 187 us
  waiting for transfers between devices  78.5 us (42%)
  starting transfers between devices  64.1 us (34%)
  Pallas kernels  30.4 us (16%)
  local copies, waits for them, and re-layouts  10.7 us (6%)
  other arithmetic  2.15 us (1%)
    ppermute x1, waiting for transfers between devices, per_device(): other = lax.ppermute(half, ('yh', 'yl'), swap_y)  35.2 us
    ppermute x8, starting transfers between devices, per_device(): landed.append(lax.ppermute(parts[r], OCC + ('x',), perm))  27.9 us
    all_to_all x2, waiting for transfers between devices, per_device(): tiles = lax.all_to_all(mid, TILE, 0, 0, tiled=True)  25.9 us
    all_to_all x2, starting transfers between devices, per_device(): tiles = lax.all_to_all(mid, TILE, 0, 0, tiled=True)  13.6 us
    pallas_call x2, Pallas kernels, ladder_rows(): pl.pallas_call(functools.partial(ladder_kernel, first), in_specs=[pl.Bloc...  12.4 us
    pallas_call x1, Pallas kernels, middle(): pl.pallas_call(functools.partial(middle_kernel, q_local, dests, widths),...  12.1 us
    all_to_all x1, starting transfers between devices, share(): lax.all_to_all(jnp.broadcast_to(x[None], (count,) + x.shape), axes, 0, 0,...  10.7 us
    all_to_all x1, waiting for transfers between devices, per_device(): half = lax.all_to_all(half, TILE[1:], 0, 0, tiled=True)  7.52 us
  transfers between devices with their start and end apart: 17, of which 8 were waited for; matrix products, arithmetic and copies ran while one was open for 4% of the time, Pallas kernels for 16%

profile of v5, /device:TPU:24, one launch (start us, length us, event | category | flops | bytes accessed | tf_op | source)
XLA Modules:
  0.0 186.6 jit_solution(16136557248087942847)
XLA Ops:
  0.0 0.9 copy.16
  0.9 0.1 broadcast_in_dim.35
  1.0 1.0 broadcast_in_dim.36
  2.1 10.7 %all-to-all-start.1 = ((bf16[128,20,128]{2,1,0:T(8,128)(2,1)}), bf16[128,20,128]{2,1,0:T(8,128)(2,1)}, u32[]{:S(2)}, u32[]{:S(2)}) async-start(bf16[128,20,128]{2,1,0:T(8,128)(2,1)} %broadcast_in_dim.36), calls=%async_computation.1 | async-start | bytes 1572864 | tf_op jit(solution)/shard_map/all_to_all | solution.py:46
  12.7 0.0 slice-start
  12.7 1.9 %slice-done = bf16[75,160,2]{2,1,0:T(8,128)(2,1)S(1)} async-done(((bf16[75,160,640]{2,1,0:T(8,128)(2,1)}), bf16[75,160,2]{2,1,0:T(8,128)(2,1)S(1)}, s32[]{:S(2)}) %slice-start) | async-done | bytes 48024 | tf_op jit(solution)/shard_map/slice | solution.py:279
  14.7 2.9 %copy.21 = bf16[75,160,2]{1,0,2:T(8,128)(2,1)S(1)} copy(bf16[75,160,2]{2,1,0:T(8,128)(2,1)S(1)} %slice-done) | data formatting | bytes 96000
  17.6 1.2 collective-permute-start.2
  18.9 2.1 %collective-permute-start.1 = (bf16[2,80,160]{2,1,0:T(8,128)(2,1)S(1)}, bf16[2,80,160]{2,1,0:T(8,128)(2,1)S(1)}, u32[]{:S(2)}, u32[]{:S(2)}) collective-permute-start(bf16[2,80,160]{2,1,0:T(8,128)(2,1)S(1)} %pad.10.refs_0_), channel_id=1, source_target_pairs={{0,64},{32,96},{64,0},{96,32},{1,65},{33,97},{65,1},{97,33},{2,66}... | collective-permute-start | bytes 153608 | tf_op jit(solution)/shard_map/ppermute | solution.py:284
  21.0 0.0 collective-permute-start
  21.0 0.1 pad_add_fusion.2.at_ref
  21.1 2.6 %collective-permute-done.2.refs_3_ = bf16[2,80,160]{2,1,0:T(8,128)(2,1)S(1)} collective-permute-done((bf16[2,80,160]{2,1,0:T(8,128)(2,1)S(1)}, bf16[2,80,160]{2,1,0:T(8,128)(2,1)S(1)}, u32[]{:S(2)}, u32[]{:S(2)}) %collective-permute-start.2) | collective-permute-done | bytes 51232 | tf_op jit(solution)/shard_map/ppermute | solution.py:284
  23.7 3.6 %collective-permute-done.1.refs_2_ = bf16[2,80,160]{2,1,0:T(8,128)(2,1)S(1)} collective-permute-done((bf16[2,80,160]{2,1,0:T(8,128)(2,1)S(1)}, bf16[2,80,160]{2,1,0:T(8,128)(2,1)S(1)}, u32[]{:S(2)}, u32[]{:S(2)}) %collective-permute-start.1) | collective-permute-done | bytes 51232 | tf_op jit(solution)/shard_map/ppermute | solution.py:284
  27.3 0.0 collective-permute-done.refs_1_
  27.3 1.9 %shard_map.64 = bf16[16,80,640]{2,1,0:T(8,128)(2,1)} custom-call(s32[2]{0:T(128)S(1)} %pad_add_fusion.2.at_ref, bf16[2,80,160]{2,1,0:T(8,128)(2,1)S(1)} %pad.10.refs_0_, bf16[2,80,160]{2,1,0:T(8,128)(2,1)S(1)} %collective-permute-done.refs_1_, bf16[2,80,160]{2,1,0:T(8,128)(2,1)S(1)} %collective-permute-done.1.refs_2_, ...), custom_call_target="tpu_custom_call" | custom-call | tf_op jit(solution)/shard_map/pallas_call | solution.py:123
  29.2 0.0 all-to-all-done.1
  29.2 6.5 %all-to-all-start = ((bf16[16,80,640]{2,1,0:T(8,128)(2,1)}), bf16[16,80,640]{2,1,0:T(8,128)(2,1)S(1)}, u32[]{:S(2)}, u32[]{:S(2)}) async-start(bf16[16,80,640]{2,1,0:T(8,128)(2,1)} %shard_map.64), calls=%async_computation | async-start | bytes 3276800 | tf_op jit(solution)/shard_map/all_to_all | solution.py:288
  35.8 0.0 copy-done.4
  35.8 0.1 select_reduce_fusion
  35.9 0.1 broadcast_bitcast_fusion
  36.0 1.3 reshape.65
  37.2 0.0 copy-done.5
  37.2 0.4 fusion.1.a_ref
  37.6 12.1 %shard_map.65 = (bf16[32,2,80,512]{3,2,1,0:T(8,128)(2,1)}, bf16[32,2,80,128]{3,2,1,0:T(8,128)(2,1)S(1)}) custom-call(bf16[75,160,640]{2,1,0:T(8,128)(2,1)} %b_ref.1, bf16[640,256]{1,0:T(8,128)(2,1)S(1)} %fusion.1.a_ref), custom_call_target="tpu_custom_call" | custom-call | flops 3932160000 | bytes 21913600 | tf_op jit(solution)/shard_map/pallas_call | solution.py:80
  49.7 1.1 copy-done
  50.8 7.5 %all-to-all-done = bf16[16,80,640]{2,1,0:T(8,128)(2,1)S(1)} async-done(((bf16[16,80,640]{2,1,0:T(8,128)(2,1)}), bf16[16,80,640]{2,1,0:T(8,128)(2,1)S(1)}, u32[]{:S(2)}, u32[]{:S(2)}) %all-to-all-start) | async-done | bytes 1638432 | tf_op jit(solution)/shard_map/all_to_all | solution.py:288
  58.3 5.2 %all-to-all-start.2 = ((bf16[32,160,512]{2,1,0:T(8,128)(2,1)}), bf16[32,160,512]{2,1,0:T(8,128)(2,1)}, u32[]{:S(2)}, u32[]{:S(2)}) async-start(bf16[32,160,512]{2,1,0:T(8,128)(2,1)} %bitcast.33), calls=%async_computation.2 | async-start | bytes 10485760 | tf_op jit(solution)/shard_map/all_to_all | solution.py:316
  63.5 1.2 copy.18
  64.8 0.0 copy-start.2
  64.8 2.0 %collective-permute-start.3 = (bf16[640,1280]{1,0:T(8,128)(2,1)S(1)}, bf16[640,1280]{1,0:T(8,128)(2,1)S(1)}, u32[]{:S(2)}, u32[]{:S(2)}) collective-permute-start(bf16[640,1280]{1,0:T(8,128)(2,1)S(1)} %bitcast.31), channel_id=1, source_target_pairs={{0,68},{68,0},{4,64},{64,4},{1,69},{69,1},{5,65},{65,5},{2,70},{70... | collective-permute-start | bytes 4915208 | tf_op jit(solution)/shard_map/ppermute | solution.py:294
  66.7 35.2 %collective-permute-done.3 = bf16[640,1280]{1,0:T(8,128)(2,1)S(1)} collective-permute-done((bf16[640,1280]{1,0:T(8,128)(2,1)S(1)}, bf16[640,1280]{1,0:T(8,128)(2,1)S(1)}, u32[]{:S(2)}, u32[]{:S(2)}) %collective-permute-start.3) | collective-permute-done | bytes 1638432 | tf_op jit(solution)/shard_map/ppermute | solution.py:294
  101.9 0.0 copy-done.2
  101.9 1.7 pad_maximum_fusion.own_ref
  103.7 0.0 copy-start.3
  103.7 0.1 collective-permute-start.4
  103.8 23.3 %all-to-all-done.2 = bf16[32,160,512]{2,1,0:T(8,128)(2,1)} async-done(((bf16[32,160,512]{2,1,0:T(8,128)(2,1)}), bf16[32,160,512]{2,1,0:T(8,128)(2,1)}, u32[]{:S(2)}, u32[]{:S(2)}) %all-to-all-start.2) | async-done | bytes 5242912 | tf_op jit(solution)/shard_map/all_to_all | solution.py:316
  127.1 8.4 %all-to-all-start.3 = ((bf16[32,160,128]{2,1,0:T(8,128)(2,1)}), bf16[32,160,128]{2,1,0:T(8,128)(2,1)}, u32[]{:S(2)}, u32[]{:S(2)}) async-start(bf16[32,160,128]{2,1,0:T(8,128)(2,1)} %bitcast.29), calls=%async_computation.3 | async-start | bytes 2621440 | tf_op jit(solution)/shard_map/all_to_all | solution.py:316
  135.5 0.1 dynamic_slice.6
  135.6 0.1 pad_add_fusion.1.at_ref
  135.7 0.1 broadcast_and_fusion
  135.7 0.0 copy-done.3
  135.8 0.0 collective-permute-done.4.far_hbm
  135.8 7.0 %shard_map.66 = (bf16[4,56,640]{2,1,0:T(8,128)(2,1)}, bf16[4,56,640]{2,1,0:T(8,128)(2,1)}, bf16[4,56,640]{2,1,0:T(8,128)(2,1)}, bf16[4,56,640]{2,1,0:T(8,128)(2,1)}) custom-call(s32[2]{0:T(128)S(1)} %pad_add_fusion.1.at_ref, bf16[2,640,1280]{2,1,0:T(8,128)(2,1)S(1)} %pad_maximum_fusion.own_ref, f32[8,640]{1,0:T(8,128)S(1)} %pad_convert_fusion.keep_ref, ...), custom_call_target="tpu_custom_call" | custom-call | flops 3355443200 | bytes 11796480 | tf_op jit(solution)/shard_map/pallas_call | solution.py:186
  142.8 6.2 %collective-permute-start.9 = (bf16[4,56,640]{2,1,0:T(8,128)(2,1)}, bf16[4,56,640]{2,1,0:T(8,128)(2,1)}, u32[]{:S(2)}, u32[]{:S(2)}) collective-permute-start(bf16[4,56,640]{2,1,0:T(8,128)(2,1)} %get-tuple-element.30), channel_id=1, source_target_pairs={{0,0},{8,32},{16,64},{24,96},{32,8},{40,40},{48,72},{56,104},{64,1... | collective-permute-start | bytes 860168 | tf_op jit(solution)/shard_map/ppermute | solution.py:334
  149.0 1.5 collective-permute-start.10
  150.4 0.0 collective-permute-start.11
  150.5 1.8 collective-permute-start.12
  152.3 2.6 %all-to-all-done.3 = bf16[32,160,128]{2,1,0:T(8,128)(2,1)} async-done(((bf16[32,160,128]{2,1,0:T(8,128)(2,1)}), bf16[32,160,128]{2,1,0:T(8,128)(2,1)}, u32[]{:S(2)}, u32[]{:S(2)}) %all-to-all-start.3) | async-done | bytes 1310752 | tf_op jit(solution)/shard_map/all_to_all | solution.py:316
  154.9 5.4 %shard_map.67 = (bf16[1,56,640]{2,1,0:T(8,128)(2,1)S(1)}, bf16[1,56,640]{2,1,0:T(8,128)(2,1)S(1)}, bf16[1,56,640]{2,1,0:T(8,128)(2,1)S(1)}, bf16[1,56,640]{2,1,0:T(8,128)(2,1)S(1)}) custom-call(s32[2]{0:T(128)S(1)} %pad_add_fusion.1.at_ref, bf16[2,640,1280]{2,1,0:T(8,128)(2,1)S(1)} %pad_maximum_fusion.own_ref, f32[8,640]{1,0:T(8,128)S(1)} %pad_convert_fusion.keep_ref, ...), custom_call_target="tpu_custom_call" | custom-call | flops 838860800 | bytes 7864320 | tf_op jit(solution)/shard_map/pallas_call | solution.py:186
  160.3 4.5 %collective-permute-start.5 = (bf16[1,56,640]{2,1,0:T(8,128)(2,1)S(1)}, bf16[1,56,640]{2,1,0:T(8,128)(2,1)S(1)}, u32[]{:S(2)}, u32[]{:S(2)}) collective-permute-start(bf16[1,56,640]{2,1,0:T(8,128)(2,1)S(1)} %get-tuple-element.35), channel_id=1, source_target_pairs={{0,0},{8,32},{16,64},{24,96},{32,8},{40,40},{48,72},{56,104},{64,1... | collective-permute-start | bytes 215048 | tf_op jit(solution)/shard_map/ppermute | solution.py:334
  164.8 0.0 collective-permute-done.9.refs_0_
  164.8 3.7 %collective-permute-start.6 = (bf16[1,56,640]{2,1,0:T(8,128)(2,1)S(1)}, bf16[1,56,640]{2,1,0:T(8,128)(2,1)S(1)}, u32[]{:S(2)}, u32[]{:S(2)}) collective-permute-start(bf16[1,56,640]{2,1,0:T(8,128)(2,1)S(1)} %get-tuple-element.36), channel_id=1, source_target_pairs={{0,32},{8,64},{16,96},{24,0},{32,40},{40,72},{48,104},{56,8},{64,4... | collective-permute-start | bytes 215048 | tf_op jit(solution)/shard_map/ppermute | solution.py:334
  168.5 0.0 collective-permute-done.10.refs_1_
  168.5 4.4 %collective-permute-start.7 = (bf16[1,56,640]{2,1,0:T(8,128)(2,1)S(1)}, bf16[1,56,640]{2,1,0:T(8,128)(2,1)S(1)}, u32[]{:S(2)}, u32[]{:S(2)}) collective-permute-start(bf16[1,56,640]{2,1,0:T(8,128)(2,1)S(1)} %get-tuple-element.37), channel_id=1, source_target_pairs={{0,64},{8,96},{16,0},{24,32},{32,72},{40,104},{48,8},{56,40},{64,8... | collective-permute-start | bytes 215048 | tf_op jit(solution)/shard_map/ppermute | solution.py:334
  172.9 0.0 collective-permute-done.11.refs_2_
  172.9 5.8 %collective-permute-start.8 = (bf16[1,56,640]{2,1,0:T(8,128)(2,1)S(1)}, bf16[1,56,640]{2,1,0:T(8,128)(2,1)S(1)}, u32[]{:S(2)}, u32[]{:S(2)}) collective-permute-start(bf16[1,56,640]{2,1,0:T(8,128)(2,1)S(1)} %get-tuple-element.38), channel_id=1, source_target_pairs={{0,96},{8,0},{16,32},{24,64},{32,104},{40,8},{48,40},{56,72},{64,1... | collective-permute-start | bytes 215048 | tf_op jit(solution)/shard_map/ppermute | solution.py:334
  178.8 0.1 pad_add_fusion.at_ref
  178.8 2.5 %collective-permute-done.12.refs_3_ = bf16[4,56,640]{2,1,0:T(8,128)(2,1)} collective-permute-done((bf16[4,56,640]{2,1,0:T(8,128)(2,1)}, bf16[4,56,640]{2,1,0:T(8,128)(2,1)}, u32[]{:S(2)}, u32[]{:S(2)}) %collective-permute-start.12) | collective-permute-done | bytes 286752 | tf_op jit(solution)/shard_map/ppermute | solution.py:334
  181.3 2.5 %shard_map.68.refs_4_ = bf16[4,4,5,16,640]{4,3,2,1,0:T(8,128)(2,1)} custom-call(s32[5]{0:T(128)S(1)} %pad_add_fusion.at_ref, bf16[4,64,56]{2,1,0:T(8,128)(2,1)S(1)} %copy-done.1, bf16[4,56,640]{2,1,0:T(8,128)(2,1)} %collective-permute-done.9.refs_0_, bf16[4,56,640]{2,1,0:T(8,128)(2,1)} %collective-permute-done.10.refs_1_, ...), custom_call_target="tpu_custom_call" | custom-call | tf_op jit(solution)/shard_map/pallas_call | solution.py:234
  183.8 0.0 collective-permute-done.5.refs_0_
  183.9 0.0 collective-permute-done.6.refs_1_
  183.9 0.0 collective-permute-done.7.refs_2_
  183.9 1.1 collective-permute-done.8.refs_3_
  185.0 1.4 shard_map.69
  (12 shorter events, 0.1 us)
Async XLA Ops:
  2.1 27.2 %all-to-all-start.1 = ((bf16[128,20,128]{2,1,0:T(8,128)(2,1)}), bf16[128,20,128]{2,1,0:T(8,128)(2,1)}, u32[]{:S(2)}, u32[]{:S(2)}) async-start(bf16[128,20,128]{2,1,0:T(8,128)(2,1)} %broadcast_in_dim.36), calls=%async_computation.1 | async-start | bytes 1572864 | tf_op jit(solution)/shard_map/all_to_all | solution.py:46
  12.7 1.9 %slice-start = ((bf16[75,160,640]{2,1,0:T(8,128)(2,1)}), bf16[75,160,2]{2,1,0:T(8,128)(2,1)S(1)}, s32[]{:S(2)}) async-start(bf16[75,160,640]{2,1,0:T(8,128)(2,1)} %b_ref.1), calls=%async_computation.4 | async-start | bytes 6144000 | tf_op jit(solution)/shard_map/slice | solution.py:279
  17.6 6.0 %collective-permute-start.2 = (bf16[2,80,160]{2,1,0:T(8,128)(2,1)S(1)}, bf16[2,80,160]{2,1,0:T(8,128)(2,1)S(1)}, u32[]{:S(2)}, u32[]{:S(2)}) collective-permute-start(bf16[2,80,160]{2,1,0:T(8,128)(2,1)S(1)} %pad.10.refs_0_), channel_id=1, source_target_pairs={{0,96},{32,0},{64,32},{96,64},{1,97},{33,1},{65,33},{97,65},{2,98}... | collective-permute-start | bytes 153608 | tf_op jit(solution)/shard_map/ppermute | solution.py:284
  18.9 8.4 %collective-permute-start.1 = (bf16[2,80,160]{2,1,0:T(8,128)(2,1)S(1)}, bf16[2,80,160]{2,1,0:T(8,128)(2,1)S(1)}, u32[]{:S(2)}, u32[]{:S(2)}) collective-permute-start(bf16[2,80,160]{2,1,0:T(8,128)(2,1)S(1)} %pad.10.refs_0_), channel_id=1, source_target_pairs={{0,64},{32,96},{64,0},{96,32},{1,65},{33,97},{65,1},{97,33},{2,66}... | collective-permute-start | bytes 153608 | tf_op jit(solution)/shard_map/ppermute | solution.py:284
  21.0 6.3 %collective-permute-start = (bf16[2,80,160]{2,1,0:T(8,128)(2,1)S(1)}, bf16[2,80,160]{2,1,0:T(8,128)(2,1)S(1)}, u32[]{:S(2)}, u32[]{:S(2)}) collective-permute-start(bf16[2,80,160]{2,1,0:T(8,128)(2,1)S(1)} %pad.10.refs_0_), channel_id=1, source_target_pairs={{0,32},{32,64},{64,96},{96,0},{1,33},{33,65},{65,97},{97,1},{2,34}... | collective-permute-start | bytes 153608 | tf_op jit(solution)/shard_map/ppermute | solution.py:284
  29.2 6.5 %copy-start.4 = (s32[8]{0:T(128)S(1)}, s32[8]{0:T(128)}, u32[]{:S(2)}) copy-start(s32[8]{0:T(128)} %param.8) | copy-start | bytes 100
  29.2 8.0 %copy-start.5 = (bf16[4,128,256]{1,2,0:T(8,128)(2,1)S(1)}, bf16[4,128,256]{1,2,0:T(8,128)(2,1)}, u32[]{:S(2)}) copy-start(bf16[4,128,256]{1,2,0:T(8,128)(2,1)} %constant.83.clone) | copy-start | bytes 786436
  29.2 29.1 %all-to-all-start = ((bf16[16,80,640]{2,1,0:T(8,128)(2,1)}), bf16[16,80,640]{2,1,0:T(8,128)(2,1)S(1)}, u32[]{:S(2)}, u32[]{:S(2)}) async-start(bf16[16,80,640]{2,1,0:T(8,128)(2,1)} %shard_map.64), calls=%async_computation | async-start | bytes 3276800 | tf_op jit(solution)/shard_map/all_to_all | solution.py:288
  49.7 1.1 copy-start
  58.3 68.8 %all-to-all-start.2 = ((bf16[32,160,512]{2,1,0:T(8,128)(2,1)}), bf16[32,160,512]{2,1,0:T(8,128)(2,1)}, u32[]{:S(2)}, u32[]{:S(2)}) async-start(bf16[32,160,512]{2,1,0:T(8,128)(2,1)} %bitcast.33), calls=%async_computation.2 | async-start | bytes 10485760 | tf_op jit(solution)/shard_map/all_to_all | solution.py:316
  64.8 37.2 %copy-start.2 = (bf16[1280,640]{0,1:T(8,128)(2,1)}, bf16[1280,640]{0,1:T(8,128)(2,1)S(1)}, u32[]{:S(2)}) copy-start(bf16[1280,640]{0,1:T(8,128)(2,1)S(1)} %copy.18) | copy-start | bytes 4915204
  64.8 37.2 %collective-permute-start.3 = (bf16[640,1280]{1,0:T(8,128)(2,1)S(1)}, bf16[640,1280]{1,0:T(8,128)(2,1)S(1)}, u32[]{:S(2)}, u32[]{:S(2)}) collective-permute-start(bf16[640,1280]{1,0:T(8,128)(2,1)S(1)} %bitcast.31), channel_id=1, source_target_pairs={{0,68},{68,0},{4,64},{64,4},{1,69},{69,1},{5,65},{65,5},{2,70},{70... | collective-permute-start | bytes 4915208 | tf_op jit(solution)/shard_map/ppermute | solution.py:294
  103.7 32.1 %copy-start.3 = (bf16[448,128]{1,0:T(8,128)(2,1)S(1)}, bf16[448,128]{1,0:T(8,128)(2,1)}, u32[]{:S(2)}) copy-start(bf16[448,128]{1,0:T(8,128)(2,1)} %constant.84.clone) | copy-start | bytes 344068
  103.7 32.1 %collective-permute-start.4 = (bf16[2,640,1280]{2,1,0:T(8,128)(2,1)S(1)}, bf16[2,640,1280]{2,1,0:T(8,128)(2,1)}, u32[]{:S(2)}, u32[]{:S(2)}) collective-permute-start(bf16[2,640,1280]{2,1,0:T(8,128)(2,1)S(1)} %pad_maximum_fusion.own_ref), channel_id=1, source_target_pairs={{0,32},{32,0},{1,33},{33,1},{2,34},{34,2},{3,35},{35,3},{4,36},{36... | collective-permute-start | bytes 9830408 | tf_op jit(solution)/shard_map/ppermute | solution.py:296
  127.1 27.8 %all-to-all-start.3 = ((bf16[32,160,128]{2,1,0:T(8,128)(2,1)}), bf16[32,160,128]{2,1,0:T(8,128)(2,1)}, u32[]{:S(2)}, u32[]{:S(2)}) async-start(bf16[32,160,128]{2,1,0:T(8,128)(2,1)} %bitcast.29), calls=%async_computation.3 | async-start | bytes 2621440 | tf_op jit(solution)/shard_map/all_to_all | solution.py:316
  142.8 22.0 %collective-permute-start.9 = (bf16[4,56,640]{2,1,0:T(8,128)(2,1)}, bf16[4,56,640]{2,1,0:T(8,128)(2,1)}, u32[]{:S(2)}, u32[]{:S(2)}) collective-permute-start(bf16[4,56,640]{2,1,0:T(8,128)(2,1)} %get-tuple-element.30), channel_id=1, source_target_pairs={{0,0},{8,32},{16,64},{24,96},{32,8},{40,40},{48,72},{56,104},{64,1... | collective-permute-start | bytes 860168 | tf_op jit(solution)/shard_map/ppermute | solution.py:334
  149.0 19.5 %collective-permute-start.10 = (bf16[4,56,640]{2,1,0:T(8,128)(2,1)}, bf16[4,56,640]{2,1,0:T(8,128)(2,1)}, u32[]{:S(2)}, u32[]{:S(2)}) collective-permute-start(bf16[4,56,640]{2,1,0:T(8,128)(2,1)} %get-tuple-element.31), channel_id=1, source_target_pairs={{0,32},{8,64},{16,96},{24,0},{32,40},{40,72},{48,104},{56,8},{64,4... | collective-permute-start | bytes 860168 | tf_op jit(solution)/shard_map/ppermute | solution.py:334
  150.4 22.5 %collective-permute-start.11 = (bf16[4,56,640]{2,1,0:T(8,128)(2,1)}, bf16[4,56,640]{2,1,0:T(8,128)(2,1)}, u32[]{:S(2)}, u32[]{:S(2)}) collective-permute-start(bf16[4,56,640]{2,1,0:T(8,128)(2,1)} %get-tuple-element.32), channel_id=1, source_target_pairs={{0,64},{8,96},{16,0},{24,32},{32,72},{40,104},{48,8},{56,40},{64,8... | collective-permute-start | bytes 860168 | tf_op jit(solution)/shard_map/ppermute | solution.py:334
  150.5 30.9 %collective-permute-start.12 = (bf16[4,56,640]{2,1,0:T(8,128)(2,1)}, bf16[4,56,640]{2,1,0:T(8,128)(2,1)}, u32[]{:S(2)}, u32[]{:S(2)}) collective-permute-start(bf16[4,56,640]{2,1,0:T(8,128)(2,1)} %get-tuple-element.33), channel_id=1, source_target_pairs={{0,96},{8,0},{16,32},{24,64},{32,104},{40,8},{48,40},{56,72},{64,1... | collective-permute-start | bytes 860168 | tf_op jit(solution)/shard_map/ppermute | solution.py:334
  154.9 26.4 %copy-start.1 = (bf16[4,64,56]{2,1,0:T(8,128)(2,1)S(1)}, bf16[4,64,56]{2,1,0:T(8,128)(2,1)}, u32[]{:S(2)}) copy-start(bf16[4,64,56]{2,1,0:T(8,128)(2,1)} %constant.85.clone.spread_ref) | copy-start | bytes 86020
  160.3 23.6 %collective-permute-start.5 = (bf16[1,56,640]{2,1,0:T(8,128)(2,1)S(1)}, bf16[1,56,640]{2,1,0:T(8,128)(2,1)S(1)}, u32[]{:S(2)}, u32[]{:S(2)}) collective-permute-start(bf16[1,56,640]{2,1,0:T(8,128)(2,1)S(1)} %get-tuple-element.35), channel_id=1, source_target_pairs={{0,0},{8,32},{16,64},{24,96},{32,8},{40,40},{48,72},{56,104},{64,1... | collective-permute-start | bytes 215048 | tf_op jit(solution)/shard_map/ppermute | solution.py:334
  164.8 19.0 %collective-permute-start.6 = (bf16[1,56,640]{2,1,0:T(8,128)(2,1)S(1)}, bf16[1,56,640]{2,1,0:T(8,128)(2,1)S(1)}, u32[]{:S(2)}, u32[]{:S(2)}) collective-permute-start(bf16[1,56,640]{2,1,0:T(8,128)(2,1)S(1)} %get-tuple-element.36), channel_id=1, source_target_pairs={{0,32},{8,64},{16,96},{24,0},{32,40},{40,72},{48,104},{56,8},{64,4... | collective-permute-start | bytes 215048 | tf_op jit(solution)/shard_map/ppermute | solution.py:334
  168.5 15.3 %collective-permute-start.7 = (bf16[1,56,640]{2,1,0:T(8,128)(2,1)S(1)}, bf16[1,56,640]{2,1,0:T(8,128)(2,1)S(1)}, u32[]{:S(2)}, u32[]{:S(2)}) collective-permute-start(bf16[1,56,640]{2,1,0:T(8,128)(2,1)S(1)} %get-tuple-element.37), channel_id=1, source_target_pairs={{0,64},{8,96},{16,0},{24,32},{32,72},{40,104},{48,8},{56,40},{64,8... | collective-permute-start | bytes 215048 | tf_op jit(solution)/shard_map/ppermute | solution.py:334
  172.9 12.1 %collective-permute-start.8 = (bf16[1,56,640]{2,1,0:T(8,128)(2,1)S(1)}, bf16[1,56,640]{2,1,0:T(8,128)(2,1)S(1)}, u32[]{:S(2)}, u32[]{:S(2)}) collective-permute-start(bf16[1,56,640]{2,1,0:T(8,128)(2,1)S(1)} %get-tuple-element.38), channel_id=1, source_target_pairs={{0,96},{8,0},{16,32},{24,64},{32,104},{40,8},{48,40},{56,72},{64,1... | collective-permute-start | bytes 215048 | tf_op jit(solution)/shard_map/ppermute | solution.py:334

commit v6 on v5

--- a/solution.py
+++ b/solution.py
@@ -152,16 +152,19 @@
     ]
     for copy in (tiles[0], tiles[1], fars[0], tiles[2], fars[1], tiles[3]):
         copy.start()
-    for n, (c, yl) in enumerate(steps):
-        tiles[n].wait()
+    for c in range(2):
+        tiles[2 * c].wait()
+        tiles[2 * c + 1].wait()
         if c:
-            fars[yl].wait()
+            fars[0].wait()
+            fars[1].wait()
+        w = far_buf if c else own_ref
         part = jnp.dot(
-            (far_buf if c else own_ref)[yl],
-            m_buf[n].reshape(sources * depth, lanes),
+            jnp.concatenate([w[0], w[1]], axis=1),
+            m_buf[2 * c : 2 * c + 2].reshape(2 * sources * depth, lanes),
             preferred_element_type=jnp.float32,
         )
-        acc[...] = part if n == 0 else acc[...] + part
+        acc[...] = part if c == 0 else acc[...] + part
     for h in range(width):
         part = acc[:, h * NPAIR : (h + 1) * NPAIR].astype(jnp.bfloat16)
         rows = lax.dot_general(

time: 187 us -> 187 us (level)
  transfers between devices with their start and end apart: 17 -> 17, of which waited for: 8 -> 9; matrix products, arithmetic and copies ran while one was open for 4% -> 4% of each run, Pallas kernels for 16% -> 16%
where the time goes in v6:
time: 187 us
  waiting for transfers between devices  78.2 us (42%)
  starting transfers between devices  64 us (34%)
  Pallas kernels  30.7 us (16%)
  local copies, waits for them, and re-layouts  10.7 us (6%)
  other arithmetic  2.15 us (1%)
    ppermute x1, waiting for transfers between devices, per_device(): other = lax.ppermute(half, ('yh', 'yl'), swap_y)  35.2 us
    ppermute x8, starting transfers between devices, per_device(): landed.append(lax.ppermute(parts[r], OCC + ('x',), perm))  27.8 us
    all_to_all x2, waiting for transfers between devices, per_device(): tiles = lax.all_to_all(mid, TILE, 0, 0, tiled=True)  25.6 us
    all_to_all x2, starting transfers between devices, per_device(): tiles = lax.all_to_all(mid, TILE, 0, 0, tiled=True)  13.6 us
    pallas_call x2, Pallas kernels, ladder_rows(): pl.pallas_call(functools.partial(ladder_kernel, first), in_specs=[pl.Bloc...  12.7 us
    pallas_call x1, Pallas kernels, middle(): pl.pallas_call(functools.partial(middle_kernel, q_local, dests, widths),...  12.1 us
    all_to_all x1, starting transfers between devices, share(): lax.all_to_all(jnp.broadcast_to(x[None], (count,) + x.shape), axes, 0, 0,...  10.7 us
    all_to_all x1, waiting for transfers between devices, per_device(): half = lax.all_to_all(half, TILE[1:], 0, 0, tiled=True)  7.52 us
  transfers between devices with their start and end apart: 17, of which 9 were waited for; matrix products, arithmetic and copies ran while one was open for 4% of the time, Pallas kernels for 16%

profile of v6, /device:TPU:24, one launch (start us, length us, event | category | flops | bytes accessed | tf_op | source)
XLA Modules:
  0.0 186.6 jit_solution(6988400957536052408)
XLA Ops:
  0.0 0.9 copy.16
  0.9 0.1 broadcast_in_dim.35
  1.0 1.0 broadcast_in_dim.36
  2.1 10.7 %all-to-all-start.1 = ((bf16[128,20,128]{2,1,0:T(8,128)(2,1)}), bf16[128,20,128]{2,1,0:T(8,128)(2,1)}, u32[]{:S(2)}, u32[]{:S(2)}) async-start(bf16[128,20,128]{2,1,0:T(8,128)(2,1)} %broadcast_in_dim.36), calls=%async_computation.1 | async-start | bytes 1572864 | tf_op jit(solution)/shard_map/all_to_all | solution.py:46
  12.7 0.0 slice-start
  12.7 1.9 %slice-done = bf16[75,160,2]{2,1,0:T(8,128)(2,1)S(1)} async-done(((bf16[75,160,640]{2,1,0:T(8,128)(2,1)}), bf16[75,160,2]{2,1,0:T(8,128)(2,1)S(1)}, s32[]{:S(2)}) %slice-start) | async-done | bytes 48024 | tf_op jit(solution)/shard_map/slice | solution.py:282
  14.7 2.9 %copy.21 = bf16[75,160,2]{1,0,2:T(8,128)(2,1)S(1)} copy(bf16[75,160,2]{2,1,0:T(8,128)(2,1)S(1)} %slice-done) | data formatting | bytes 96000
  17.6 1.2 collective-permute-start.2
  18.9 2.1 %collective-permute-start.1 = (bf16[2,80,160]{2,1,0:T(8,128)(2,1)S(1)}, bf16[2,80,160]{2,1,0:T(8,128)(2,1)S(1)}, u32[]{:S(2)}, u32[]{:S(2)}) collective-permute-start(bf16[2,80,160]{2,1,0:T(8,128)(2,1)S(1)} %pad.10.refs_0_), channel_id=1, source_target_pairs={{0,64},{32,96},{64,0},{96,32},{1,65},{33,97},{65,1},{97,33},{2,66}... | collective-permute-start | bytes 153608 | tf_op jit(solution)/shard_map/ppermute | solution.py:287
  21.0 0.0 collective-permute-start
  21.0 0.1 pad_add_fusion.2.at_ref
  21.1 2.6 %collective-permute-done.2.refs_3_ = bf16[2,80,160]{2,1,0:T(8,128)(2,1)S(1)} collective-permute-done((bf16[2,80,160]{2,1,0:T(8,128)(2,1)S(1)}, bf16[2,80,160]{2,1,0:T(8,128)(2,1)S(1)}, u32[]{:S(2)}, u32[]{:S(2)}) %collective-permute-start.2) | collective-permute-done | bytes 51232 | tf_op jit(solution)/shard_map/ppermute | solution.py:287
  23.7 3.6 %collective-permute-done.1.refs_2_ = bf16[2,80,160]{2,1,0:T(8,128)(2,1)S(1)} collective-permute-done((bf16[2,80,160]{2,1,0:T(8,128)(2,1)S(1)}, bf16[2,80,160]{2,1,0:T(8,128)(2,1)S(1)}, u32[]{:S(2)}, u32[]{:S(2)}) %collective-permute-start.1) | collective-permute-done | bytes 51232 | tf_op jit(solution)/shard_map/ppermute | solution.py:287
  27.3 0.0 collective-permute-done.refs_1_
  27.3 1.9 %shard_map.64 = bf16[16,80,640]{2,1,0:T(8,128)(2,1)} custom-call(s32[2]{0:T(128)S(1)} %pad_add_fusion.2.at_ref, bf16[2,80,160]{2,1,0:T(8,128)(2,1)S(1)} %pad.10.refs_0_, bf16[2,80,160]{2,1,0:T(8,128)(2,1)S(1)} %collective-permute-done.refs_1_, bf16[2,80,160]{2,1,0:T(8,128)(2,1)S(1)} %collective-permute-done.1.refs_2_, ...), custom_call_target="tpu_custom_call" | custom-call | tf_op jit(solution)/shard_map/pallas_call | solution.py:123
  29.2 0.0 all-to-all-done.1
  29.2 6.5 %all-to-all-start = ((bf16[16,80,640]{2,1,0:T(8,128)(2,1)}), bf16[16,80,640]{2,1,0:T(8,128)(2,1)S(1)}, u32[]{:S(2)}, u32[]{:S(2)}) async-start(bf16[16,80,640]{2,1,0:T(8,128)(2,1)} %shard_map.64), calls=%async_computation | async-start | bytes 3276800 | tf_op jit(solution)/shard_map/all_to_all | solution.py:291
  35.8 0.0 copy-done.4
  35.8 0.1 select_reduce_fusion
  35.9 0.1 broadcast_bitcast_fusion
  36.0 1.3 reshape.65
  37.2 0.0 copy-done.5
  37.2 0.4 fusion.1.a_ref
  37.6 12.1 %shard_map.65 = (bf16[32,2,80,512]{3,2,1,0:T(8,128)(2,1)}, bf16[32,2,80,128]{3,2,1,0:T(8,128)(2,1)S(1)}) custom-call(bf16[75,160,640]{2,1,0:T(8,128)(2,1)} %b_ref.1, bf16[640,256]{1,0:T(8,128)(2,1)S(1)} %fusion.1.a_ref), custom_call_target="tpu_custom_call" | custom-call | flops 3932160000 | bytes 21913600 | tf_op jit(solution)/shard_map/pallas_call | solution.py:80
  49.7 1.1 copy-done
  50.8 7.5 %all-to-all-done = bf16[16,80,640]{2,1,0:T(8,128)(2,1)S(1)} async-done(((bf16[16,80,640]{2,1,0:T(8,128)(2,1)}), bf16[16,80,640]{2,1,0:T(8,128)(2,1)S(1)}, u32[]{:S(2)}, u32[]{:S(2)}) %all-to-all-start) | async-done | bytes 1638432 | tf_op jit(solution)/shard_map/all_to_all | solution.py:291
  58.3 5.2 %all-to-all-start.2 = ((bf16[32,160,512]{2,1,0:T(8,128)(2,1)}), bf16[32,160,512]{2,1,0:T(8,128)(2,1)}, u32[]{:S(2)}, u32[]{:S(2)}) async-start(bf16[32,160,512]{2,1,0:T(8,128)(2,1)} %bitcast.33), calls=%async_computation.2 | async-start | bytes 10485760 | tf_op jit(solution)/shard_map/all_to_all | solution.py:319
  63.5 1.2 copy.18
  64.8 0.0 copy-start.2
  64.8 2.0 %collective-permute-start.3 = (bf16[640,1280]{1,0:T(8,128)(2,1)S(1)}, bf16[640,1280]{1,0:T(8,128)(2,1)S(1)}, u32[]{:S(2)}, u32[]{:S(2)}) collective-permute-start(bf16[640,1280]{1,0:T(8,128)(2,1)S(1)} %bitcast.31), channel_id=1, source_target_pairs={{0,68},{68,0},{4,64},{64,4},{1,69},{69,1},{5,65},{65,5},{2,70},{70... | collective-permute-start | bytes 4915208 | tf_op jit(solution)/shard_map/ppermute | solution.py:297
  66.7 35.2 %collective-permute-done.3 = bf16[640,1280]{1,0:T(8,128)(2,1)S(1)} collective-permute-done((bf16[640,1280]{1,0:T(8,128)(2,1)S(1)}, bf16[640,1280]{1,0:T(8,128)(2,1)S(1)}, u32[]{:S(2)}, u32[]{:S(2)}) %collective-permute-start.3) | collective-permute-done | bytes 1638432 | tf_op jit(solution)/shard_map/ppermute | solution.py:297
  101.9 0.0 copy-done.2
  101.9 1.7 pad_maximum_fusion.own_ref
  103.7 0.0 copy-start.3
  103.7 0.1 collective-permute-start.4
  103.8 23.3 %all-to-all-done.2 = bf16[32,160,512]{2,1,0:T(8,128)(2,1)} async-done(((bf16[32,160,512]{2,1,0:T(8,128)(2,1)}), bf16[32,160,512]{2,1,0:T(8,128)(2,1)}, u32[]{:S(2)}, u32[]{:S(2)}) %all-to-all-start.2) | async-done | bytes 5242912 | tf_op jit(solution)/shard_map/all_to_all | solution.py:319
  127.1 8.4 %all-to-all-start.3 = ((bf16[32,160,128]{2,1,0:T(8,128)(2,1)}), bf16[32,160,128]{2,1,0:T(8,128)(2,1)}, u32[]{:S(2)}, u32[]{:S(2)}) async-start(bf16[32,160,128]{2,1,0:T(8,128)(2,1)} %bitcast.29), calls=%async_computation.3 | async-start | bytes 2621440 | tf_op jit(solution)/shard_map/all_to_all | solution.py:319
  135.5 0.1 dynamic_slice.6
  135.6 0.1 pad_add_fusion.1.at_ref
  135.7 0.1 broadcast_and_fusion
  135.7 0.0 copy-done.3
  135.8 0.0 collective-permute-done.4.far_hbm
  135.8 7.3 %shard_map.66 = (bf16[4,56,640]{2,1,0:T(8,128)(2,1)}, bf16[4,56,640]{2,1,0:T(8,128)(2,1)}, bf16[4,56,640]{2,1,0:T(8,128)(2,1)}, bf16[4,56,640]{2,1,0:T(8,128)(2,1)}) custom-call(s32[2]{0:T(128)S(1)} %pad_add_fusion.1.at_ref, bf16[2,640,1280]{2,1,0:T(8,128)(2,1)S(1)} %pad_maximum_fusion.own_ref, f32[8,640]{1,0:T(8,128)S(1)} %pad_convert_fusion.keep_ref, ...), custom_call_target="tpu_custom_call" | custom-call | flops 3355443200 | bytes 11796480 | tf_op jit(solution)/shard_map/pallas_call | solution.py:189
  143.1 6.2 %collective-permute-start.9 = (bf16[4,56,640]{2,1,0:T(8,128)(2,1)}, bf16[4,56,640]{2,1,0:T(8,128)(2,1)}, u32[]{:S(2)}, u32[]{:S(2)}) collective-permute-start(bf16[4,56,640]{2,1,0:T(8,128)(2,1)} %get-tuple-element.30), channel_id=1, source_target_pairs={{0,0},{8,32},{16,64},{24,96},{32,8},{40,40},{48,72},{56,104},{64,1... | collective-permute-start | bytes 860168 | tf_op jit(solution)/shard_map/ppermute | solution.py:337
  149.3 1.4 collective-permute-start.10
  150.7 0.0 collective-permute-start.11
  150.7 1.8 collective-permute-start.12
  152.6 2.3 %all-to-all-done.3 = bf16[32,160,128]{2,1,0:T(8,128)(2,1)} async-done(((bf16[32,160,128]{2,1,0:T(8,128)(2,1)}), bf16[32,160,128]{2,1,0:T(8,128)(2,1)}, u32[]{:S(2)}, u32[]{:S(2)}) %all-to-all-start.3) | async-done | bytes 1310752 | tf_op jit(solution)/shard_map/all_to_all | solution.py:319
  154.9 5.4 %shard_map.67 = (bf16[1,56,640]{2,1,0:T(8,128)(2,1)S(1)}, bf16[1,56,640]{2,1,0:T(8,128)(2,1)S(1)}, bf16[1,56,640]{2,1,0:T(8,128)(2,1)S(1)}, bf16[1,56,640]{2,1,0:T(8,128)(2,1)S(1)}) custom-call(s32[2]{0:T(128)S(1)} %pad_add_fusion.1.at_ref, bf16[2,640,1280]{2,1,0:T(8,128)(2,1)S(1)} %pad_maximum_fusion.own_ref, f32[8,640]{1,0:T(8,128)S(1)} %pad_convert_fusion.keep_ref, ...), custom_call_target="tpu_custom_call" | custom-call | flops 838860800 | bytes 7864320 | tf_op jit(solution)/shard_map/pallas_call | solution.py:189
  160.3 4.2 %collective-permute-start.5 = (bf16[1,56,640]{2,1,0:T(8,128)(2,1)S(1)}, bf16[1,56,640]{2,1,0:T(8,128)(2,1)S(1)}, u32[]{:S(2)}, u32[]{:S(2)}) collective-permute-start(bf16[1,56,640]{2,1,0:T(8,128)(2,1)S(1)} %get-tuple-element.35), channel_id=1, source_target_pairs={{0,0},{8,32},{16,64},{24,96},{32,8},{40,40},{48,72},{56,104},{64,1... | collective-permute-start | bytes 215048 | tf_op jit(solution)/shard_map/ppermute | solution.py:337
  164.6 0.0 collective-permute-done.9.refs_0_
  164.6 3.9 %collective-permute-start.6 = (bf16[1,56,640]{2,1,0:T(8,128)(2,1)S(1)}, bf16[1,56,640]{2,1,0:T(8,128)(2,1)S(1)}, u32[]{:S(2)}, u32[]{:S(2)}) collective-permute-start(bf16[1,56,640]{2,1,0:T(8,128)(2,1)S(1)} %get-tuple-element.36), channel_id=1, source_target_pairs={{0,32},{8,64},{16,96},{24,0},{32,40},{40,72},{48,104},{56,8},{64,4... | collective-permute-start | bytes 215048 | tf_op jit(solution)/shard_map/ppermute | solution.py:337
  168.5 0.0 collective-permute-done.10.refs_1_
  168.5 4.1 %collective-permute-start.7 = (bf16[1,56,640]{2,1,0:T(8,128)(2,1)S(1)}, bf16[1,56,640]{2,1,0:T(8,128)(2,1)S(1)}, u32[]{:S(2)}, u32[]{:S(2)}) collective-permute-start(bf16[1,56,640]{2,1,0:T(8,128)(2,1)S(1)} %get-tuple-element.37), channel_id=1, source_target_pairs={{0,64},{8,96},{16,0},{24,32},{32,72},{40,104},{48,8},{56,40},{64,8... | collective-permute-start | bytes 215048 | tf_op jit(solution)/shard_map/ppermute | solution.py:337
  172.6 0.2 collective-permute-done.11.refs_2_
  172.8 6.1 %collective-permute-start.8 = (bf16[1,56,640]{2,1,0:T(8,128)(2,1)S(1)}, bf16[1,56,640]{2,1,0:T(8,128)(2,1)S(1)}, u32[]{:S(2)}, u32[]{:S(2)}) collective-permute-start(bf16[1,56,640]{2,1,0:T(8,128)(2,1)S(1)} %get-tuple-element.38), channel_id=1, source_target_pairs={{0,96},{8,0},{16,32},{24,64},{32,104},{40,8},{48,40},{56,72},{64,1... | collective-permute-start | bytes 215048 | tf_op jit(solution)/shard_map/ppermute | solution.py:337
  178.9 0.1 pad_add_fusion.at_ref
  179.0 2.3 %collective-permute-done.12.refs_3_ = bf16[4,56,640]{2,1,0:T(8,128)(2,1)} collective-permute-done((bf16[4,56,640]{2,1,0:T(8,128)(2,1)}, bf16[4,56,640]{2,1,0:T(8,128)(2,1)}, u32[]{:S(2)}, u32[]{:S(2)}) %collective-permute-start.12) | collective-permute-done | bytes 286752 | tf_op jit(solution)/shard_map/ppermute | solution.py:337
  181.3 2.5 %shard_map.68.refs_4_ = bf16[4,4,5,16,640]{4,3,2,1,0:T(8,128)(2,1)} custom-call(s32[5]{0:T(128)S(1)} %pad_add_fusion.at_ref, bf16[4,64,56]{2,1,0:T(8,128)(2,1)S(1)} %copy-done.1, bf16[4,56,640]{2,1,0:T(8,128)(2,1)} %collective-permute-done.9.refs_0_, bf16[4,56,640]{2,1,0:T(8,128)(2,1)} %collective-permute-done.10.refs_1_, ...), custom_call_target="tpu_custom_call" | custom-call | tf_op jit(solution)/shard_map/pallas_call | solution.py:237
  183.8 0.0 collective-permute-done.5.refs_0_
  183.9 0.0 collective-permute-done.6.refs_1_
  183.9 0.0 collective-permute-done.7.refs_2_
  183.9 1.1 collective-permute-done.8.refs_3_
  185.0 1.5 shard_map.69
  (12 shorter events, 0.1 us)
Async XLA Ops:
  2.1 27.2 %all-to-all-start.1 = ((bf16[128,20,128]{2,1,0:T(8,128)(2,1)}), bf16[128,20,128]{2,1,0:T(8,128)(2,1)}, u32[]{:S(2)}, u32[]{:S(2)}) async-start(bf16[128,20,128]{2,1,0:T(8,128)(2,1)} %broadcast_in_dim.36), calls=%async_computation.1 | async-start | bytes 1572864 | tf_op jit(solution)/shard_map/all_to_all | solution.py:46
  12.7 1.9 %slice-start = ((bf16[75,160,640]{2,1,0:T(8,128)(2,1)}), bf16[75,160,2]{2,1,0:T(8,128)(2,1)S(1)}, s32[]{:S(2)}) async-start(bf16[75,160,640]{2,1,0:T(8,128)(2,1)} %b_ref.1), calls=%async_computation.4 | async-start | bytes 6144000 | tf_op jit(solution)/shard_map/slice | solution.py:282
  17.6 6.0 %collective-permute-start.2 = (bf16[2,80,160]{2,1,0:T(8,128)(2,1)S(1)}, bf16[2,80,160]{2,1,0:T(8,128)(2,1)S(1)}, u32[]{:S(2)}, u32[]{:S(2)}) collective-permute-start(bf16[2,80,160]{2,1,0:T(8,128)(2,1)S(1)} %pad.10.refs_0_), channel_id=1, source_target_pairs={{0,96},{32,0},{64,32},{96,64},{1,97},{33,1},{65,33},{97,65},{2,98}... | collective-permute-start | bytes 153608 | tf_op jit(solution)/shard_map/ppermute | solution.py:287
  18.9 8.4 %collective-permute-start.1 = (bf16[2,80,160]{2,1,0:T(8,128)(2,1)S(1)}, bf16[2,80,160]{2,1,0:T(8,128)(2,1)S(1)}, u32[]{:S(2)}, u32[]{:S(2)}) collective-permute-start(bf16[2,80,160]{2,1,0:T(8,128)(2,1)S(1)} %pad.10.refs_0_), channel_id=1, source_target_pairs={{0,64},{32,96},{64,0},{96,32},{1,65},{33,97},{65,1},{97,33},{2,66}... | collective-permute-start | bytes 153608 | tf_op jit(solution)/shard_map/ppermute | solution.py:287
  21.0 6.3 %collective-permute-start = (bf16[2,80,160]{2,1,0:T(8,128)(2,1)S(1)}, bf16[2,80,160]{2,1,0:T(8,128)(2,1)S(1)}, u32[]{:S(2)}, u32[]{:S(2)}) collective-permute-start(bf16[2,80,160]{2,1,0:T(8,128)(2,1)S(1)} %pad.10.refs_0_), channel_id=1, source_target_pairs={{0,32},{32,64},{64,96},{96,0},{1,33},{33,65},{65,97},{97,1},{2,34}... | collective-permute-start | bytes 153608 | tf_op jit(solution)/shard_map/ppermute | solution.py:287
  29.2 6.5 %copy-start.4 = (s32[8]{0:T(128)S(1)}, s32[8]{0:T(128)}, u32[]{:S(2)}) copy-start(s32[8]{0:T(128)} %param.8) | copy-start | bytes 100
  29.2 8.0 %copy-start.5 = (bf16[4,128,256]{1,2,0:T(8,128)(2,1)S(1)}, bf16[4,128,256]{1,2,0:T(8,128)(2,1)}, u32[]{:S(2)}) copy-start(bf16[4,128,256]{1,2,0:T(8,128)(2,1)} %constant.83.clone) | copy-start | bytes 786436
  29.2 29.1 %all-to-all-start = ((bf16[16,80,640]{2,1,0:T(8,128)(2,1)}), bf16[16,80,640]{2,1,0:T(8,128)(2,1)S(1)}, u32[]{:S(2)}, u32[]{:S(2)}) async-start(bf16[16,80,640]{2,1,0:T(8,128)(2,1)} %shard_map.64), calls=%async_computation | async-start | bytes 3276800 | tf_op jit(solution)/shard_map/all_to_all | solution.py:291
  49.7 1.1 copy-start
  58.3 68.8 %all-to-all-start.2 = ((bf16[32,160,512]{2,1,0:T(8,128)(2,1)}), bf16[32,160,512]{2,1,0:T(8,128)(2,1)}, u32[]{:S(2)}, u32[]{:S(2)}) async-start(bf16[32,160,512]{2,1,0:T(8,128)(2,1)} %bitcast.33), calls=%async_computation.2 | async-start | bytes 10485760 | tf_op jit(solution)/shard_map/all_to_all | solution.py:319
  64.8 37.2 %copy-start.2 = (bf16[1280,640]{0,1:T(8,128)(2,1)}, bf16[1280,640]{0,1:T(8,128)(2,1)S(1)}, u32[]{:S(2)}) copy-start(bf16[1280,640]{0,1:T(8,128)(2,1)S(1)} %copy.18) | copy-start | bytes 4915204
  64.8 37.2 %collective-permute-start.3 = (bf16[640,1280]{1,0:T(8,128)(2,1)S(1)}, bf16[640,1280]{1,0:T(8,128)(2,1)S(1)}, u32[]{:S(2)}, u32[]{:S(2)}) collective-permute-start(bf16[640,1280]{1,0:T(8,128)(2,1)S(1)} %bitcast.31), channel_id=1, source_target_pairs={{0,68},{68,0},{4,64},{64,4},{1,69},{69,1},{5,65},{65,5},{2,70},{70... | collective-permute-start | bytes 4915208 | tf_op jit(solution)/shard_map/ppermute | solution.py:297
  103.7 32.1 %copy-start.3 = (bf16[448,128]{1,0:T(8,128)(2,1)S(1)}, bf16[448,128]{1,0:T(8,128)(2,1)}, u32[]{:S(2)}) copy-start(bf16[448,128]{1,0:T(8,128)(2,1)} %constant.84.clone) | copy-start | bytes 344068
  103.7 32.1 %collective-permute-start.4 = (bf16[2,640,1280]{2,1,0:T(8,128)(2,1)S(1)}, bf16[2,640,1280]{2,1,0:T(8,128)(2,1)}, u32[]{:S(2)}, u32[]{:S(2)}) collective-permute-start(bf16[2,640,1280]{2,1,0:T(8,128)(2,1)S(1)} %pad_maximum_fusion.own_ref), channel_id=1, source_target_pairs={{0,32},{32,0},{1,33},{33,1},{2,34},{34,2},{3,35},{35,3},{4,36},{36... | collective-permute-start | bytes 9830408 | tf_op jit(solution)/shard_map/ppermute | solution.py:299
  127.1 27.8 %all-to-all-start.3 = ((bf16[32,160,128]{2,1,0:T(8,128)(2,1)}), bf16[32,160,128]{2,1,0:T(8,128)(2,1)}, u32[]{:S(2)}, u32[]{:S(2)}) async-start(bf16[32,160,128]{2,1,0:T(8,128)(2,1)} %bitcast.29), calls=%async_computation.3 | async-start | bytes 2621440 | tf_op jit(solution)/shard_map/all_to_all | solution.py:319
  143.1 21.5 %collective-permute-start.9 = (bf16[4,56,640]{2,1,0:T(8,128)(2,1)}, bf16[4,56,640]{2,1,0:T(8,128)(2,1)}, u32[]{:S(2)}, u32[]{:S(2)}) collective-permute-start(bf16[4,56,640]{2,1,0:T(8,128)(2,1)} %get-tuple-element.30), channel_id=1, source_target_pairs={{0,0},{8,32},{16,64},{24,96},{32,8},{40,40},{48,72},{56,104},{64,1... | collective-permute-start | bytes 860168 | tf_op jit(solution)/shard_map/ppermute | solution.py:337
  149.3 19.2 %collective-permute-start.10 = (bf16[4,56,640]{2,1,0:T(8,128)(2,1)}, bf16[4,56,640]{2,1,0:T(8,128)(2,1)}, u32[]{:S(2)}, u32[]{:S(2)}) collective-permute-start(bf16[4,56,640]{2,1,0:T(8,128)(2,1)} %get-tuple-element.31), channel_id=1, source_target_pairs={{0,32},{8,64},{16,96},{24,0},{32,40},{40,72},{48,104},{56,8},{64,4... | collective-permute-start | bytes 860168 | tf_op jit(solution)/shard_map/ppermute | solution.py:337
  150.7 22.1 %collective-permute-start.11 = (bf16[4,56,640]{2,1,0:T(8,128)(2,1)}, bf16[4,56,640]{2,1,0:T(8,128)(2,1)}, u32[]{:S(2)}, u32[]{:S(2)}) collective-permute-start(bf16[4,56,640]{2,1,0:T(8,128)(2,1)} %get-tuple-element.32), channel_id=1, source_target_pairs={{0,64},{8,96},{16,0},{24,32},{32,72},{40,104},{48,8},{56,40},{64,8... | collective-permute-start | bytes 860168 | tf_op jit(solution)/shard_map/ppermute | solution.py:337
  150.7 30.6 %collective-permute-start.12 = (bf16[4,56,640]{2,1,0:T(8,128)(2,1)}, bf16[4,56,640]{2,1,0:T(8,128)(2,1)}, u32[]{:S(2)}, u32[]{:S(2)}) collective-permute-start(bf16[4,56,640]{2,1,0:T(8,128)(2,1)} %get-tuple-element.33), channel_id=1, source_target_pairs={{0,96},{8,0},{16,32},{24,64},{32,104},{40,8},{48,40},{56,72},{64,1... | collective-permute-start | bytes 860168 | tf_op jit(solution)/shard_map/ppermute | solution.py:337
  154.9 26.4 %copy-start.1 = (bf16[4,64,56]{2,1,0:T(8,128)(2,1)S(1)}, bf16[4,64,56]{2,1,0:T(8,128)(2,1)}, u32[]{:S(2)}) copy-start(bf16[4,64,56]{2,1,0:T(8,128)(2,1)} %constant.85.clone.spread_ref) | copy-start | bytes 86020
  160.3 23.5 %collective-permute-start.5 = (bf16[1,56,640]{2,1,0:T(8,128)(2,1)S(1)}, bf16[1,56,640]{2,1,0:T(8,128)(2,1)S(1)}, u32[]{:S(2)}, u32[]{:S(2)}) collective-permute-start(bf16[1,56,640]{2,1,0:T(8,128)(2,1)S(1)} %get-tuple-element.35), channel_id=1, source_target_pairs={{0,0},{8,32},{16,64},{24,96},{32,8},{40,40},{48,72},{56,104},{64,1... | collective-permute-start | bytes 215048 | tf_op jit(solution)/shard_map/ppermute | solution.py:337
  164.6 19.3 %collective-permute-start.6 = (bf16[1,56,640]{2,1,0:T(8,128)(2,1)S(1)}, bf16[1,56,640]{2,1,0:T(8,128)(2,1)S(1)}, u32[]{:S(2)}, u32[]{:S(2)}) collective-permute-start(bf16[1,56,640]{2,1,0:T(8,128)(2,1)S(1)} %get-tuple-element.36), channel_id=1, source_target_pairs={{0,32},{8,64},{16,96},{24,0},{32,40},{40,72},{48,104},{56,8},{64,4... | collective-permute-start | bytes 215048 | tf_op jit(solution)/shard_map/ppermute | solution.py:337
  168.5 15.4 %collective-permute-start.7 = (bf16[1,56,640]{2,1,0:T(8,128)(2,1)S(1)}, bf16[1,56,640]{2,1,0:T(8,128)(2,1)S(1)}, u32[]{:S(2)}, u32[]{:S(2)}) collective-permute-start(bf16[1,56,640]{2,1,0:T(8,128)(2,1)S(1)} %get-tuple-element.37), channel_id=1, source_target_pairs={{0,64},{8,96},{16,0},{24,32},{32,72},{40,104},{48,8},{56,40},{64,8... | collective-permute-start | bytes 215048 | tf_op jit(solution)/shard_map/ppermute | solution.py:337
  172.8 12.2 %collective-permute-start.8 = (bf16[1,56,640]{2,1,0:T(8,128)(2,1)S(1)}, bf16[1,56,640]{2,1,0:T(8,128)(2,1)S(1)}, u32[]{:S(2)}, u32[]{:S(2)}) collective-permute-start(bf16[1,56,640]{2,1,0:T(8,128)(2,1)S(1)} %get-tuple-element.38), channel_id=1, source_target_pairs={{0,96},{8,0},{16,32},{24,64},{32,104},{40,8},{48,40},{56,72},{64,1... | collective-permute-start | bytes 215048 | tf_op jit(solution)/shard_map/ppermute | solution.py:337
